TPU v7x, 128 devices: a whole 4x4x4 slice. The times are simulated.
128 devices in a mesh: fsdp: 128 (over z, y, x, core).
Axes of the slice: x: 4, y: 4, z: 4, core: 2. Of those that a mesh axis runs over, the one named last changes fastest.
Arguments:
- tokens: bfloat16 [32768, 640], P('fsdp'), may hold values from -6 to 6
- out_grad: bfloat16 [32768, 640], P('fsdp'), may hold values from -6 to 6
- seq_start: int32 [25], replicated, may hold values from 0 to 31744, as said below
- seq_len: int32 [25], replicated, may hold values from 384 to 1024, as said below
- w_query: bfloat16 [640, 1024], P('fsdp'), may hold values from -0.25 to 0.25
- w_key_value: bfloat16 [640, 512], P('fsdp'), may hold values from -0.25 to 0.25
- w_output: bfloat16 [1024, 640], P('fsdp'), may hold values from -0.1875 to 0.1875
- w_gate_up: bfloat16 [640, 4096], P('fsdp'), may hold values from -0.25 to 0.25
- w_down: bfloat16 [2048, 640], P('fsdp'), may hold values from -0.125 to 0.125
- norm_attn_in: bfloat16 [640], P('fsdp'), may hold values from 0.099609375 to 1.8984375
- norm_attn_out: bfloat16 [640], P('fsdp'), may hold values from 0.099609375 to 1.8984375
- norm_mlp_in: bfloat16 [640], P('fsdp'), may hold values from 0.099609375 to 1.8984375
- norm_mlp_out: bfloat16 [640], P('fsdp'), may hold values from 0.099609375 to 1.8984375
- norm_query: bfloat16 [256], P('fsdp'), may hold values from 0.099609375 to 1.8984375
- norm_key: bfloat16 [256], P('fsdp'), may hold values from 0.099609375 to 1.8984375
Outputs:
- mixed: bfloat16 [32768, 640], P('fsdp')
- tokens_grad: bfloat16 [32768, 640], P('fsdp')
- grad_w_query: float32 [640, 1024], P('fsdp')
- grad_w_key_value: float32 [640, 512], P('fsdp')
- grad_w_output: float32 [1024, 640], P('fsdp')
- grad_w_gate_up: float32 [640, 4096], P('fsdp')
- grad_w_down: float32 [2048, 640], P('fsdp')
- grad_norm_attn_in: float32 [640], P('fsdp')
- grad_norm_attn_out: float32 [640], P('fsdp')
- grad_norm_mlp_in: float32 [640], P('fsdp')
- grad_norm_mlp_out: float32 [640], P('fsdp')
- grad_norm_query: float32 [256], P('fsdp')
- grad_norm_key: float32 [256], P('fsdp')
Inputs may be any that keep to these rules, and one draw needn't show every extreme that they name: `seq_start`: sequence s starts at a multiple of 128 and lies within the blocks of 128 slots numbered s * 256 // 25 to (s + 1) * 256 // 25 - 1; the first sequence starts at slot 0 and the last one ends at the last slot. `seq_len`: the last sequence has exactly 1024 tokens and another exactly 384.
All inputs are finite; a program needn't handle non-finite values.
Results may differ from a plain program's by a relative error of at most 0.035.
Values may be sent and summed in bfloat16 or wider, within the bound.
No kernel may reach another device: no remote copies, remote signals or barrier semaphores. Data moves between devices by JAX's collectives and lax.ppermute only.
A program may use at most 128 MiB of HBM per device.

v0:
```python
import jax
import jax.numpy as jnp
from jax import lax
from jax.experimental import pallas as pl
from jax.experimental.pallas import tpu as pltpu
from jax.sharding import PartitionSpec as P

WINDOW = 512


epsilon = 1e-06
theta_base = 10000.0
query_scale = 0.0625


def shifted(block, axis, distance):
    devices = range(lax.axis_size(axis))
    route = [(i - distance, i) for i in devices if i - distance in devices]
    return lax.ppermute(block, axis, route)


def token_layout(seq_start, seq_len, first_token, token_count):
    indices = first_token + jnp.arange(token_count, dtype=jnp.int32)
    offsets = indices[:, None] - seq_start[None, :]
    inside = (offsets >= 0) & (offsets < seq_len[None, :])
    live_mask = jnp.any(inside, axis=1)
    seq_numbers = jnp.arange(seq_start.shape[0], dtype=jnp.int32)
    seq_id = jnp.sum(jnp.where(inside, seq_numbers[None, :], 0), axis=1)
    seq_id = jnp.where(live_mask, seq_id, -1)
    positions = jnp.sum(jnp.where(inside, offsets, 0), axis=1)
    return (indices, seq_id, positions, live_mask)


BF16 = jnp.bfloat16
F32 = jnp.float32
SLOTS = 8
GAIN_SLOT = 5
MASKED = -1e30
VMEM_BYTES = 56 * 1024 * 1024
LANES = 128


def same_core_groups(size):
    return [[2 * chip + core for chip in range(size // 2)] for core in range(2)]


def swap_cores(block):
    size = lax.axis_size("fsdp")
    return lax.ppermute(block, "fsdp", [(i, i ^ 1) for i in range(size)])


def exchange(blocks):
    return lax.all_to_all(
        blocks,
        "fsdp",
        split_axis=0,
        concat_axis=0,
        tiled=True,
        axis_index_groups=same_core_groups(lax.axis_size("fsdp")),
    )


def spread(block):
    chips = lax.axis_size("fsdp") // 2
    return exchange(jnp.broadcast_to(block[None], (chips,) + block.shape))


def call(kernel, outs, ins, scratch=(), specs=None, flops=4e9):
    return pl.pallas_call(
        kernel,
        out_shape=outs,
        in_specs=specs,
        scratch_shapes=list(scratch),
        compiler_params=pltpu.CompilerParams(vmem_limit_bytes=VMEM_BYTES),
        cost_estimate=pl.CostEstimate(
            flops=int(flops), bytes_accessed=8_000_000, transcendentals=0
        ),
    )(*ins)


SCALAR = pl.BlockSpec(memory_space=pltpu.SMEM)
WHOLE = pl.BlockSpec(memory_space=pltpu.VMEM)
AWAY = pl.BlockSpec(memory_space=pl.ANY)


def shape(dims, kind):
    return jax.ShapeDtypeStruct(dims, kind)


def dot(left, right):
    return jnp.dot(left, right, preferred_element_type=F32)


def dot_nt(left, right):
    return lax.dot_general(left, right, (((1,), (1,)), ((), ())), preferred_element_type=F32)


def dot_tn(left, right):
    return lax.dot_general(left, right, (((0,), (0,)), ((), ())), preferred_element_type=F32)


def normed(values):
    scale = lax.rsqrt(jnp.mean(values * values, axis=-1, keepdims=True) + epsilon)
    return values * scale, scale


def normed_back(cot, unit, scale, gain):
    weighted = cot * gain
    inner = jnp.mean(weighted * unit, axis=-1, keepdims=True)
    return scale * (weighted - unit * inner), jnp.sum(cot * unit, axis=0, keepdims=True)


def ones_where(mask):
    return jnp.where(mask, 1.0, 0.0).astype(BF16)


def places(count):
    place = lax.broadcasted_iota(jnp.int32, (1, count), 1)
    return lax.shift_right_logical(place, 3), place & (SLOTS - 1)


def pick_rows(rows, count, per, core):
    block, slot = places(count)
    device = block if core is None else 2 * block + core
    source = jnp.where(slot < per, device * per + slot, -1)
    return ones_where(lax.broadcasted_iota(jnp.int32, (rows, count), 0) == source)


def pick_slot(rows, count, per, core):
    block, slot = places(count)
    low = jnp.where(slot == GAIN_SLOT, (2 * block + core) * per, -2 * rows)
    natural = lax.broadcasted_iota(jnp.int32, (rows, count), 0)
    return ones_where((natural >= low) & (natural < low + per))


def gain_mask(first, per, rows, columns):
    row = lax.broadcasted_iota(jnp.int32, (rows, columns), 0)
    column = lax.broadcasted_iota(jnp.int32, (rows, columns), 1)
    return row == first + lax.rem(column, per)


def turned(values, cos, sin):
    half = values.shape[-1] // 2
    first, second = values[:, :half], values[:, half:]
    return jnp.concatenate([first * cos - second * sin, second * cos + first * sin], axis=1)


def before_attention(
    core_ref, tok, own, peer, cos, sin, attn_rel, raw, query_low, own_kv, gains, head_gains
):
    core = core_ref[0]
    width, rows = tok.shape[1], own.shape[0]
    kv_cols = own_kv.shape[1]
    head = kv_cols // 2
    q_cols = query_low.shape[1]
    per, per_head = width // LANES, head // LANES

    def gather(natural, count):
        mine = dot(pick_slot(natural, rows, count, core), own[:, :LANES])
        theirs = dot(pick_slot(natural, rows, count, 1 - core), peer[:, :LANES])
        return jnp.transpose(mine + theirs)[:32]

    wide = gather(width, per)
    for which in range(4):
        mask = gain_mask(which * per, per, 32, width)
        gains[which : which + 1, :] = jnp.sum(jnp.where(mask, wide, 0.0), 0, keepdims=True)
    narrow = gather(head, per_head)
    for which in range(2):
        mask = gain_mask(4 * per + which * per_head, per_head, 32, head)
        head_gains[which : which + 1, :] = jnp.sum(jnp.where(mask, narrow, 0.0), 0, keepdims=True)
    unit, _ = normed(tok[...].astype(F32))
    low = (unit * gains[0:1, :]).astype(BF16)
    attn_rel[:, :rows] = dot(low, pick_rows(width, rows, per, core)).astype(BF16)
    attn_rel[:, rows:] = dot(low, pick_rows(width, rows, per, 1 - core)).astype(BF16)
    columns = q_cols + kv_cols
    raw[...] = dot(attn_rel[:, :rows], own[:, :columns]) + dot(attn_rel[:, rows:], peer[:, :columns])
    for index in range(q_cols // head):
        span = slice(index * head, (index + 1) * head)
        unit, _ = normed(raw[:, span])
        query_low[:, span] = turned(unit * head_gains[0:1, :], cos[...], sin[...]).astype(BF16)
    unit, _ = normed(raw[:, q_cols : q_cols + head])
    own_kv[:, :head] = turned(unit * head_gains[1:2, :], cos[...], sin[...]).astype(BF16)
    own_kv[:, head:] = raw[:, q_cols + head :].astype(BF16)


def visible(q_seq, k_seq):
    queries, keys = q_seq.shape[0], k_seq.shape[1]
    row = lax.broadcasted_iota(jnp.int32, (queries, keys), 0)
    column = lax.broadcasted_iota(jnp.int32, (queries, keys), 1)
    distance = row - column + (keys - queries)
    same = (q_seq[...] == k_seq[...]) & (q_seq[...] >= 0)
    return (same & (distance >= 0) & (distance < WINDOW)) | (distance == 0)


def attention(
    core_ref, query_low, kv_far, kv_near, kv_own, q_seq, k_seq, own, peer, tok, gains,
    heads_low, log_total, proj, state,
):
    core = core_ref[0]
    head = kv_own.shape[1] // 2
    width, rows = tok.shape[1], own.shape[0]
    q_cols = query_low.shape[1]
    parts = (kv_far, kv_near, kv_own)
    keys = jnp.concatenate([part[:, :head] for part in parts], axis=0)
    values = jnp.concatenate([part[:, head:] for part in parts], axis=0)
    allowed = visible(q_seq, k_seq)
    for index in range(q_cols // head):
        span = slice(index * head, (index + 1) * head)
        scores = dot_nt(query_low[:, span], keys) * query_scale
        scores = jnp.where(allowed, scores, MASKED)
        top = jnp.max(scores, axis=-1, keepdims=True)
        terms = jnp.exp(scores - top)
        total = jnp.sum(terms, axis=-1, keepdims=True)
        probs = (terms * (1.0 / total)).astype(BF16)
        heads_low[:, span] = dot(probs, values).astype(BF16)
        log_total[:, index : index + 1] = top + jnp.log(total)
    offset = own.shape[1] - width
    heads = heads_low[...]
    first = dot(heads, pick_rows(q_cols, rows, SLOTS, core)).astype(BF16)
    second = dot(heads, pick_rows(q_cols, rows, SLOTS, 1 - core)).astype(BF16)
    proj[...] = dot(first, own[:, offset:]) + dot(second, peer[:, offset:])
    unit, _ = normed(proj[...])
    state[...] = tok[...].astype(F32) + unit * gains[1:2, :]


def feed_forward(
    core_ref, state, proj, out_grad, live, gains, heads_low, own, peer, gate_up, own_down, peer_down,
    mixed, d_state, d_heads, gain_grads, keep, send,
    weights, down, act, act_slope, hidden, total, back, low_flat, low, low_branch, turn, turn_down,
    turn_out, weight_sem, down_sem,
):
    core = core_ref[0]
    tiles, tile = weights.shape[0], weights.shape[2]
    half = tiles // 2
    width = state.shape[1]
    rows = own.shape[0]
    q_cols = heads_low.shape[1]
    per = width // LANES
    down_rows = own_down.shape[1]
    blocks, strips = keep.shape[0], keep.shape[1]
    block_rows = width // blocks
    tile_chips = tile // (2 * down_rows)

    def weight_copy(index):
        return pltpu.make_async_copy(
            gate_up.at[:, pl.ds(pl.multiple_of(index * tile, tile), tile)],
            weights.at[index],
            weight_sem.at[index],
        )

    down_copies = (
        pltpu.make_async_copy(own_down, down.at[:, core], down_sem.at[0]),
        pltpu.make_async_copy(peer_down, down.at[:, 1 - core], down_sem.at[1]),
    )
    for index in range(half):
        weight_copy(index).start()
        weight_copy(half + index).start()
        if index == 0:
            for copy in down_copies:
                copy.start()

    spread_flat = pick_rows(width, weights.shape[1], per, None)
    unit, scale = normed(state[...])
    low[...] = (unit * gains[2:3, :]).astype(BF16)
    low_flat[...] = dot(low[...], spread_flat).astype(BF16)
    total[...] = jnp.zeros_like(total)
    for copy in down_copies:
        copy.wait()

    def down_tile(index):
        chunk = down[pl.ds(index * tile_chips, tile_chips)]
        return chunk.reshape(tile, width)

    def forward(index, carry):
        columns = pl.ds(pl.multiple_of(index * tile, tile), tile)
        weight_copy(index).wait()
        weight_copy(half + index).wait()
        gate = dot(low_flat[...], weights[index])
        up = dot(low_flat[...], weights[half + index])
        square = gate * gate
        bend = jnp.tanh(gate * (0.7978845608028654 * (1.0 + 0.044715 * square)))
        rise = 0.5 * (1.0 + bend)
        gelu = gate * rise
        slope = rise + 0.5 * gate * (1.0 - bend * bend) * (
            0.7978845608028654 * (1.0 + 0.134145 * square)
        )
        act[:, columns] = gelu
        act_slope[:, columns] = up * slope
        hidden[:, columns] = (gelu * up).astype(BF16)
        total[...] += dot(hidden[:, columns], down_tile(index))
        return carry

    lax.fori_loop(0, half, forward, 0)

    branch_unit, branch_scale = normed(total[...])
    mixed[...] = ((state[...] + branch_unit * gains[3:4, :]) * live[...]).astype(BF16)
    cotangent = out_grad[...].astype(F32) * live[...]
    d_branch, gain_grads[3:4, :] = normed_back(
        cotangent, branch_unit, branch_scale, gains[3:4, :]
    )
    low_branch[...] = d_branch.astype(BF16)
    back[...] = jnp.zeros_like(back)

    def place(strip, grads):
        turn[0] = grads[:, : tile // 2].astype(BF16)
        turn[1] = grads[:, tile // 2 :].astype(BF16)
        for target, parity in ((keep, core), (send, 1 - core)):
            for part in range(tile // 2 // LANES):
                target[:, strip, part * block_rows : (part + 1) * block_rows, :] = turn[
                    parity, :, part * LANES : (part + 1) * LANES
                ].reshape(blocks, block_rows, LANES)

    down_at = block_rows * (tile // 2 // LANES)
    out_at = down_at + down_rows * (width // LANES)

    def backward(index, carry):
        columns = pl.ds(pl.multiple_of(index * tile, tile), tile)
        d_hidden = dot_nt(low_branch[...], down_tile(index))
        d_gate = (d_hidden * act_slope[:, columns]).astype(BF16)
        d_up = (d_hidden * act[:, columns]).astype(BF16)
        back[...] += dot_nt(d_gate, weights[index]) + dot_nt(d_up, weights[half + index])
        place(index, dot_tn(low[...], d_gate))
        place(half + index, dot_tn(low[...], d_up))
        turn_down[...] = (
            dot_tn(hidden[:, columns], low_branch[...])
            .astype(BF16)
            .reshape(tile_chips // strips, strips, 2, down_rows, width)
        )
        tall = pl.ds(index * (tile_chips // strips), tile_chips // strips)
        for target, parity in ((keep, core), (send, 1 - core)):
            for part in range(width // LANES):
                top = down_at + part * down_rows
                target[tall, :, top : top + down_rows, :] = turn_down[
                    :, :, parity, :, part * LANES : (part + 1) * LANES
                ]
        return carry

    lax.fori_loop(0, half, backward, 0)

    high = back[...].astype(BF16)
    rest = (back[...] - high.astype(F32)).astype(BF16)
    d_low = dot_nt(high, spread_flat) + dot_nt(rest, spread_flat)
    d_norm, gain_grads[2:3, :] = normed_back(d_low, unit, scale, gains[2:3, :])
    d_state[...] = cotangent + d_norm
    proj_unit, proj_scale = normed(proj[...])
    d_proj, gain_grads[1:2, :] = normed_back(d_state[...], proj_unit, proj_scale, gains[1:2, :])
    proj_low = d_proj.astype(BF16)
    offset = own.shape[1] - width
    first = dot_nt(proj_low, own[:, offset:]).astype(BF16)
    second = dot_nt(proj_low, peer[:, offset:]).astype(BF16)
    d_heads[...] = (
        dot_nt(first, pick_rows(q_cols, rows, SLOTS, core))
        + dot_nt(second, pick_rows(q_cols, rows, SLOTS, 1 - core))
    ).astype(BF16)
    out_rows = 2 * SLOTS
    for part in range(width // LANES):
        turn_out[part] = (
            dot_tn(heads_low[...], proj_low[:, part * LANES : (part + 1) * LANES])
            .astype(BF16)
            .reshape(blocks, strips, out_rows, LANES)
        )
    for target, parity in ((keep, core), (send, 1 - core)):
        target[:, :, out_at : out_at + out_rows, :] = turn_out[2 * parity]
        target[:, :, out_at + out_rows : out_at + 2 * out_rows, :] = turn_out[2 * parity + 1]
        target[:, :, out_at + 2 * out_rows : out_at + 3 * out_rows, :] = turn_out[4]


def attention_back(
    query_low, kv_far, kv_near, kv_own, d_heads, log_total, q_seq, k_seq,
    d_query, d_own, d_near, d_far, sum_keys, sum_values,
):
    head = kv_own.shape[1] // 2
    rows = kv_own.shape[0]
    parts = (kv_far, kv_near, kv_own)
    keys = jnp.concatenate([part[:, :head] for part in parts], axis=0)
    values = jnp.concatenate([part[:, head:] for part in parts], axis=0)
    allowed = visible(q_seq, k_seq)
    for index in range(query_low.shape[1] // head):
        span = slice(index * head, (index + 1) * head)
        scores = dot_nt(query_low[:, span], keys) * query_scale
        scores = jnp.where(allowed, scores, MASKED)
        probs = jnp.exp(scores - log_total[:, index : index + 1])
        d_probs = dot_nt(d_heads[:, span], values)
        inner = jnp.sum(probs * d_probs, axis=-1, keepdims=True)
        d_scores = (probs * (d_probs - inner)).astype(BF16)
        d_query[:, span] = dot(d_scores, keys) * query_scale
        key_term = dot_tn(d_scores, query_low[:, span]) * query_scale
        value_term = dot_tn(probs.astype(BF16), d_heads[:, span])
        if index == 0:
            sum_keys[...] = key_term
            sum_values[...] = value_term
        else:
            sum_keys[...] += key_term
            sum_values[...] += value_term
    for target, start in ((d_far, 0), (d_near, rows), (d_own, 2 * rows)):
        target[:, :head] = sum_keys[start : start + rows, :].astype(target.dtype)
        target[:, head:] = sum_values[start : start + rows, :].astype(target.dtype)


def after_attention(
    core_ref, raw, d_query, d_own, near, far, attn_rel, own, peer, tok, gains, head_gains, cos, sin,
    d_state, gain_grads, tokens_grad, keep, send, low,
):
    core = core_ref[0]
    width, rows = tok.shape[1], own.shape[0]
    q_cols, kv_cols = d_query.shape[1], d_own.shape[1]
    head = kv_cols // 2
    per, per_head = width // LANES, head // LANES
    cosine, minus_sine = cos[...], -sin[...]
    query_gain_grad = jnp.zeros((1, head), F32)
    for index in range(q_cols // head):
        span = slice(index * head, (index + 1) * head)
        unit, scale = normed(raw[:, span])
        cot = turned(d_query[:, span], cosine, minus_sine)
        d_raw, part = normed_back(cot, unit, scale, head_gains[0:1, :])
        query_gain_grad += part
        low[:, span] = d_raw.astype(BF16)
    d_kv = d_own[...] + near[...].astype(F32) + far[...].astype(F32)
    unit, scale = normed(raw[:, q_cols : q_cols + head])
    cot = turned(d_kv[:, :head], cosine, minus_sine)
    d_raw, key_gain_grad = normed_back(cot, unit, scale, head_gains[1:2, :])
    low[:, q_cols : q_cols + head] = d_raw.astype(BF16)
    low[:, q_cols + head :] = d_kv[:, head:].astype(BF16)

    columns = q_cols + kv_cols
    d_low = jnp.zeros(tok.shape, F32)
    for weight, parity in ((own, core), (peer, 1 - core)):
        part = dot_nt(low[...], weight[:, :columns])
        high = part.astype(BF16)
        rest = (part - high.astype(F32)).astype(BF16)
        selector = pick_rows(width, rows, per, parity)
        d_low += dot_nt(high, selector) + dot_nt(rest, selector)
    unit, scale = normed(tok[...].astype(F32))
    d_norm, in_gain_grad = normed_back(d_low, unit, scale, gains[0:1, :])
    tokens_grad[...] = (d_state[...] + d_norm).astype(BF16)

    wide = jnp.zeros((LANES, width), F32)
    vectors = [in_gain_grad] + [gain_grads[i : i + 1, :] for i in range(1, 4)]
    for which, vector in enumerate(vectors):
        wide = jnp.where(gain_mask(which * per, per, LANES, width), vector, wide)
    narrow = jnp.zeros((LANES, head), F32)
    for which, vector in enumerate((query_gain_grad, key_gain_grad)):
        mask = gain_mask(4 * per + which * per_head, per_head, LANES, head)
        narrow = jnp.where(mask, vector, narrow)
    wide, narrow = wide.astype(BF16), narrow.astype(BF16)
    for target, start, parity in ((keep, 0, core), (send, rows, 1 - core)):
        extra = dot(wide, pick_slot(width, rows, per, parity)) + dot(
            narrow, pick_slot(head, rows, per_head, parity)
        )
        block = dot_tn(attn_rel[:, start : start + rows], low[:, :LANES])
        target[:, :LANES] = (block + jnp.transpose(extra)).astype(BF16)
        target[:, LANES:] = dot_tn(attn_rel[:, start : start + rows], low[:, LANES:]).astype(BF16)


def on_device(
    tokens,
    out_grad,
    seq_start,
    seq_len,
    w_query,
    w_key_value,
    w_output,
    w_gate_up,
    w_down,
    norm_attn_in,
    norm_attn_out,
    norm_mlp_in,
    norm_mlp_out,
    norm_query,
    norm_key,
):
    size = lax.axis_size("fsdp")
    chips = size // 2
    me = lax.axis_index("fsdp")
    core = me % 2
    core_arg = core.astype(jnp.int32).reshape(1)
    tok_rows, width = tokens.shape
    shard = w_query.shape[0]
    q_cols, kv_cols = w_query.shape[1], w_key_value.shape[1]
    qkv_cols = q_cols + kv_cols
    gu_cols, ff = w_gate_up.shape[1], w_down.shape[0] * size
    down_rows = w_down.shape[0]
    head = kv_cols // 2
    hshard = norm_query.shape[0]
    half_rows = chips * SLOTS

    gateup_flat = lax.all_gather(
        jnp.pad(w_gate_up, ((0, SLOTS - shard), (0, 0))), "fsdp", axis=0, tiled=True
    )

    gain_row = jnp.concatenate(
        [norm_attn_in, norm_attn_out, norm_mlp_in, norm_mlp_out, norm_query, norm_key]
    )
    gain_count = gain_row.shape[0]
    pack = jnp.concatenate(
        [
            jnp.concatenate([w_query, w_key_value], axis=1),
            jnp.pad(gain_row, (0, qkv_cols - gain_count))[None],
            jnp.zeros((SLOTS - shard - 1, qkv_cols), BF16),
        ],
        axis=0,
    )
    own_attn = spread(jnp.concatenate([pack, w_output], axis=1))
    own = own_attn.reshape(half_rows, qkv_cols + width)
    peer = swap_cores(own)

    key_reach = (WINDOW + tok_rows - 2) // tok_rows
    first_token = me * tok_rows
    q_index, q_seq, q_pos, q_live = token_layout(seq_start, seq_len, first_token, tok_rows)
    k_index, k_seq, k_pos, k_live = token_layout(
        seq_start, seq_len, first_token - key_reach * tok_rows, (key_reach + 1) * tok_rows
    )
    live = q_live.astype(F32)[:, None]
    q_seq, k_seq = q_seq[:, None], k_seq[None, :]
    inv_freq = theta_base ** (-2.0 * jnp.arange(head // 2, dtype=F32) / head)
    angles = q_pos.astype(F32)[:, None] * inv_freq[None, :]
    cos_vals, sin_vals = jnp.cos(angles), jnp.sin(angles)

    attn_rel, raw, query_low, own_kv, gains, head_gains = call(
        before_attention,
        (
            shape((tok_rows, 2 * half_rows), BF16),
            shape((tok_rows, qkv_cols), F32),
            shape((tok_rows, q_cols), BF16),
            shape((tok_rows, kv_cols), BF16),
            shape((8, width), F32),
            shape((8, head), F32),
        ),
        (core_arg, tokens, own, peer, cos_vals, sin_vals),
        specs=[SCALAR] + [WHOLE] * 5,
    )
    down_block, own_kv = lax.optimization_barrier((w_down, own_kv))
    own_down = spread(down_block)
    kv_near = shifted(own_kv, "fsdp", 1)
    kv_far = shifted(own_kv, "fsdp", 2)
    heads_low, log_total, proj, state = call(
        attention,
        (
            shape((tok_rows, q_cols), BF16),
            shape((tok_rows, LANES), F32),
            shape((tok_rows, width), F32),
            shape((tok_rows, width), F32),
        ),
        (core_arg, query_low, kv_far, kv_near, own_kv, q_seq, k_seq, own, peer, tokens, gains),
        specs=[SCALAR] + [WHOLE] * 10,
        flops=20e9,
    )

    own_down, state = lax.optimization_barrier((own_down, state))
    peer_down = swap_cores(own_down)

    tile = 512
    blocks, strips = 8, chips // 8
    chunk_rows = (width // blocks) * 2 + down_rows * (width // LANES) + 6 * SLOTS
    mixed, d_state, d_heads, gain_grads, keep, send = call(
        feed_forward,
        (
            shape((tok_rows, width), BF16),
            shape((tok_rows, width), F32),
            shape((tok_rows, q_cols), BF16),
            shape((8, width), F32),
            shape((blocks, strips, chunk_rows, LANES), BF16),
            shape((blocks, strips, chunk_rows, LANES), BF16),
        ),
        (
            core_arg, state, proj, out_grad, live, gains, heads_low, own, peer,
            gateup_flat, own_down, peer_down,
        ),
        scratch=(
            pltpu.VMEM((gu_cols // tile, size * SLOTS, tile), BF16),
            pltpu.VMEM((chips, 2, down_rows, width), BF16),
            pltpu.VMEM((tok_rows, ff), F32),
            pltpu.VMEM((tok_rows, ff), F32),
            pltpu.VMEM((tok_rows, ff), BF16),
            pltpu.VMEM((tok_rows, width), F32),
            pltpu.VMEM((tok_rows, size * SLOTS), F32),
            pltpu.VMEM((tok_rows, size * SLOTS), BF16),
            pltpu.VMEM((tok_rows, width), BF16),
            pltpu.VMEM((tok_rows, width), BF16),
            pltpu.VMEM((2, width, tile // 2), BF16),
            pltpu.VMEM((tile // (2 * down_rows) // strips, strips, 2, down_rows, width), BF16),
            pltpu.VMEM((width // LANES, blocks, strips, 2 * SLOTS, LANES), BF16),
            pltpu.SemaphoreType.DMA((gu_cols // tile,)),
            pltpu.SemaphoreType.DMA((2,)),
        ),
        specs=[SCALAR] + [WHOLE] * 8 + [AWAY] * 3,
        flops=12e9,
    )
    both = keep.astype(F32) + swap_cores(send).astype(F32)
    mlp_parts = exchange(both.astype(BF16).reshape(chips, chunk_rows, LANES))

    d_query, d_own, d_near, d_far = call(
        attention_back,
        (
            shape((tok_rows, q_cols), F32),
            shape((tok_rows, kv_cols), F32),
            shape((tok_rows, kv_cols), BF16),
            shape((tok_rows, kv_cols), BF16),
        ),
        (query_low, kv_far, kv_near, own_kv, d_heads, log_total, q_seq, k_seq),
        scratch=(
            pltpu.VMEM(((key_reach + 1) * tok_rows, head), F32),
            pltpu.VMEM(((key_reach + 1) * tok_rows, head), F32),
        ),
        specs=[WHOLE] * 8,
        flops=20e9,
    )
    near = shifted(d_near, "fsdp", -1)
    far = shifted(d_far, "fsdp", -2)
    tokens_grad, keep, send = call(
        after_attention,
        (
            shape((tok_rows, width), BF16),
            shape((half_rows, qkv_cols), BF16),
            shape((half_rows, qkv_cols), BF16),
        ),
        (
            core_arg, raw, d_query, d_own, near, far, attn_rel, own, peer, tokens, gains,
            head_gains, cos_vals, sin_vals, d_state, gain_grads,
        ),
        scratch=(pltpu.VMEM((tok_rows, qkv_cols), BF16),),
        specs=[SCALAR] + [WHOLE] * 15,
        flops=20e9,
    )
    both = (keep.astype(F32) + swap_cores(send).astype(F32)).astype(BF16)
    both, mlp_parts = lax.optimization_barrier((both, mlp_parts))
    share_attn = jnp.sum(
        exchange(both.reshape(chips, SLOTS, qkv_cols)).astype(F32), axis=0
    )
    share_gains = share_attn[GAIN_SLOT, :gain_count]

    share_mlp = jnp.sum(mlp_parts.astype(F32), axis=0)
    block_rows = width // blocks
    group = size // blocks
    strip = jnp.concatenate([share_mlp[:block_rows], share_mlp[block_rows : 2 * block_rows]], axis=1)
    strip = lax.all_to_all(
        strip.reshape(group, shard, gu_cols // group),
        "fsdp",
        split_axis=0,
        concat_axis=0,
        tiled=True,
        axis_index_groups=[[b * group + i for i in range(group)] for b in range(blocks)],
    )
    share_gate_up = strip.transpose(1, 0, 2).reshape(shard, gu_cols)
    down_at = 2 * block_rows
    out_at = down_at + down_rows * (width // LANES)
    share_down = (
        share_mlp[down_at:out_at]
        .reshape(width // LANES, down_rows, LANES)
        .transpose(1, 0, 2)
        .reshape(down_rows, width)
    )
    out_tiles = share_mlp[out_at:].reshape(3, 2, SLOTS, LANES)
    mine = jnp.where(core == 0, out_tiles[:, 0], out_tiles[:, 1])
    theirs = swap_cores(jnp.where(core == 0, out_tiles[:, 1], out_tiles[:, 0]))
    first = jnp.where(core == 0, mine[:2], theirs[:2])
    second = jnp.where(core == 0, theirs[:2], mine[:2])
    share_output = (
        jnp.concatenate([first, second, mine[2:]], axis=0)
        .transpose(1, 0, 2)
        .reshape(SLOTS, width)
    )
    return (
        mixed,
        tokens_grad,
        share_attn[:shard, :q_cols],
        share_attn[:shard, q_cols:],
        share_output,
        share_gate_up,
        share_down,
        share_gains[:shard],
        share_gains[shard : 2 * shard],
        share_gains[2 * shard : 3 * shard],
        share_gains[3 * shard : 4 * shard],
        share_gains[4 * shard : 4 * shard + hshard],
        share_gains[4 * shard + hshard :],
    )


def solution(mesh):
    placed = (
        P("fsdp", None),
        P("fsdp", None),
        P(),
        P(),
        P("fsdp", None),
        P("fsdp", None),
        P("fsdp", None),
        P("fsdp", None),
        P("fsdp", None),
        P("fsdp"),
        P("fsdp"),
        P("fsdp"),
        P("fsdp"),
        P("fsdp"),
        P("fsdp"),
    )
    return jax.shard_map(
        on_device,
        mesh=mesh,
        in_specs=placed,
        out_specs=(
            P("fsdp", None),
            P("fsdp", None),
            P("fsdp", None),
            P("fsdp", None),
            P("fsdp", None),
            P("fsdp", None),
            P("fsdp", None),
            P("fsdp"),
            P("fsdp"),
            P("fsdp"),
            P("fsdp"),
            P("fsdp"),
            P("fsdp"),
        ),
        check_vma=False,
    )
```

profile of v0, /device:TPU:0, one launch (start us, length us, event | category | flops | bytes accessed | tf_op | source)
XLA Modules:
  0.0 307.5 jit_solution(12923285225317510403)
XLA Ops:
  7.2 0.0 all-gather.2.cloned.1.call-start
  7.2 1.5 pad.9
  8.7 0.0 all-gather.2.cloned.1.call-update
  8.7 4.1 %concatenate.19 = bf16[24]{0:T(256)(128)(2,1)S(1)} concatenate(bf16[5]{0:T(256)(128)(2,1)} %param.24, bf16[5]{0:T(256)(128)(2,1)} %param.25, bf16[5]{0:T(256)(128)(2,1)} %param.26, bf16[5]{0:T(256)(128)(2,1)} %param.27, bf16[2]{0:T(256)(128)(2,1)} %param.28, bf16[2]{0:T(256)(128)(2,1)} %param.29), dimensions={0} | concatenate | bytes 96 | tf_op jit(solution)/shard_map/concatenate | solution.py:491
  12.9 0.8 pad_maximum_fusion.1
  13.6 0.0 copy-start.3
  13.7 0.0 copy-start.4
  13.7 0.2 broadcast_in_dim.40
  13.8 43.7 %all_to_all.25 = bf16[64,8,2176]{2,1,0:T(8,128)(2,1)S(1)} all-to-all(bf16[64,8,2176]{2,1,0:T(8,128)(2,1)S(1)} %broadcast_in_dim.40), channel_id=1, replica_groups={{0,2,4,6,8,10,12,14,16,18,20,22,24,26,28,30,32,34,36,38,40,42,44,46,48,..., dimensions={0} | all-to-all | bytes 4456448 | tf_op jit(solution)/shard_map/all_to_all | solution.py:53
  57.5 0.0 collective-permute-start
  57.6 0.1 select_reduce_fusion.1
  57.7 0.1 fusion.6
  57.8 0.1 select_reduce_fusion
  57.9 1.2 multiply_sine_fusion
  59.2 2.8 collective-permute-done.peer
  62.0 0.0 copy-done
  62.0 6.8 %shard_map.246 = (bf16[256,1024]{1,0:T(8,128)(2,1)}, f32[256,1536]{1,0:T(8,128)}, bf16[256,1024]{1,0:T(8,128)(2,1)}, bf16[256,512]{1,0:T(8,128)(2,1)}, f32[8,640]{1,0:T(8,128)}, /*index=5*/f32[8,256]{1,0:T(8,128)}) custom-call(s32[1]{0:T(128)} %bitcast.core_ref, bf16[256,640]{1,0:T(8,128)(2,1)} %tok.5, bf16[512,2176]{1,0:T(8,128)(2,1)} %bitcast.45, ...), custom_call_target="tpu_custom_call" | custom-call | flops 4000000000 | bytes 8000000 | tf_op jit(solution)/shard_map/pallas_call | solution.py:69
  68.8 2.4 collective-permute-start.1
  71.2 1.8 collective-permute-start.2
  73.0 0.1 fusion.1
  73.1 0.8 copy.35.q_seq
  73.9 0.6 select_n.82.k_seq
  74.5 0.0 copy-done.2
  74.5 1.3 broadcast_in_dim.41
  75.7 8.5 %all-to-all-start.1 = ((bf16[64,16,640]{2,1,0:T(8,128)(2,1)}), bf16[64,16,640]{2,1,0:T(8,128)(2,1)S(1)}, u32[]{:S(2)}, u32[]{:S(2)}) async-start(bf16[64,16,640]{2,1,0:T(8,128)(2,1)} %broadcast_in_dim.41), calls=%async_computation.1 | async-start | bytes 2621440 | tf_op jit(solution)/shard_map/all_to_all | solution.py:53
  84.2 0.0 collective-permute-done.1.kv_far
  84.2 0.0 collective-permute-done.2.kv_near
  84.3 0.7 copy-done.5
  85.0 0.1 copy-done.6
  85.0 6.9 %shard_map.247 = (bf16[256,1024]{1,0:T(8,128)(2,1)}, f32[256,128]{1,0:T(8,128)}, f32[256,640]{1,0:T(8,128)}, f32[256,640]{1,0:T(8,128)}) custom-call(s32[1]{0:T(128)} %bitcast.core_ref, bf16[256,1024]{1,0:T(8,128)(2,1)} %get-tuple-element.44.query_low, bf16[256,512]{1,0:T(8,128)(2,1)} %copy-done.5, bf16[256,512]{1,0:T(8,128)(2,1)} %copy-done.6, ...), custom_call_target="tpu_custom_call" | custom-call | flops 20000000000 | bytes 8000000 | tf_op jit(solution)/shard_map/pallas_call | solution.py:69
  92.0 24.2 %all-to-all-done.1.own_down = bf16[64,16,640]{2,1,0:T(8,128)(2,1)S(1)} async-done(((bf16[64,16,640]{2,1,0:T(8,128)(2,1)}), bf16[64,16,640]{2,1,0:T(8,128)(2,1)S(1)}, u32[]{:S(2)}, u32[]{:S(2)}) %all-to-all-start.1) | async-done | bytes 1310752 | tf_op jit(solution)/shard_map/all_to_all | solution.py:53
  116.2 0.1 collective-permute-start.3
  116.2 1.0 copy.36.live
  117.2 2.1 collective-permute-done.3.peer_down
  119.3 26.8 %shard_map.248 = (bf16[256,640]{1,0:T(8,128)(2,1)}, f32[256,640]{1,0:T(8,128)}, bf16[256,1024]{1,0:T(8,128)(2,1)}, f32[8,640]{1,0:T(8,128)}, bf16[8,8,288,128]{3...) custom-call(s32[1]{0:T(128)} %bitcast.core_ref, f32[256,640]{1,0:T(8,128)} %get-tuple-element.48.state, ...), custom_call_target="tpu_custom_call" | custom-call | flops 12000000000 | bytes 8000000 | tf_op jit(solution)/shard_map/pallas_call | solution.py:69
  146.2 0.2 collective-permute-start.7
  146.4 8.0 %collective-permute-done.7 = bf16[8,8,288,128]{3,2,1,0:T(8,128)(2,1)S(1)} collective-permute-done((bf16[8,8,288,128]{3,2,1,0:T(8,128)(2,1)}, bf16[8,8,288,128]{3,2,1,0:T(8,128)(2,1)S(1)}, u32[]{:S(2)}, u32[]{:S(2)}) %collective-permute-start.7) | collective-permute-done | bytes 4718624 | tf_op jit(solution)/shard_map/ppermute | solution.py:49
  154.4 5.8 %add_convert_fusion = bf16[8,8,288,128]{3,2,1,0:T(8,128)(2,1)} fusion(bf16[8,8,288,128]{3,2,1,0:T(8,128)(2,1)S(1)} %collective-permute-done.7, bf16[8,8,288,128]{3,2,1,0:T(8,128)(2,1)} %get-tuple-element.67), kind=kLoop, calls=%fused_computation.1 | loop fusion | flops 9437184 | bytes 14155776 | tf_op jit(solution)/shard_map/convert_element_type | solution.py:590
  160.2 5.9 %all-to-all-start.2 = ((bf16[64,288,128]{2,1,0:T(8,128)(2,1)}), bf16[64,288,128]{2,1,0:T(8,128)(2,1)}, u32[]{:S(2)}, u32[]{:S(2)}) async-start(bf16[64,288,128]{2,1,0:T(8,128)(2,1)} %bitcast.43), calls=%async_computation.2 | async-start | bytes 9437184 | tf_op jit(solution)/shard_map/all_to_all | solution.py:53
  166.1 6.2 %shard_map.249 = (f32[256,1024]{1,0:T(8,128)}, f32[256,512]{1,0:T(8,128)}, bf16[256,512]{1,0:T(8,128)(2,1)}, bf16[256,512]{1,0:T(8,128)(2,1)}) custom-call(bf16[256,1024]{1,0:T(8,128)(2,1)} %get-tuple-element.44.query_low, bf16[256,512]{1,0:T(8,128)(2,1)} %copy-done.5, bf16[256,512]{1,0:T(8,128)(2,1)} %copy-done.6, ...), custom_call_target="tpu_custom_call" | custom-call | flops 20000000000 | bytes 8000000 | tf_op jit(solution)/shard_map/pallas_call | solution.py:69
  172.3 1.3 collective-permute-start.4
  173.6 1.3 collective-permute-start.5
  174.9 1.0 collective-permute-done.4.near
  175.9 54.2 %collective-permute-done.5.far = bf16[256,512]{1,0:T(8,128)(2,1)S(1)} collective-permute-done((bf16[256,512]{1,0:T(8,128)(2,1)}, bf16[256,512]{1,0:T(8,128)(2,1)S(1)}, u32[]{:S(2)}, u32[]{:S(2)}) %collective-permute-start.5) | collective-permute-done | bytes 262176 | tf_op jit(solution)/shard_map/ppermute | solution.py:19
  230.1 0.7 copy-done.8
  230.8 9.7 %shard_map.250 = (bf16[256,640]{1,0:T(8,128)(2,1)}, bf16[512,1536]{1,0:T(8,128)(2,1)}, bf16[512,1536]{1,0:T(8,128)(2,1)}) custom-call(s32[1]{0:T(128)} %bitcast.core_ref, f32[256,1536]{1,0:T(8,128)} %get-tuple-element.53.raw, f32[256,1024]{1,0:T(8,128)} %get-tuple-element.56.d_query, f32[256,512]{1,0:T(8,128)} %get-tuple-element.57.d_own, ...), custom_call_target="tpu_custom_call" | custom-call | flops 20000000000 | bytes 8000000 | tf_op jit(solution)/shard_map/pallas_call | solution.py:69
  240.5 0.0 collective-permute-start.6
  240.5 3.6 %collective-permute-done.6 = bf16[512,1536]{1,0:T(8,128)(2,1)S(1)} collective-permute-done((bf16[512,1536]{1,0:T(8,128)(2,1)}, bf16[512,1536]{1,0:T(8,128)(2,1)S(1)}, u32[]{:S(2)}, u32[]{:S(2)}) %collective-permute-start.6) | collective-permute-done | bytes 1572896 | tf_op jit(solution)/shard_map/ppermute | solution.py:49
  244.1 2.9 add_convert_fusion.1
  247.1 0.0 all-to-all-done.2
  247.1 3.0 convert_reduce_fusion
  250.2 11.6 %all_to_all.26 = f32[16,5,256]{2,1,0:T(8,128)S(1)} all-to-all(f32[16,5,256]{2,1,0:T(8,128)S(1)} %reshape.129), channel_id=1, replica_groups={{0,1,2,3,4,5,6,7,8,9,10,11,12,13,14,15},{16,17,18,19,20,21,22,23,24,25,..., dimensions={0} | all-to-all | bytes 163840 | tf_op jit(solution)/shard_map/all_to_all | solution.py:636
  261.7 10.9 %all-to-all-start.3 = ((bf16[64,8,1536]{2,1,0:T(8,128)(2,1)}), bf16[64,8,1536]{2,1,0:T(8,128)(2,1)S(1)}, u32[]{:S(2)}, u32[]{:S(2)}) async-start(bf16[64,8,1536]{2,1,0:T(8,128)(2,1)} %bitcast.5), calls=%async_computation.3 | async-start | bytes 3145728 | tf_op jit(solution)/shard_map/all_to_all | solution.py:53
  272.6 0.1 collective-permute-start.8
  272.7 0.6 copy.41
  273.4 0.5 collective-permute-done.8
  273.9 0.6 maximum_bitcast_fusion
  274.5 22.9 %all-to-all-done.3 = bf16[64,8,1536]{2,1,0:T(8,128)(2,1)S(1)} async-done(((bf16[64,8,1536]{2,1,0:T(8,128)(2,1)}), bf16[64,8,1536]{2,1,0:T(8,128)(2,1)S(1)}, u32[]{:S(2)}, u32[]{:S(2)}) %all-to-all-start.3) | async-done | bytes 1572896 | tf_op jit(solution)/shard_map/all_to_all | solution.py:53
  297.4 0.2 convert_reduce_fusion.1
  297.6 0.6 slice.111
  298.2 0.6 slice.112
  298.8 0.6 slice_bitcast_fusion.4
  299.4 0.6 slice_bitcast_fusion.2
  300.0 0.7 copy.43
  (29 shorter events, 0.1 us)
Async XLA Ops:
  7.2 112.1 %all-gather.2.cloned.1.call-start = ((), (), s32[]{:S(2)}) async-start(), calls=%async_computation.5 | async-start | bytes 8454144 | tf_op jit(solution)/shard_map/all_gather | solution.py:487
  13.6 43.9 %copy-start.3 = (s32[25]{0:T(128)S(1)}, s32[25]{0:T(128)}, u32[]{:S(2)}) copy-start(s32[25]{0:T(128)} %param.18) | copy-start | bytes 304
  13.7 43.9 %copy-start.4 = (s32[25]{0:T(128)S(1)}, s32[25]{0:T(128)}, u32[]{:S(2)}) copy-start(s32[25]{0:T(128)} %param.17) | copy-start | bytes 304
  57.5 4.5 %copy-start = (bf16[64,8,2176]{2,1,0:T(8,128)(2,1)}, bf16[64,8,2176]{2,1,0:T(8,128)(2,1)S(1)}, u32[]{:S(2)}) copy-start(bf16[64,8,2176]{2,1,0:T(8,128)(2,1)S(1)} %all_to_all.25) | copy-start | bytes 6684676
  57.5 4.5 %collective-permute-start = (bf16[512,2176]{1,0:T(8,128)(2,1)S(1)}, bf16[512,2176]{1,0:T(8,128)(2,1)}, u32[]{:S(2)}, u32[]{:S(2)}) collective-permute-start(bf16[512,2176]{1,0:T(8,128)(2,1)S(1)} %bitcast.44), channel_id=1, source_target_pairs={{0,1},{1,0},{2,3},{3,2},{4,5},{5,4},{6,7},{7,6},{8,9},{9,8},{10,11... | collective-permute-start | bytes 6684680 | tf_op jit(solution)/shard_map/ppermute | solution.py:49
  62.0 12.4 %copy-start.2 = (bf16[16,640]{1,0:T(8,128)(2,1)S(1)}, bf16[16,640]{1,0:T(8,128)(2,1)}, u32[]{:S(2)}) copy-start(bf16[16,640]{1,0:T(8,128)(2,1)} %param.23) | copy-start | bytes 61444
  68.8 15.4 %collective-permute-start.1 = (bf16[256,512]{1,0:T(8,128)(2,1)}, bf16[256,512]{1,0:T(8,128)(2,1)S(1)}, u32[]{:S(2)}, u32[]{:S(2)}) collective-permute-start(bf16[256,512]{1,0:T(8,128)(2,1)} %get-tuple-element.45.kv_own), channel_id=1, source_target_pairs={{0,2},{1,3},{2,4},{3,5},{4,6},{5,7},{6,8},{7,9},{8,10},{9,11},{10,... | collective-permute-start | bytes 786440 | tf_op jit(solution)/shard_map/ppermute | solution.py:19
  71.2 13.1 %collective-permute-start.2 = (bf16[256,512]{1,0:T(8,128)(2,1)}, bf16[256,512]{1,0:T(8,128)(2,1)S(1)}, u32[]{:S(2)}, u32[]{:S(2)}) collective-permute-start(bf16[256,512]{1,0:T(8,128)(2,1)} %get-tuple-element.45.kv_own), channel_id=1, source_target_pairs={{0,1},{1,2},{2,3},{3,4},{4,5},{5,6},{6,7},{7,8},{8,9},{9,10},{10,1... | collective-permute-start | bytes 786440 | tf_op jit(solution)/shard_map/ppermute | solution.py:19
  75.7 40.4 %all-to-all-start.1 = ((bf16[64,16,640]{2,1,0:T(8,128)(2,1)}), bf16[64,16,640]{2,1,0:T(8,128)(2,1)S(1)}, u32[]{:S(2)}, u32[]{:S(2)}) async-start(bf16[64,16,640]{2,1,0:T(8,128)(2,1)} %broadcast_in_dim.41), calls=%async_computation.1 | async-start | bytes 2621440 | tf_op jit(solution)/shard_map/all_to_all | solution.py:53
  84.2 0.7 copy-start.5
  84.3 0.8 copy-start.6
  116.2 3.2 %copy-start.1 = (bf16[64,16,640]{2,1,0:T(8,128)(2,1)}, bf16[64,16,640]{2,1,0:T(8,128)(2,1)S(1)}, u32[]{:S(2)}) copy-start(bf16[64,16,640]{2,1,0:T(8,128)(2,1)S(1)} %all-to-all-done.1.own_down) | copy-start | bytes 3932164
  116.2 3.2 %collective-permute-start.3 = (bf16[64,16,640]{2,1,0:T(8,128)(2,1)S(1)}, bf16[64,16,640]{2,1,0:T(8,128)(2,1)}, u32[]{:S(2)}, u32[]{:S(2)}) collective-permute-start(bf16[64,16,640]{2,1,0:T(8,128)(2,1)S(1)} %all-to-all-done.1.own_down), channel_id=1, source_target_pairs={{0,1},{1,0},{2,3},{3,2},{4,5},{5,4},{6,7},{7,6},{8,9},{9,8},{10,11... | collective-permute-start | bytes 3932168 | tf_op jit(solution)/shard_map/ppermute | solution.py:49
  146.2 8.2 %collective-permute-start.7 = (bf16[8,8,288,128]{3,2,1,0:T(8,128)(2,1)}, bf16[8,8,288,128]{3,2,1,0:T(8,128)(2,1)S(1)}, u32[]{:S(2)}, u32[]{:S(2)}) collective-permute-start(bf16[8,8,288,128]{3,2,1,0:T(8,128)(2,1)} %get-tuple-element.68), channel_id=1, source_target_pairs={{0,1},{1,0},{2,3},{3,2},{4,5},{5,4},{6,7},{7,6},{8,9},{9,8},{10,11... | collective-permute-start | bytes 14155784 | tf_op jit(solution)/shard_map/ppermute | solution.py:49
  160.2 86.9 %all-to-all-start.2 = ((bf16[64,288,128]{2,1,0:T(8,128)(2,1)}), bf16[64,288,128]{2,1,0:T(8,128)(2,1)}, u32[]{:S(2)}, u32[]{:S(2)}) async-start(bf16[64,288,128]{2,1,0:T(8,128)(2,1)} %bitcast.43), calls=%async_computation.2 | async-start | bytes 9437184 | tf_op jit(solution)/shard_map/all_to_all | solution.py:53
  172.3 3.6 %collective-permute-start.4 = (bf16[256,512]{1,0:T(8,128)(2,1)}, bf16[256,512]{1,0:T(8,128)(2,1)S(1)}, u32[]{:S(2)}, u32[]{:S(2)}) collective-permute-start(bf16[256,512]{1,0:T(8,128)(2,1)} %get-tuple-element.58), channel_id=1, source_target_pairs={{1,0},{2,1},{3,2},{4,3},{5,4},{6,5},{7,6},{8,7},{9,8},{10,9},{11,1... | collective-permute-start | bytes 786440 | tf_op jit(solution)/shard_map/ppermute | solution.py:19
  173.6 56.5 %collective-permute-start.5 = (bf16[256,512]{1,0:T(8,128)(2,1)}, bf16[256,512]{1,0:T(8,128)(2,1)S(1)}, u32[]{:S(2)}, u32[]{:S(2)}) collective-permute-start(bf16[256,512]{1,0:T(8,128)(2,1)} %get-tuple-element.59), channel_id=1, source_target_pairs={{2,0},{3,1},{4,2},{5,3},{6,4},{7,5},{8,6},{9,7},{10,8},{11,9},{12,... | collective-permute-start | bytes 786440 | tf_op jit(solution)/shard_map/ppermute | solution.py:19
  175.9 54.2 %copy-start.7 = (bf16[256,512]{1,0:T(8,128)(2,1)}, bf16[256,512]{1,0:T(8,128)(2,1)S(1)}, u32[]{:S(2)}) copy-start(bf16[256,512]{1,0:T(8,128)(2,1)S(1)} %collective-permute-done.4.near) | copy-start | bytes 786436
  230.1 0.7 copy-start.8
  240.5 3.6 %collective-permute-start.6 = (bf16[512,1536]{1,0:T(8,128)(2,1)}, bf16[512,1536]{1,0:T(8,128)(2,1)S(1)}, u32[]{:S(2)}, u32[]{:S(2)}) collective-permute-start(bf16[512,1536]{1,0:T(8,128)(2,1)} %get-tuple-element.66), channel_id=1, source_target_pairs={{0,1},{1,0},{2,3},{3,2},{4,5},{5,4},{6,7},{7,6},{8,9},{9,8},{10,11... | collective-permute-start | bytes 4718600 | tf_op jit(solution)/shard_map/ppermute | solution.py:49
  261.7 35.6 %all-to-all-start.3 = ((bf16[64,8,1536]{2,1,0:T(8,128)(2,1)}), bf16[64,8,1536]{2,1,0:T(8,128)(2,1)S(1)}, u32[]{:S(2)}, u32[]{:S(2)}) async-start(bf16[64,8,1536]{2,1,0:T(8,128)(2,1)} %bitcast.5), calls=%async_computation.3 | async-start | bytes 3145728 | tf_op jit(solution)/shard_map/all_to_all | solution.py:53
  272.6 1.3 collective-permute-start.8
Sparse Core Ops, SparseCore 0:
  11.6 102.4 all-gather.1
where the time goes:
time: 308 us
  waiting for transfers between devices  119 us (39%)
  Pallas kernels  56.4 us (18%)
  blocking collectives  55.3 us (18%)
  starting transfers between devices  32.4 us (11%)
  other arithmetic  15.1 us (5%)
  local copies, waits for them, and re-layouts  14.6 us (5%)
  between operations  14.3 us (5%)
    pallas_call x5, Pallas kernels, call(): pl.pallas_call(kernel, out_shape=outs, in_specs=specs, scratch_shapes=lis...  56.4 us
    ppermute x4, waiting for transfers between devices, shifted(): return lax.ppermute(block, axis, route)  55.2 us
    all_to_all x3, waiting for transfers between devices, exchange(): lax.all_to_all(blocks, 'fsdp', split_axis=0, concat_axis=0, tiled=True, a...  47.1 us
    all_to_all x1, blocking collectives, exchange(): lax.all_to_all(blocks, 'fsdp', split_axis=0, concat_axis=0, tiled=True, a...  43.7 us
    all_to_all x3, starting transfers between devices, exchange(): lax.all_to_all(blocks, 'fsdp', split_axis=0, concat_axis=0, tiled=True, a...  25.3 us
    ppermute x5, waiting for transfers between devices, swap_cores(): return lax.ppermute(block, 'fsdp', [(i, i ^ 1) for i in range(size)])  17.1 us
    all_to_all x1, blocking collectives, on_device(): lax.all_to_all(strip.reshape(group, shard, gu_cols // group), 'fsdp', spl...  11.6 us
    ppermute x4, starting transfers between devices, shifted(): return lax.ppermute(block, axis, route)  6.74 us
  transfers between devices with their start and end apart: 13, of which 9 were waited for; matrix products, arithmetic and copies ran while one was open for 5% of the time, Pallas kernels for 10%

commit v1 on v0

--- a/solution.py
+++ b/solution.py
@@ -224,7 +224,7 @@
 
 
 def feed_forward(
-    core_ref, state, proj, out_grad, live, gains, heads_low, own, peer, gate_up, own_down, peer_down,
+    core_ref, state, proj, out_grad, live, gains, heads_low, own, peer, gate_up, down_full,
     mixed, d_state, d_heads, gain_grads, keep, send,
     weights, down, act, act_slope, hidden, total, back, low_flat, low, low_branch, turn, turn_down,
     turn_out, weight_sem, down_sem,
@@ -236,7 +236,7 @@
     rows = own.shape[0]
     q_cols = heads_low.shape[1]
     per = width // LANES
-    down_rows = own_down.shape[1]
+    down_rows = down_full.shape[2]
     blocks, strips = keep.shape[0], keep.shape[1]
     block_rows = width // blocks
     tile_chips = tile // (2 * down_rows)
@@ -248,24 +248,19 @@
             weight_sem.at[index],
         )
 
-    down_copies = (
-        pltpu.make_async_copy(own_down, down.at[:, core], down_sem.at[0]),
-        pltpu.make_async_copy(peer_down, down.at[:, 1 - core], down_sem.at[1]),
-    )
+    down_copy = pltpu.make_async_copy(down_full, down, down_sem)
     for index in range(half):
         weight_copy(index).start()
         weight_copy(half + index).start()
         if index == 0:
-            for copy in down_copies:
-                copy.start()
+            down_copy.start()
 
     spread_flat = pick_rows(width, weights.shape[1], per, None)
     unit, scale = normed(state[...])
     low[...] = (unit * gains[2:3, :]).astype(BF16)
     low_flat[...] = dot(low[...], spread_flat).astype(BF16)
     total[...] = jnp.zeros_like(total)
-    for copy in down_copies:
-        copy.wait()
+    down_copy.wait()
 
     def down_tile(index):
         chunk = down[pl.ds(index * tile_chips, tile_chips)]
@@ -484,23 +479,48 @@
     hshard = norm_query.shape[0]
     half_rows = chips * SLOTS
 
-    gateup_flat = lax.all_gather(
-        jnp.pad(w_gate_up, ((0, SLOTS - shard), (0, 0))), "fsdp", axis=0, tiled=True
-    )
-
-    gain_row = jnp.concatenate(
-        [norm_attn_in, norm_attn_out, norm_mlp_in, norm_mlp_out, norm_query, norm_key]
-    )
-    gain_count = gain_row.shape[0]
-    pack = jnp.concatenate(
+    mlp_full = lax.all_gather(
+        jnp.concatenate(
+            [
+                jnp.pad(w_gate_up, ((0, SLOTS - shard), (0, 0))),
+                w_down[:SLOTS],
+                w_down[SLOTS:],
+            ],
+            axis=1,
+        ),
+        "fsdp",
+        axis=0,
+        tiled=True,
+    )
+    down_full = jnp.concatenate(
         [
-            jnp.concatenate([w_query, w_key_value], axis=1),
-            jnp.pad(gain_row, (0, qkv_cols - gain_count))[None],
-            jnp.zeros((SLOTS - shard - 1, qkv_cols), BF16),
+            mlp_full[:, gu_cols : gu_cols + width].reshape(chips, 2, SLOTS, width),
+            mlp_full[:, gu_cols + width :].reshape(chips, 2, SLOTS, width),
         ],
-        axis=0,
-    )
-    own_attn = spread(jnp.concatenate([pack, w_output], axis=1))
+        axis=2,
+    )
+
+    pack = jnp.zeros((SLOTS, qkv_cols + width), BF16)
+    gain_count = 0
+    for row, column, part in (
+        (0, 0, w_query),
+        (0, q_cols, w_key_value),
+        (0, qkv_cols, w_output),
+        (GAIN_SLOT, None, norm_attn_in[None]),
+        (GAIN_SLOT, None, norm_attn_out[None]),
+        (GAIN_SLOT, None, norm_mlp_in[None]),
+        (GAIN_SLOT, None, norm_mlp_out[None]),
+        (GAIN_SLOT, None, norm_query[None]),
+        (GAIN_SLOT, None, norm_key[None]),
+    ):
+        high, wide = part.shape
+        if column is None:
+            column = gain_count
+            gain_count += wide
+        pack = pack + jnp.pad(
+            part, ((row, SLOTS - row - high), (column, qkv_cols + width - column - wide))
+        )
+    own_attn = spread(pack)
     own = own_attn.reshape(half_rows, qkv_cols + width)
     peer = swap_cores(own)
 
@@ -529,8 +549,6 @@
         (core_arg, tokens, own, peer, cos_vals, sin_vals),
         specs=[SCALAR] + [WHOLE] * 5,
     )
-    down_block, own_kv = lax.optimization_barrier((w_down, own_kv))
-    own_down = spread(down_block)
     kv_near = shifted(own_kv, "fsdp", 1)
     kv_far = shifted(own_kv, "fsdp", 2)
     heads_low, log_total, proj, state = call(
@@ -545,9 +563,6 @@
         specs=[SCALAR] + [WHOLE] * 10,
         flops=20e9,
     )
-
-    own_down, state = lax.optimization_barrier((own_down, state))
-    peer_down = swap_cores(own_down)
 
     tile = 512
     blocks, strips = 8, chips // 8
@@ -564,7 +579,7 @@
         ),
         (
             core_arg, state, proj, out_grad, live, gains, heads_low, own, peer,
-            gateup_flat, own_down, peer_down,
+            mlp_full, down_full,
         ),
         scratch=(
             pltpu.VMEM((gu_cols // tile, size * SLOTS, tile), BF16),
@@ -581,13 +596,12 @@
             pltpu.VMEM((tile // (2 * down_rows) // strips, strips, 2, down_rows, width), BF16),
             pltpu.VMEM((width // LANES, blocks, strips, 2 * SLOTS, LANES), BF16),
             pltpu.SemaphoreType.DMA((gu_cols // tile,)),
-            pltpu.SemaphoreType.DMA((2,)),
-        ),
-        specs=[SCALAR] + [WHOLE] * 8 + [AWAY] * 3,
+            pltpu.SemaphoreType.DMA,
+        ),
+        specs=[SCALAR] + [WHOLE] * 8 + [AWAY] * 2,
         flops=12e9,
     )
-    both = keep.astype(F32) + swap_cores(send).astype(F32)
-    mlp_parts = exchange(both.astype(BF16).reshape(chips, chunk_rows, LANES))
+    both_mlp = (keep.astype(F32) + swap_cores(send).astype(F32)).astype(BF16)
 
     d_query, d_own, d_near, d_far = call(
         attention_back,
@@ -607,6 +621,8 @@
     )
     near = shifted(d_near, "fsdp", -1)
     far = shifted(d_far, "fsdp", -2)
+    both_mlp, near, far = lax.optimization_barrier((both_mlp, near, far))
+    mlp_parts = exchange(both_mlp.reshape(chips, chunk_rows, LANES))
     tokens_grad, keep, send = call(
         after_attention,
         (

time: 308 us -> 282 us (0.916)
  waiting for transfers between devices: 119 us -> 100 us
  starting transfers between devices: 32.4 us -> 26.6 us
  local copies, waits for them, and re-layouts: 14.6 us -> 10.3 us
  other arithmetic: 15.1 us -> 18.5 us
    ppermute x4, waiting for transfers between devices: 55.2 us -> 9.15 us  [shifted(): return lax.ppermute(block, axis, route)]
    all_gather x1, waiting for transfers between devices: 0.01 us -> 19.1 us  [on_device(): lax.all_gather(jnp.concatenate([jnp.pad(w_gate_up, ((0, SLOTS - shard), (...]
    all_to_all x3 -> x2, waiting for transfers between devices: 47.1 us -> 65.1 us  [exchange(): lax.all_to_all(blocks, 'fsdp', split_axis=0, concat_axis=0, tiled=True, a...]
    ppermute x5 -> x4, waiting for transfers between devices: 17.1 us -> 7.01 us  [swap_cores(): return lax.ppermute(block, 'fsdp', [(i, i ^ 1) for i in range(size)])]
    all_to_all x3 -> x2, starting transfers between devices: 25.3 us -> 19 us  [exchange(): lax.all_to_all(blocks, 'fsdp', split_axis=0, concat_axis=0, tiled=True, a...]
    concatenate x1 -> x0, local copies, waits for them, and re-layouts: 4.1 us -> none  [on_device(): jnp.concatenate([norm_attn_in, norm_attn_out, norm_mlp_in, norm_mlp_out,...]
  transfers between devices with their start and end apart: 13 -> 11, of which waited for: 9 -> 8; matrix products, arithmetic and copies ran while one was open for 5% -> 5% of each run, Pallas kernels for 10% -> 11%
where the time goes in v1:
time: 282 us; the launch traced here: 281 us
  waiting for transfers between devices  100 us (35%)
  Pallas kernels  56.6 us (20%)
  blocking collectives  54.1 us (19%)
  starting transfers between devices  26.6 us (9%)
  other arithmetic  18.5 us (7%)
  between operations  14.3 us (5%)
  local copies, waits for them, and re-layouts  10.3 us (4%)
    all_to_all x2, waiting for transfers between devices, exchange(): lax.all_to_all(blocks, 'fsdp', split_axis=0, concat_axis=0, tiled=True, a...  65.1 us
    pallas_call x5, Pallas kernels, call(): pl.pallas_call(kernel, out_shape=outs, in_specs=specs, scratch_shapes=lis...  56.6 us
    all_to_all x1, blocking collectives, exchange(): lax.all_to_all(blocks, 'fsdp', split_axis=0, concat_axis=0, tiled=True, a...  43.9 us
    all_gather x1, waiting for transfers between devices, on_device(): lax.all_gather(jnp.concatenate([jnp.pad(w_gate_up, ((0, SLOTS - shard), (...  19.1 us
    all_to_all x2, starting transfers between devices, exchange(): lax.all_to_all(blocks, 'fsdp', split_axis=0, concat_axis=0, tiled=True, a...  19 us
    all_to_all x1, blocking collectives, on_device(): lax.all_to_all(strip.reshape(group, shard, gu_cols // group), 'fsdp', spl...  10.2 us
    ppermute x4, waiting for transfers between devices, shifted(): return lax.ppermute(block, axis, route)  9.15 us
    ppermute x4, waiting for transfers between devices, swap_cores(): return lax.ppermute(block, 'fsdp', [(i, i ^ 1) for i in range(size)])  7.01 us
  transfers between devices with their start and end apart: 11, of which 8 were waited for; matrix products, arithmetic and copies ran while one was open for 5% of the time, Pallas kernels for 11%

profile of v1, /device:TPU:0, one launch (start us, length us, event | category | flops | bytes accessed | tf_op | source)
XLA Modules:
  0.0 280.8 jit_solution(15980498636176290309)
XLA Ops:
  7.2 0.0 all-gather.2.cloned.1.call-start
  7.2 0.7 fusion.12
  7.9 1.5 fusion.3
  9.4 0.0 all-gather.2.cloned.1.call-update
  9.5 0.9 pad_add_fusion
  10.4 0.2 broadcast_in_dim.73
  10.6 0.0 copy-start.1
  10.6 0.0 copy-start.2
  10.6 43.9 %all_to_all.20 = bf16[64,8,2176]{2,1,0:T(8,128)(2,1)S(1)} all-to-all(bf16[64,8,2176]{2,1,0:T(8,128)(2,1)S(1)} %broadcast_in_dim.73), channel_id=1, replica_groups={{0,2,4,6,8,10,12,14,16,18,20,22,24,26,28,30,32,34,36,38,40,42,44,46,48,..., dimensions={0} | all-to-all | bytes 4456448 | tf_op jit(solution)/shard_map/all_to_all | solution.py:53
  54.5 0.0 collective-permute-start
  54.5 0.0 copy-done.1
  54.5 0.1 select_reduce_fusion.1
  54.6 0.1 fusion.9
  54.7 0.1 select_reduce_fusion
  54.8 1.2 multiply_sine_fusion
  56.1 2.9 %collective-permute-done.peer = bf16[512,2176]{1,0:T(8,128)(2,1)} collective-permute-done((bf16[512,2176]{1,0:T(8,128)(2,1)S(1)}, bf16[512,2176]{1,0:T(8,128)(2,1)}, u32[]{:S(2)}, u32[]{:S(2)}) %collective-permute-start) | collective-permute-done | bytes 2228256 | tf_op jit(solution)/shard_map/ppermute | solution.py:49
  58.9 0.0 copy-done
  58.9 6.8 %shard_map.246 = (bf16[256,1024]{1,0:T(8,128)(2,1)}, f32[256,1536]{1,0:T(8,128)}, bf16[256,1024]{1,0:T(8,128)(2,1)}, bf16[256,512]{1,0:T(8,128)(2,1)}, f32[8,640]{1,0:T(8,128)}, /*index=5*/f32[8,256]{1,0:T(8,128)}) custom-call(s32[1]{0:T(128)} %bitcast.core_ref, bf16[256,640]{1,0:T(8,128)(2,1)} %tok.5, bf16[512,2176]{1,0:T(8,128)(2,1)} %bitcast.57, ...), custom_call_target="tpu_custom_call" | custom-call | flops 4000000000 | bytes 8000000 | tf_op jit(solution)/shard_map/pallas_call | solution.py:69
  65.7 2.4 collective-permute-start.1
  68.1 2.0 collective-permute-start.2
  70.1 0.1 fusion.4
  70.2 0.8 copy.35.q_seq
  71.0 0.6 select_n.82.k_seq
  71.6 0.8 copy.36.live
  72.4 3.6 %collective-permute-done.1.kv_far = bf16[256,512]{1,0:T(8,128)(2,1)S(1)} collective-permute-done((bf16[256,512]{1,0:T(8,128)(2,1)}, bf16[256,512]{1,0:T(8,128)(2,1)S(1)}, u32[]{:S(2)}, u32[]{:S(2)}) %collective-permute-start.1) | collective-permute-done | bytes 262176 | tf_op jit(solution)/shard_map/ppermute | solution.py:19
  76.0 0.0 collective-permute-done.2.kv_near
  76.0 0.7 copy-done.3
  76.7 0.1 copy-done.4
  76.8 6.9 %shard_map.247 = (bf16[256,1024]{1,0:T(8,128)(2,1)}, f32[256,128]{1,0:T(8,128)}, f32[256,640]{1,0:T(8,128)}, f32[256,640]{1,0:T(8,128)}) custom-call(s32[1]{0:T(128)} %bitcast.core_ref, bf16[256,1024]{1,0:T(8,128)(2,1)} %get-tuple-element.41.query_low, bf16[256,512]{1,0:T(8,128)(2,1)} %copy-done.3, bf16[256,512]{1,0:T(8,128)(2,1)} %copy-done.4, ...), custom_call_target="tpu_custom_call" | custom-call | flops 20000000000 | bytes 8000000 | tf_op jit(solution)/shard_map/pallas_call | solution.py:69
  83.7 19.1 %all-gather.2.cloned.1.call-done.gate_up = bf16[1024,5376]{1,0:T(8,128)(2,1)} async-done(((bf16[8,5376]{1,0:T(8,128)(2,1)}), bf16[1024,5376]{1,0:T(8,128)(2,1)}) %all-gather.2.cloned.1.call-update) | async-done | bytes 11010064 | tf_op jit(solution)/shard_map/all_gather | solution.py:482
  102.8 2.0 fusion.10
  104.8 1.8 pad_maximum_fusion.down_full
  106.6 26.9 %shard_map.248 = (bf16[256,640]{1,0:T(8,128)(2,1)}, f32[256,640]{1,0:T(8,128)}, bf16[256,1024]{1,0:T(8,128)(2,1)}, f32[8,640]{1,0:T(8,128)}, bf16[8,8,288,128]{3...) custom-call(s32[1]{0:T(128)} %bitcast.core_ref, f32[256,640]{1,0:T(8,128)} %get-tuple-element.44.state, ...), custom_call_target="tpu_custom_call" | custom-call | flops 12000000000 | bytes 8000000 | tf_op jit(solution)/shard_map/pallas_call | solution.py:69
  133.5 0.6 collective-permute-start.3
  134.0 6.3 %shard_map.249 = (f32[256,1024]{1,0:T(8,128)}, f32[256,512]{1,0:T(8,128)}, bf16[256,512]{1,0:T(8,128)(2,1)}, bf16[256,512]{1,0:T(8,128)(2,1)}) custom-call(bf16[256,1024]{1,0:T(8,128)(2,1)} %get-tuple-element.41.query_low, bf16[256,512]{1,0:T(8,128)(2,1)} %copy-done.3, bf16[256,512]{1,0:T(8,128)(2,1)} %copy-done.4, ...), custom_call_target="tpu_custom_call" | custom-call | flops 20000000000 | bytes 8000000 | tf_op jit(solution)/shard_map/pallas_call | solution.py:69
  140.3 1.3 collective-permute-start.4
  141.6 1.3 collective-permute-start.5
  142.9 0.0 collective-permute-done.3
  142.9 0.0 slice-done
  142.9 0.0 slice-done.1
  142.9 5.8 %add_convert_fusion = bf16[8,8,288,128]{3,2,1,0:T(8,128)(2,1)} fusion(bf16[8,8,288,128]{3,2,1,0:T(8,128)(2,1)} %collective-permute-done.3, bf16[8,8,288,128]{3,2,1,0:T(8,128)(2,1)S(1)} %bitcast.55), kind=kLoop, calls=%fused_computation.1 | loop fusion | flops 9437184 | bytes 14155776 | tf_op jit(solution)/shard_map/convert_element_type | solution.py:604
  148.8 0.0 collective-permute-done.4.near
  148.8 5.5 %collective-permute-done.5.far = bf16[256,512]{1,0:T(8,128)(2,1)S(1)} collective-permute-done((bf16[256,512]{1,0:T(8,128)(2,1)}, bf16[256,512]{1,0:T(8,128)(2,1)S(1)}, u32[]{:S(2)}, u32[]{:S(2)}) %collective-permute-start.5) | collective-permute-done | bytes 262176 | tf_op jit(solution)/shard_map/ppermute | solution.py:19
  154.3 0.7 copy-done.6
  155.0 11.2 %all-to-all-start.1 = ((bf16[64,288,128]{2,1,0:T(8,128)(2,1)}), bf16[64,288,128]{2,1,0:T(8,128)(2,1)}, u32[]{:S(2)}, u32[]{:S(2)}) async-start(bf16[64,288,128]{2,1,0:T(8,128)(2,1)} %bitcast.51), calls=%async_computation.1 | async-start | bytes 9437184 | tf_op jit(solution)/shard_map/all_to_all | solution.py:53
  166.2 9.8 %shard_map.250 = (bf16[256,640]{1,0:T(8,128)(2,1)}, bf16[512,1536]{1,0:T(8,128)(2,1)}, bf16[512,1536]{1,0:T(8,128)(2,1)}) custom-call(s32[1]{0:T(128)} %bitcast.core_ref, f32[256,1536]{1,0:T(8,128)} %get-tuple-element.48.raw, f32[256,1024]{1,0:T(8,128)} %get-tuple-element.51.d_query, f32[256,512]{1,0:T(8,128)} %get-tuple-element.52.d_own, ...), custom_call_target="tpu_custom_call" | custom-call | flops 20000000000 | bytes 8000000 | tf_op jit(solution)/shard_map/pallas_call | solution.py:69
  176.0 0.0 collective-permute-start.6
  176.0 3.6 %collective-permute-done.6 = bf16[512,1536]{1,0:T(8,128)(2,1)S(1)} collective-permute-done((bf16[512,1536]{1,0:T(8,128)(2,1)}, bf16[512,1536]{1,0:T(8,128)(2,1)S(1)}, u32[]{:S(2)}, u32[]{:S(2)}) %collective-permute-start.6) | collective-permute-done | bytes 1572896 | tf_op jit(solution)/shard_map/ppermute | solution.py:49
  179.6 3.0 %add_convert_fusion.1 = bf16[512,1536]{1,0:T(8,128)(2,1)} fusion(bf16[512,1536]{1,0:T(8,128)(2,1)S(1)} %collective-permute-done.6, bf16[512,1536]{1,0:T(8,128)(2,1)} %get-tuple-element.64), kind=kLoop, calls=%fused_computation.3 | loop fusion | flops 3145728 | bytes 4718592 | tf_op jit(solution)/shard_map/convert_element_type | solution.py:641
  182.5 42.3 %all-to-all-done.1 = bf16[64,288,128]{2,1,0:T(8,128)(2,1)} async-done(((bf16[64,288,128]{2,1,0:T(8,128)(2,1)}), bf16[64,288,128]{2,1,0:T(8,128)(2,1)}, u32[]{:S(2)}, u32[]{:S(2)}) %all-to-all-start.1) | async-done | bytes 4718624 | tf_op jit(solution)/shard_map/all_to_all | solution.py:53
  224.8 3.0 %convert_reduce_fusion = f32[288,128]{1,0:T(8,128)S(1)} fusion(bf16[64,288,128]{2,1,0:T(8,128)(2,1)} %all-to-all-done.1), kind=kLoop, calls=%fused_computation | loop fusion | flops 4681728 | bytes 4866048 | tf_op jit(solution)/shard_map/reduce_sum | solution.py:648
  227.9 10.2 %all_to_all.21 = f32[16,5,256]{2,1,0:T(8,128)S(1)} all-to-all(f32[16,5,256]{2,1,0:T(8,128)S(1)} %reshape.136), channel_id=1, replica_groups={{0,1,2,3,4,5,6,7,8,9,10,11,12,13,14,15},{16,17,18,19,20,21,22,23,24,25,..., dimensions={0} | all-to-all | bytes 163840 | tf_op jit(solution)/shard_map/all_to_all | solution.py:652
  238.1 7.8 %all-to-all-start.2 = ((bf16[64,8,1536]{2,1,0:T(8,128)(2,1)}), bf16[64,8,1536]{2,1,0:T(8,128)(2,1)S(1)}, u32[]{:S(2)}, u32[]{:S(2)}) async-start(bf16[64,8,1536]{2,1,0:T(8,128)(2,1)} %bitcast.13), calls=%async_computation.2 | async-start | bytes 3145728 | tf_op jit(solution)/shard_map/all_to_all | solution.py:53
  245.9 0.1 collective-permute-start.7
  246.0 0.6 copy.41
  246.7 0.5 collective-permute-done.7
  247.2 0.6 maximum_bitcast_fusion
  247.8 22.9 %all-to-all-done.2 = bf16[64,8,1536]{2,1,0:T(8,128)(2,1)S(1)} async-done(((bf16[64,8,1536]{2,1,0:T(8,128)(2,1)}), bf16[64,8,1536]{2,1,0:T(8,128)(2,1)S(1)}, u32[]{:S(2)}, u32[]{:S(2)}) %all-to-all-start.2) | async-done | bytes 1572896 | tf_op jit(solution)/shard_map/all_to_all | solution.py:53
  270.7 0.2 convert_reduce_fusion.1
  270.9 0.6 slice.129
  271.5 0.6 slice.130
  272.1 0.6 slice_bitcast_fusion.4
  272.7 0.6 slice_bitcast_fusion.2
  273.3 0.7 copy.43
  (24 shorter events, 0.1 us)
Async XLA Ops:
  7.2 95.6 %all-gather.2.cloned.1.call-start = ((), (), s32[]{:S(2)}) async-start(), calls=%async_computation.4 | async-start | bytes 11096064 | tf_op jit(solution)/shard_map/all_gather | solution.py:482
  10.6 43.9 %copy-start.1 = (s32[25]{0:T(128)S(1)}, s32[25]{0:T(128)}, u32[]{:S(2)}) copy-start(s32[25]{0:T(128)} %param.18) | copy-start | bytes 304
  10.6 43.9 %copy-start.2 = (s32[25]{0:T(128)S(1)}, s32[25]{0:T(128)}, u32[]{:S(2)}) copy-start(s32[25]{0:T(128)} %param.17) | copy-start | bytes 304
  54.5 4.5 %copy-start = (bf16[64,8,2176]{2,1,0:T(8,128)(2,1)}, bf16[64,8,2176]{2,1,0:T(8,128)(2,1)S(1)}, u32[]{:S(2)}) copy-start(bf16[64,8,2176]{2,1,0:T(8,128)(2,1)S(1)} %all_to_all.20) | copy-start | bytes 6684676
  54.5 4.5 %collective-permute-start = (bf16[512,2176]{1,0:T(8,128)(2,1)S(1)}, bf16[512,2176]{1,0:T(8,128)(2,1)}, u32[]{:S(2)}, u32[]{:S(2)}) collective-permute-start(bf16[512,2176]{1,0:T(8,128)(2,1)S(1)} %bitcast.56), channel_id=1, source_target_pairs={{0,1},{1,0},{2,3},{3,2},{4,5},{5,4},{6,7},{7,6},{8,9},{9,8},{10,11... | collective-permute-start | bytes 6684680 | tf_op jit(solution)/shard_map/ppermute | solution.py:49
  65.7 10.3 %collective-permute-start.1 = (bf16[256,512]{1,0:T(8,128)(2,1)}, bf16[256,512]{1,0:T(8,128)(2,1)S(1)}, u32[]{:S(2)}, u32[]{:S(2)}) collective-permute-start(bf16[256,512]{1,0:T(8,128)(2,1)} %get-tuple-element.42.kv_own), channel_id=1, source_target_pairs={{0,2},{1,3},{2,4},{3,5},{4,6},{5,7},{6,8},{7,9},{8,10},{9,11},{10,... | collective-permute-start | bytes 786440 | tf_op jit(solution)/shard_map/ppermute | solution.py:19
  68.1 7.9 %collective-permute-start.2 = (bf16[256,512]{1,0:T(8,128)(2,1)}, bf16[256,512]{1,0:T(8,128)(2,1)S(1)}, u32[]{:S(2)}, u32[]{:S(2)}) collective-permute-start(bf16[256,512]{1,0:T(8,128)(2,1)} %get-tuple-element.42.kv_own), channel_id=1, source_target_pairs={{0,1},{1,2},{2,3},{3,4},{4,5},{5,6},{6,7},{7,8},{8,9},{9,10},{10,1... | collective-permute-start | bytes 786440 | tf_op jit(solution)/shard_map/ppermute | solution.py:19
  76.0 0.7 copy-start.3
  76.0 0.8 copy-start.4
  133.5 9.4 %collective-permute-start.3 = (bf16[8,8,288,128]{3,2,1,0:T(8,128)(2,1)}, bf16[8,8,288,128]{3,2,1,0:T(8,128)(2,1)}, u32[]{:S(2)}, u32[]{:S(2)}) collective-permute-start(bf16[8,8,288,128]{3,2,1,0:T(8,128)(2,1)} %get-tuple-element.54), channel_id=1, source_target_pairs={{0,1},{1,0},{2,3},{3,2},{4,5},{5,4},{6,7},{7,6},{8,9},{9,8},{10,11... | collective-permute-start | bytes 14155784 | tf_op jit(solution)/shard_map/ppermute | solution.py:49
  134.0 8.9 %slice-start = ((s8[4718592]{0:T(1024)(128)(4,1)}), s8[4194304]{0:T(1024)(128)(4,1)S(1)}, s32[]{:S(2)}) async-start(s8[4718592]{0:T(1024)(128)(4,1)} %bitcast.54), calls=%async_computation.5 | async-start | bytes 8388608
  134.0 8.9 %slice-start.1 = ((s8[4718592]{0:T(1024)(128)(4,1)}), s8[524288]{0:T(1024)(128)(4,1)S(1)}, s32[]{:S(2)}) async-start(s8[4718592]{0:T(1024)(128)(4,1)} %bitcast.54), calls=%async_computation.6 | async-start | bytes 1048576
  140.3 8.4 %collective-permute-start.4 = (bf16[256,512]{1,0:T(8,128)(2,1)}, bf16[256,512]{1,0:T(8,128)(2,1)S(1)}, u32[]{:S(2)}, u32[]{:S(2)}) collective-permute-start(bf16[256,512]{1,0:T(8,128)(2,1)} %get-tuple-element.55), channel_id=1, source_target_pairs={{1,0},{2,1},{3,2},{4,3},{5,4},{6,5},{7,6},{8,7},{9,8},{10,9},{11,1... | collective-permute-start | bytes 786440 | tf_op jit(solution)/shard_map/ppermute | solution.py:19
  141.6 12.7 %collective-permute-start.5 = (bf16[256,512]{1,0:T(8,128)(2,1)}, bf16[256,512]{1,0:T(8,128)(2,1)S(1)}, u32[]{:S(2)}, u32[]{:S(2)}) collective-permute-start(bf16[256,512]{1,0:T(8,128)(2,1)} %get-tuple-element.56), channel_id=1, source_target_pairs={{2,0},{3,1},{4,2},{5,3},{6,4},{7,5},{8,6},{9,7},{10,8},{11,9},{12,... | collective-permute-start | bytes 786440 | tf_op jit(solution)/shard_map/ppermute | solution.py:19
  148.8 5.5 %copy-start.5 = (bf16[256,512]{1,0:T(8,128)(2,1)}, bf16[256,512]{1,0:T(8,128)(2,1)S(1)}, u32[]{:S(2)}) copy-start(bf16[256,512]{1,0:T(8,128)(2,1)S(1)} %collective-permute-done.4.near) | copy-start | bytes 786436
  154.3 0.7 copy-start.6
  155.0 69.9 %all-to-all-start.1 = ((bf16[64,288,128]{2,1,0:T(8,128)(2,1)}), bf16[64,288,128]{2,1,0:T(8,128)(2,1)}, u32[]{:S(2)}, u32[]{:S(2)}) async-start(bf16[64,288,128]{2,1,0:T(8,128)(2,1)} %bitcast.51), calls=%async_computation.1 | async-start | bytes 9437184 | tf_op jit(solution)/shard_map/all_to_all | solution.py:53
  176.0 3.6 %collective-permute-start.6 = (bf16[512,1536]{1,0:T(8,128)(2,1)}, bf16[512,1536]{1,0:T(8,128)(2,1)S(1)}, u32[]{:S(2)}, u32[]{:S(2)}) collective-permute-start(bf16[512,1536]{1,0:T(8,128)(2,1)} %get-tuple-element.65), channel_id=1, source_target_pairs={{0,1},{1,0},{2,3},{3,2},{4,5},{5,4},{6,7},{7,6},{8,9},{9,8},{10,11... | collective-permute-start | bytes 4718600 | tf_op jit(solution)/shard_map/ppermute | solution.py:49
  238.1 32.6 %all-to-all-start.2 = ((bf16[64,8,1536]{2,1,0:T(8,128)(2,1)}), bf16[64,8,1536]{2,1,0:T(8,128)(2,1)S(1)}, u32[]{:S(2)}, u32[]{:S(2)}) async-start(bf16[64,8,1536]{2,1,0:T(8,128)(2,1)} %bitcast.13), calls=%async_computation.2 | async-start | bytes 3145728 | tf_op jit(solution)/shard_map/all_to_all | solution.py:53
  245.9 1.3 collective-permute-start.7
Sparse Core Ops, SparseCore 0:
  11.6 91.1 all-gather.1

commit v2 on v1

--- a/solution.py
+++ b/solution.py
@@ -34,7 +34,6 @@
 BF16 = jnp.bfloat16
 F32 = jnp.float32
 SLOTS = 8
-GAIN_SLOT = 5
 MASKED = -1e30
 VMEM_BYTES = 56 * 1024 * 1024
 LANES = 128
@@ -114,22 +113,30 @@
     return jnp.where(mask, 1.0, 0.0).astype(BF16)
 
 
-def places(count):
+def pick_flat(rows, count, per):
     place = lax.broadcasted_iota(jnp.int32, (1, count), 1)
-    return lax.shift_right_logical(place, 3), place & (SLOTS - 1)
-
-
-def pick_rows(rows, count, per, core):
-    block, slot = places(count)
-    device = block if core is None else 2 * block + core
+    device, slot = lax.shift_right_logical(place, 3), place & (SLOTS - 1)
     source = jnp.where(slot < per, device * per + slot, -1)
     return ones_where(lax.broadcasted_iota(jnp.int32, (rows, count), 0) == source)
 
 
-def pick_slot(rows, count, per, core):
-    block, slot = places(count)
-    low = jnp.where(slot == GAIN_SLOT, (2 * block + core) * per, -2 * rows)
-    natural = lax.broadcasted_iota(jnp.int32, (rows, count), 0)
+def pick_core(rows, chips, per, core):
+    place = lax.broadcasted_iota(jnp.int32, (1, chips * per), 1)
+    row, chip = lax.div(place, chips), lax.rem(place, chips)
+    source = (2 * chip + core) * per + row
+    return ones_where(lax.broadcasted_iota(jnp.int32, (rows, chips * per), 0) == source)
+
+
+def pick_out(rows, count, core):
+    place = lax.broadcasted_iota(jnp.int32, (1, count), 1)
+    chip, row = lax.shift_right_logical(place, 3), place & (SLOTS - 1)
+    source = (2 * chip + core) * SLOTS + row
+    return ones_where(lax.broadcasted_iota(jnp.int32, (rows, count), 0) == source)
+
+
+def pick_chip(rows, chips, per, core):
+    low = (2 * lax.broadcasted_iota(jnp.int32, (1, chips), 1) + core) * per
+    natural = lax.broadcasted_iota(jnp.int32, (rows, chips), 0)
     return ones_where((natural >= low) & (natural < low + per))
 
 
@@ -146,34 +153,42 @@
 
 
 def before_attention(
-    core_ref, tok, own, peer, cos, sin, attn_rel, raw, query_low, own_kv, gains, head_gains
+    core_ref, tok, own, peer, cos, sin, raw, query_low, own_kv, gains, head_gains, weights, loose
 ):
     core = core_ref[0]
-    width, rows = tok.shape[1], own.shape[0]
+    width = tok.shape[1]
     kv_cols = own_kv.shape[1]
     head = kv_cols // 2
     q_cols = query_low.shape[1]
+    columns = q_cols + kv_cols
+    tiles = columns // LANES
     per, per_head = width // LANES, head // LANES
-
-    def gather(natural, count):
-        mine = dot(pick_slot(natural, rows, count, core), own[:, :LANES])
-        theirs = dot(pick_slot(natural, rows, count, 1 - core), peer[:, :LANES])
-        return jnp.transpose(mine + theirs)[:32]
-
-    wide = gather(width, per)
+    chips = weights.shape[1] // per
+    chunk = own.shape[0] // chips
+    wide = jnp.zeros((width, LANES), F32)
+    narrow = jnp.zeros((head, LANES), F32)
+    for which, (block, parity) in enumerate(((own, core), (peer, 1 - core))):
+        loose[...] = block[...].astype(F32)
+        for row in range(per):
+            for tile in range(tiles):
+                weights[
+                    which, row * chips : (row + 1) * chips, tile * LANES : (tile + 1) * LANES
+                ] = loose[pl.ds(row * tiles + tile, chips, stride=chunk), :].astype(BF16)
+        found = loose[pl.ds(per * tiles, chips, stride=chunk), :].astype(BF16)
+        wide += dot(pick_chip(width, chips, per, parity), found)
+        narrow += dot(pick_chip(head, chips, per_head, parity), found)
+    wide, narrow = jnp.transpose(wide)[:32], jnp.transpose(narrow)[:32]
     for which in range(4):
         mask = gain_mask(which * per, per, 32, width)
         gains[which : which + 1, :] = jnp.sum(jnp.where(mask, wide, 0.0), 0, keepdims=True)
-    narrow = gather(head, per_head)
     for which in range(2):
         mask = gain_mask(4 * per + which * per_head, per_head, 32, head)
         head_gains[which : which + 1, :] = jnp.sum(jnp.where(mask, narrow, 0.0), 0, keepdims=True)
     unit, _ = normed(tok[...].astype(F32))
     low = (unit * gains[0:1, :]).astype(BF16)
-    attn_rel[:, :rows] = dot(low, pick_rows(width, rows, per, core)).astype(BF16)
-    attn_rel[:, rows:] = dot(low, pick_rows(width, rows, per, 1 - core)).astype(BF16)
-    columns = q_cols + kv_cols
-    raw[...] = dot(attn_rel[:, :rows], own[:, :columns]) + dot(attn_rel[:, rows:], peer[:, :columns])
+    raw[...] = dot(dot(low, pick_core(width, chips, per, core)).astype(BF16), weights[0]) + dot(
+        dot(low, pick_core(width, chips, per, 1 - core)).astype(BF16), weights[1]
+    )
     for index in range(q_cols // head):
         span = slice(index * head, (index + 1) * head)
         unit, _ = normed(raw[:, span])
@@ -192,19 +207,13 @@
     return (same & (distance >= 0) & (distance < WINDOW)) | (distance == 0)
 
 
-def attention(
-    core_ref, query_low, kv_far, kv_near, kv_own, q_seq, k_seq, own, peer, tok, gains,
-    heads_low, log_total, proj, state,
-):
-    core = core_ref[0]
+def attention(query_low, kv_far, kv_near, kv_own, q_seq, k_seq, heads_low, log_total):
     head = kv_own.shape[1] // 2
-    width, rows = tok.shape[1], own.shape[0]
-    q_cols = query_low.shape[1]
     parts = (kv_far, kv_near, kv_own)
     keys = jnp.concatenate([part[:, :head] for part in parts], axis=0)
     values = jnp.concatenate([part[:, head:] for part in parts], axis=0)
     allowed = visible(q_seq, k_seq)
-    for index in range(q_cols // head):
+    for index in range(query_low.shape[1] // head):
         span = slice(index * head, (index + 1) * head)
         scores = dot_nt(query_low[:, span], keys) * query_scale
         scores = jnp.where(allowed, scores, MASKED)
@@ -214,60 +223,66 @@
         probs = (terms * (1.0 / total)).astype(BF16)
         heads_low[:, span] = dot(probs, values).astype(BF16)
         log_total[:, index : index + 1] = top + jnp.log(total)
-    offset = own.shape[1] - width
-    heads = heads_low[...]
-    first = dot(heads, pick_rows(q_cols, rows, SLOTS, core)).astype(BF16)
-    second = dot(heads, pick_rows(q_cols, rows, SLOTS, 1 - core)).astype(BF16)
-    proj[...] = dot(first, own[:, offset:]) + dot(second, peer[:, offset:])
-    unit, _ = normed(proj[...])
-    state[...] = tok[...].astype(F32) + unit * gains[1:2, :]
 
 
 def feed_forward(
-    core_ref, state, proj, out_grad, live, gains, heads_low, own, peer, gate_up, down_full,
+    core_ref, tok, out_grad, live, gains, heads_low, full,
     mixed, d_state, d_heads, gain_grads, keep, send,
-    weights, down, act, act_slope, hidden, total, back, low_flat, low, low_branch, turn, turn_down,
-    turn_out, weight_sem, down_sem,
+    weights, rest, down, act, act_slope, hidden, proj, state, total, back, low_flat, low, low_core,
+    low_branch, loose, loose_out, turn_down, weight_sem, rest_sem,
 ):
     core = core_ref[0]
     tiles, tile = weights.shape[0], weights.shape[2]
     half = tiles // 2
     width = state.shape[1]
-    rows = own.shape[0]
     q_cols = heads_low.shape[1]
     per = width // LANES
-    down_rows = down_full.shape[2]
-    blocks, strips = keep.shape[0], keep.shape[1]
-    block_rows = width // blocks
+    blocks, strips, down_rows = keep.shape[0], keep.shape[1], turn_down.shape[3]
+    chips = blocks * strips
     tile_chips = tile // (2 * down_rows)
+    tile_rows = tile // down_rows * SLOTS
+    columns_at = tiles * tile
 
     def weight_copy(index):
         return pltpu.make_async_copy(
-            gate_up.at[:, pl.ds(pl.multiple_of(index * tile, tile), tile)],
+            full.at[:, pl.ds(pl.multiple_of(index * tile, tile), tile)],
             weights.at[index],
             weight_sem.at[index],
         )
 
-    down_copy = pltpu.make_async_copy(down_full, down, down_sem)
+    rest_copy = pltpu.make_async_copy(
+        full.at[:, columns_at : columns_at + rest.shape[1]], rest, rest_sem
+    )
+    rest_copy.start()
     for index in range(half):
         weight_copy(index).start()
         weight_copy(half + index).start()
-        if index == 0:
-            down_copy.start()
-
-    spread_flat = pick_rows(width, weights.shape[1], per, None)
+
+    spread_flat = pick_flat(width, weights.shape[1], per)
+    rest_copy.wait()
+    w_out = rest[:, 2 * width :]
+    proj[...] = dot(heads_low[...], w_out)
+    unit, _ = normed(proj[...])
+    state[...] = tok[...].astype(F32) + unit * gains[1:2, :]
     unit, scale = normed(state[...])
     low[...] = (unit * gains[2:3, :]).astype(BF16)
     low_flat[...] = dot(low[...], spread_flat).astype(BF16)
+    low_core[0] = dot(low[...], pick_core(width, chips, per, core)).astype(BF16)
+    low_core[1] = dot(low[...], pick_core(width, chips, per, 1 - core)).astype(BF16)
     total[...] = jnp.zeros_like(total)
-    down_copy.wait()
 
     def down_tile(index):
-        chunk = down[pl.ds(index * tile_chips, tile_chips)]
-        return chunk.reshape(tile, width)
+        return down[pl.ds(pl.multiple_of(index * tile, tile), tile)]
 
     def forward(index, carry):
         columns = pl.ds(pl.multiple_of(index * tile, tile), tile)
+        stored = rest[pl.ds(pl.multiple_of(index * tile_rows, tile_rows), tile_rows), : 2 * width]
+        stored = stored.astype(F32).reshape(tile_rows // SLOTS, SLOTS, 2 * width)
+        down[pl.ds(pl.multiple_of(index * tile, tile), tile)] = (
+            jnp.concatenate([stored[:, :, :width], stored[:, :, width:]], axis=1)
+            .reshape(tile, width)
+            .astype(BF16)
+        )
         weight_copy(index).wait()
         weight_copy(half + index).wait()
         gate = dot(low_flat[...], weights[index])
@@ -296,16 +311,19 @@
     low_branch[...] = d_branch.astype(BF16)
     back[...] = jnp.zeros_like(back)
 
-    def place(strip, grads):
-        turn[0] = grads[:, : tile // 2].astype(BF16)
-        turn[1] = grads[:, tile // 2 :].astype(BF16)
-        for target, parity in ((keep, core), (send, 1 - core)):
-            for part in range(tile // 2 // LANES):
-                target[:, strip, part * block_rows : (part + 1) * block_rows, :] = turn[
-                    parity, :, part * LANES : (part + 1) * LANES
-                ].reshape(blocks, block_rows, LANES)
-
-    down_at = block_rows * (tile // 2 // LANES)
+    row_tiles = tiles * tile // LANES
+    chunk = per * row_tiles
+
+    def place(start, grad):
+        for which in range(2):
+            block = dot_tn(low_core[which], grad)
+            for row in range(per):
+                for part in range(tile // LANES):
+                    loose[which, pl.ds(row * row_tiles + start + part, chips, stride=chunk), :] = (
+                        block[row * chips : (row + 1) * chips, part * LANES : (part + 1) * LANES]
+                    )
+
+    down_at = chunk
     out_at = down_at + down_rows * (width // LANES)
 
     def backward(index, carry):
@@ -314,8 +332,8 @@
         d_gate = (d_hidden * act_slope[:, columns]).astype(BF16)
         d_up = (d_hidden * act[:, columns]).astype(BF16)
         back[...] += dot_nt(d_gate, weights[index]) + dot_nt(d_up, weights[half + index])
-        place(index, dot_tn(low[...], d_gate))
-        place(half + index, dot_tn(low[...], d_up))
+        place(index * (tile // LANES), d_gate)
+        place((half + index) * (tile // LANES), d_up)
         turn_down[...] = (
             dot_tn(hidden[:, columns], low_branch[...])
             .astype(BF16)
@@ -332,32 +350,37 @@
 
     lax.fori_loop(0, half, backward, 0)
 
+    def pack(block, carry):
+        rows = pl.ds(pl.multiple_of(block * strips * chunk, strips * chunk), strips * chunk)
+        for which, target in enumerate((keep, send)):
+            target[block, :, :chunk, :] = (
+                loose[which, rows, :].reshape(strips, chunk, LANES).astype(BF16)
+            )
+        return carry
+
+    lax.fori_loop(0, blocks, pack, 0)
+
     high = back[...].astype(BF16)
-    rest = (back[...] - high.astype(F32)).astype(BF16)
-    d_low = dot_nt(high, spread_flat) + dot_nt(rest, spread_flat)
+    rounding = (back[...] - high.astype(F32)).astype(BF16)
+    d_low = dot_nt(high, spread_flat) + dot_nt(rounding, spread_flat)
     d_norm, gain_grads[2:3, :] = normed_back(d_low, unit, scale, gains[2:3, :])
     d_state[...] = cotangent + d_norm
     proj_unit, proj_scale = normed(proj[...])
     d_proj, gain_grads[1:2, :] = normed_back(d_state[...], proj_unit, proj_scale, gains[1:2, :])
     proj_low = d_proj.astype(BF16)
-    offset = own.shape[1] - width
-    first = dot_nt(proj_low, own[:, offset:]).astype(BF16)
-    second = dot_nt(proj_low, peer[:, offset:]).astype(BF16)
-    d_heads[...] = (
-        dot_nt(first, pick_rows(q_cols, rows, SLOTS, core))
-        + dot_nt(second, pick_rows(q_cols, rows, SLOTS, 1 - core))
-    ).astype(BF16)
-    out_rows = 2 * SLOTS
-    for part in range(width // LANES):
-        turn_out[part] = (
-            dot_tn(heads_low[...], proj_low[:, part * LANES : (part + 1) * LANES])
-            .astype(BF16)
-            .reshape(blocks, strips, out_rows, LANES)
-        )
+    d_heads[...] = dot_nt(proj_low, w_out).astype(BF16)
+    out_tiles = width // LANES
+    loose_out[:, :, out_tiles * SLOTS :, :] = jnp.zeros(
+        (blocks, strips, loose_out.shape[2] - out_tiles * SLOTS, LANES), F32
+    )
     for target, parity in ((keep, core), (send, 1 - core)):
-        target[:, :, out_at : out_at + out_rows, :] = turn_out[2 * parity]
-        target[:, :, out_at + out_rows : out_at + 2 * out_rows, :] = turn_out[2 * parity + 1]
-        target[:, :, out_at + 2 * out_rows : out_at + 3 * out_rows, :] = turn_out[4]
+        heads = dot(heads_low[...], pick_out(q_cols, chips * SLOTS, parity)).astype(BF16)
+        block = dot_tn(heads, proj_low)
+        for part in range(out_tiles):
+            loose_out[:, :, part * SLOTS : (part + 1) * SLOTS, :] = block[
+                :, part * LANES : (part + 1) * LANES
+            ].reshape(blocks, strips, SLOTS, LANES)
+        target[:, :, out_at:, :] = loose_out[...].astype(BF16)
 
 
 def attention_back(
@@ -393,14 +416,17 @@
 
 
 def after_attention(
-    core_ref, raw, d_query, d_own, near, far, attn_rel, own, peer, tok, gains, head_gains, cos, sin,
-    d_state, gain_grads, tokens_grad, keep, send, low,
+    core_ref, raw, d_query, d_own, near, far, weights, tok, gains, head_gains, cos, sin,
+    d_state, gain_grads, tokens_grad, keep, send, low, loose,
 ):
     core = core_ref[0]
-    width, rows = tok.shape[1], own.shape[0]
+    width = tok.shape[1]
     q_cols, kv_cols = d_query.shape[1], d_own.shape[1]
     head = kv_cols // 2
+    tiles = (q_cols + kv_cols) // LANES
     per, per_head = width // LANES, head // LANES
+    chips = weights.shape[1] // per
+    chunk = keep.shape[0] // chips
     cosine, minus_sine = cos[...], -sin[...]
     query_gain_grad = jnp.zeros((1, head), F32)
     for index in range(q_cols // head):
@@ -417,14 +443,13 @@
     low[:, q_cols : q_cols + head] = d_raw.astype(BF16)
     low[:, q_cols + head :] = d_kv[:, head:].astype(BF16)
 
-    columns = q_cols + kv_cols
+    selectors = [pick_core(width, chips, per, parity) for parity in (core, 1 - core)]
     d_low = jnp.zeros(tok.shape, F32)
-    for weight, parity in ((own, core), (peer, 1 - core)):
-        part = dot_nt(low[...], weight[:, :columns])
+    for which, selector in enumerate(selectors):
+        part = dot_nt(low[...], weights[which])
         high = part.astype(BF16)
-        rest = (part - high.astype(F32)).astype(BF16)
-        selector = pick_rows(width, rows, per, parity)
-        d_low += dot_nt(high, selector) + dot_nt(rest, selector)
+        rounding = (part - high.astype(F32)).astype(BF16)
+        d_low += dot_nt(high, selector) + dot_nt(rounding, selector)
     unit, scale = normed(tok[...].astype(F32))
     d_norm, in_gain_grad = normed_back(d_low, unit, scale, gains[0:1, :])
     tokens_grad[...] = (d_state[...] + d_norm).astype(BF16)
@@ -438,13 +463,21 @@
         mask = gain_mask(4 * per + which * per_head, per_head, LANES, head)
         narrow = jnp.where(mask, vector, narrow)
     wide, narrow = wide.astype(BF16), narrow.astype(BF16)
-    for target, start, parity in ((keep, 0, core), (send, rows, 1 - core)):
-        extra = dot(wide, pick_slot(width, rows, per, parity)) + dot(
-            narrow, pick_slot(head, rows, per_head, parity)
+    attn_low = (unit * gains[0:1, :]).astype(BF16)
+    for row in range(per * tiles + 1, chunk):
+        loose[pl.ds(row, chips, stride=chunk), :] = jnp.zeros((chips, LANES), F32)
+    for target, selector, parity in ((keep, selectors[0], core), (send, selectors[1], 1 - core)):
+        extra = dot(wide, pick_chip(width, chips, per, parity)) + dot(
+            narrow, pick_chip(head, chips, per_head, parity)
         )
-        block = dot_tn(attn_rel[:, start : start + rows], low[:, :LANES])
-        target[:, :LANES] = (block + jnp.transpose(extra)).astype(BF16)
-        target[:, LANES:] = dot_tn(attn_rel[:, start : start + rows], low[:, LANES:]).astype(BF16)
+        loose[pl.ds(per * tiles, chips, stride=chunk), :] = jnp.transpose(extra)
+        block = dot_tn(dot(attn_low, selector).astype(BF16), low[...])
+        for row in range(per):
+            for tile in range(tiles):
+                loose[pl.ds(row * tiles + tile, chips, stride=chunk), :] = block[
+                    row * chips : (row + 1) * chips, tile * LANES : (tile + 1) * LANES
+                ]
+        target[...] = loose[...].astype(BF16)
 
 
 def on_device(
@@ -477,7 +510,6 @@
     down_rows = w_down.shape[0]
     head = kv_cols // 2
     hshard = norm_query.shape[0]
-    half_rows = chips * SLOTS
 
     mlp_full = lax.all_gather(
         jnp.concatenate(
@@ -485,6 +517,7 @@
                 jnp.pad(w_gate_up, ((0, SLOTS - shard), (0, 0))),
                 w_down[:SLOTS],
                 w_down[SLOTS:],
+                w_output,
             ],
             axis=1,
         ),
@@ -492,36 +525,23 @@
         axis=0,
         tiled=True,
     )
-    down_full = jnp.concatenate(
+
+    tiles = qkv_cols // LANES
+    chunk = 64
+    gain_row = jnp.zeros((1, LANES), BF16)
+    gain_count = 0
+    for part in (norm_attn_in, norm_attn_out, norm_mlp_in, norm_mlp_out, norm_query, norm_key):
+        wide = part.shape[0]
+        gain_row = gain_row + jnp.pad(part[None], ((0, 0), (gain_count, LANES - gain_count - wide)))
+        gain_count += wide
+    pack = jnp.concatenate(
         [
-            mlp_full[:, gu_cols : gu_cols + width].reshape(chips, 2, SLOTS, width),
-            mlp_full[:, gu_cols + width :].reshape(chips, 2, SLOTS, width),
+            jnp.concatenate([w_query, w_key_value], axis=1).reshape(shard * tiles, LANES),
+            jnp.pad(gain_row, ((0, chunk - shard * tiles - 1), (0, 0))),
         ],
-        axis=2,
-    )
-
-    pack = jnp.zeros((SLOTS, qkv_cols + width), BF16)
-    gain_count = 0
-    for row, column, part in (
-        (0, 0, w_query),
-        (0, q_cols, w_key_value),
-        (0, qkv_cols, w_output),
-        (GAIN_SLOT, None, norm_attn_in[None]),
-        (GAIN_SLOT, None, norm_attn_out[None]),
-        (GAIN_SLOT, None, norm_mlp_in[None]),
-        (GAIN_SLOT, None, norm_mlp_out[None]),
-        (GAIN_SLOT, None, norm_query[None]),
-        (GAIN_SLOT, None, norm_key[None]),
-    ):
-        high, wide = part.shape
-        if column is None:
-            column = gain_count
-            gain_count += wide
-        pack = pack + jnp.pad(
-            part, ((row, SLOTS - row - high), (column, qkv_cols + width - column - wide))
-        )
-    own_attn = spread(pack)
-    own = own_attn.reshape(half_rows, qkv_cols + width)
+        axis=0,
+    )
+    own = spread(pack).reshape(chips * chunk, LANES)
     peer = swap_cores(own)
 
     key_reach = (WINDOW + tok_rows - 2) // tok_rows
@@ -536,37 +556,35 @@
     angles = q_pos.astype(F32)[:, None] * inv_freq[None, :]
     cos_vals, sin_vals = jnp.cos(angles), jnp.sin(angles)
 
-    attn_rel, raw, query_low, own_kv, gains, head_gains = call(
+    raw, query_low, own_kv, gains, head_gains, attn_weights = call(
         before_attention,
         (
-            shape((tok_rows, 2 * half_rows), BF16),
             shape((tok_rows, qkv_cols), F32),
             shape((tok_rows, q_cols), BF16),
             shape((tok_rows, kv_cols), BF16),
             shape((8, width), F32),
             shape((8, head), F32),
+            shape((2, chips * shard, qkv_cols), BF16),
         ),
         (core_arg, tokens, own, peer, cos_vals, sin_vals),
+        scratch=(pltpu.VMEM((chips * chunk, LANES), F32),),
         specs=[SCALAR] + [WHOLE] * 5,
     )
     kv_near = shifted(own_kv, "fsdp", 1)
     kv_far = shifted(own_kv, "fsdp", 2)
-    heads_low, log_total, proj, state = call(
+    heads_low, log_total = call(
         attention,
-        (
-            shape((tok_rows, q_cols), BF16),
-            shape((tok_rows, LANES), F32),
-            shape((tok_rows, width), F32),
-            shape((tok_rows, width), F32),
-        ),
-        (core_arg, query_low, kv_far, kv_near, own_kv, q_seq, k_seq, own, peer, tokens, gains),
-        specs=[SCALAR] + [WHOLE] * 10,
+        (shape((tok_rows, q_cols), BF16), shape((tok_rows, LANES), F32)),
+        (query_low, kv_far, kv_near, own_kv, q_seq, k_seq),
+        specs=[WHOLE] * 6,
         flops=20e9,
     )
 
     tile = 512
     blocks, strips = 8, chips // 8
-    chunk_rows = (width // blocks) * 2 + down_rows * (width // LANES) + 6 * SLOTS
+    down_at = shard * gu_cols // LANES
+    out_at = down_at + down_rows * (width // LANES)
+    chunk_rows = out_at + 6 * SLOTS
     mixed, d_state, d_heads, gain_grads, keep, send = call(
         feed_forward,
         (
@@ -578,27 +596,30 @@
             shape((blocks, strips, chunk_rows, LANES), BF16),
         ),
         (
-            core_arg, state, proj, out_grad, live, gains, heads_low, own, peer,
-            mlp_full, down_full,
+            core_arg, tokens, out_grad, live, gains, heads_low, mlp_full,
         ),
         scratch=(
             pltpu.VMEM((gu_cols // tile, size * SLOTS, tile), BF16),
-            pltpu.VMEM((chips, 2, down_rows, width), BF16),
+            pltpu.VMEM((size * SLOTS, 3 * width), BF16),
+            pltpu.VMEM((ff, width), BF16),
             pltpu.VMEM((tok_rows, ff), F32),
             pltpu.VMEM((tok_rows, ff), F32),
             pltpu.VMEM((tok_rows, ff), BF16),
             pltpu.VMEM((tok_rows, width), F32),
+            pltpu.VMEM((tok_rows, width), F32),
+            pltpu.VMEM((tok_rows, width), F32),
             pltpu.VMEM((tok_rows, size * SLOTS), F32),
             pltpu.VMEM((tok_rows, size * SLOTS), BF16),
             pltpu.VMEM((tok_rows, width), BF16),
+            pltpu.VMEM((2, tok_rows, width // 2), BF16),
             pltpu.VMEM((tok_rows, width), BF16),
-            pltpu.VMEM((2, width, tile // 2), BF16),
+            pltpu.VMEM((2, chips * down_at, LANES), F32),
+            pltpu.VMEM((blocks, strips, 6 * SLOTS, LANES), F32),
             pltpu.VMEM((tile // (2 * down_rows) // strips, strips, 2, down_rows, width), BF16),
-            pltpu.VMEM((width // LANES, blocks, strips, 2 * SLOTS, LANES), BF16),
             pltpu.SemaphoreType.DMA((gu_cols // tile,)),
             pltpu.SemaphoreType.DMA,
         ),
-        specs=[SCALAR] + [WHOLE] * 8 + [AWAY] * 2,
+        specs=[SCALAR] + [WHOLE] * 5 + [AWAY],
         flops=12e9,
     )
     both_mlp = (keep.astype(F32) + swap_cores(send).astype(F32)).astype(BF16)
@@ -627,60 +648,45 @@
         after_attention,
         (
             shape((tok_rows, width), BF16),
-            shape((half_rows, qkv_cols), BF16),
-            shape((half_rows, qkv_cols), BF16),
+            shape((chips * chunk, LANES), BF16),
+            shape((chips * chunk, LANES), BF16),
         ),
         (
-            core_arg, raw, d_query, d_own, near, far, attn_rel, own, peer, tokens, gains,
+            core_arg, raw, d_query, d_own, near, far, attn_weights, tokens, gains,
             head_gains, cos_vals, sin_vals, d_state, gain_grads,
         ),
-        scratch=(pltpu.VMEM((tok_rows, qkv_cols), BF16),),
-        specs=[SCALAR] + [WHOLE] * 15,
+        scratch=(
+            pltpu.VMEM((tok_rows, qkv_cols), BF16),
+            pltpu.VMEM((chips * chunk, LANES), F32),
+        ),
+        specs=[SCALAR] + [WHOLE] * 13,
         flops=20e9,
     )
     both = (keep.astype(F32) + swap_cores(send).astype(F32)).astype(BF16)
     both, mlp_parts = lax.optimization_barrier((both, mlp_parts))
-    share_attn = jnp.sum(
-        exchange(both.reshape(chips, SLOTS, qkv_cols)).astype(F32), axis=0
-    )
-    share_gains = share_attn[GAIN_SLOT, :gain_count]
+    share_attn = jnp.sum(exchange(both.reshape(chips, chunk, LANES)).astype(F32), axis=0)
+    share_qkv = share_attn[: shard * tiles].reshape(shard, tiles * LANES)
+    share_gains = share_attn[shard * tiles, :gain_count]
 
     share_mlp = jnp.sum(mlp_parts.astype(F32), axis=0)
-    block_rows = width // blocks
-    group = size // blocks
-    strip = jnp.concatenate([share_mlp[:block_rows], share_mlp[block_rows : 2 * block_rows]], axis=1)
-    strip = lax.all_to_all(
-        strip.reshape(group, shard, gu_cols // group),
-        "fsdp",
-        split_axis=0,
-        concat_axis=0,
-        tiled=True,
-        axis_index_groups=[[b * group + i for i in range(group)] for b in range(blocks)],
-    )
-    share_gate_up = strip.transpose(1, 0, 2).reshape(shard, gu_cols)
-    down_at = 2 * block_rows
-    out_at = down_at + down_rows * (width // LANES)
+    share_gate_up = share_mlp[:down_at].reshape(shard, gu_cols)
     share_down = (
         share_mlp[down_at:out_at]
         .reshape(width // LANES, down_rows, LANES)
         .transpose(1, 0, 2)
         .reshape(down_rows, width)
     )
-    out_tiles = share_mlp[out_at:].reshape(3, 2, SLOTS, LANES)
-    mine = jnp.where(core == 0, out_tiles[:, 0], out_tiles[:, 1])
-    theirs = swap_cores(jnp.where(core == 0, out_tiles[:, 1], out_tiles[:, 0]))
-    first = jnp.where(core == 0, mine[:2], theirs[:2])
-    second = jnp.where(core == 0, theirs[:2], mine[:2])
     share_output = (
-        jnp.concatenate([first, second, mine[2:]], axis=0)
+        share_mlp[out_at : out_at + SLOTS * (width // LANES)]
+        .reshape(width // LANES, SLOTS, LANES)
         .transpose(1, 0, 2)
         .reshape(SLOTS, width)
     )
     return (
         mixed,
         tokens_grad,
-        share_attn[:shard, :q_cols],
-        share_attn[:shard, q_cols:],
+        share_qkv[:, :q_cols],
+        share_qkv[:, q_cols:],
         share_output,
         share_gate_up,
         share_down,

time: 282 us -> 257 us (0.911)
  blocking collectives: 54.1 us -> 0 us
  starting transfers between devices: 26.6 us -> 41.3 us
  waiting for transfers between devices: 100 us -> 109 us
  Pallas kernels: 56.6 us -> 62.8 us
    all_to_all x2 -> x0, blocking collectives: 54.1 us -> none  [the longest x1 43.9 us: exchange(): lax.all_to_all(blocks, 'fsdp', split_axis=0, concat_axis=0, tiled=True, a...]
    all_to_all x2 -> x3, starting transfers between devices: 19 us -> 33.1 us  [exchange(): lax.all_to_all(blocks, 'fsdp', split_axis=0, concat_axis=0, tiled=True, a...]
    all_to_all x2 -> x3, waiting for transfers between devices: 65.1 us -> 76.6 us  [exchange(): lax.all_to_all(blocks, 'fsdp', split_axis=0, concat_axis=0, tiled=True, a...]
    pallas_call x5, Pallas kernels: 56.6 us -> 62.8 us  [call(): pl.pallas_call(kernel, out_shape=outs, in_specs=specs, scratch_shapes=lis...]
    ppermute x4 -> x3, waiting for transfers between devices: 7.01 us -> 2.87 us  [swap_cores(): return lax.ppermute(block, 'fsdp', [(i, i ^ 1) for i in range(size)])]
  transfers between devices with their start and end apart: 11 -> 11, of which waited for: 8 -> 7; matrix products, arithmetic and copies ran while one was open for 5% -> 9% of each run, Pallas kernels for 11% -> 12%
where the time goes in v2:
time: 257 us
  waiting for transfers between devices  109 us (42%)
  Pallas kernels  62.8 us (24%)
  starting transfers between devices  41.3 us (16%)
  other arithmetic  18.3 us (7%)
  between operations  14.2 us (6%)
  local copies, waits for them, and re-layouts  11 us (4%)
    all_to_all x3, waiting for transfers between devices, exchange(): lax.all_to_all(blocks, 'fsdp', split_axis=0, concat_axis=0, tiled=True, a...  76.6 us
    pallas_call x5, Pallas kernels, call(): pl.pallas_call(kernel, out_shape=outs, in_specs=specs, scratch_shapes=lis...  62.8 us
    all_to_all x3, starting transfers between devices, exchange(): lax.all_to_all(blocks, 'fsdp', split_axis=0, concat_axis=0, tiled=True, a...  33.1 us
    all_gather x1, waiting for transfers between devices, on_device(): lax.all_gather(jnp.concatenate([jnp.pad(w_gate_up, ((0, SLOTS - shard), (...  19.4 us
    ppermute x4, waiting for transfers between devices, shifted(): return lax.ppermute(block, axis, route)  10.1 us
    ppermute x4, starting transfers between devices, shifted(): return lax.ppermute(block, axis, route)  7.55 us
    convert_element_type x1, other arithmetic, on_device(): both_mlp = (keep.astype(F32) + swap_cores(send).astype(F32)).astype(BF16)  5.8 us
  transfers between devices with their start and end apart: 11, of which 7 were waited for; matrix products, arithmetic and copies ran while one was open for 9% of the time, Pallas kernels for 12%

profile of v2, /device:TPU:0, one launch (start us, length us, event | category | flops | bytes accessed | tf_op | source)
XLA Modules:
  0.0 256.6 jit_solution(9672031570259967800)
XLA Ops:
  7.2 0.0 all-gather.2.cloned.1.call-start
  7.2 0.7 fusion.11
  7.9 1.5 fusion.4
  9.4 0.0 all-gather.2.cloned.1.call-update
  9.5 0.7 pad_maximum_fusion
  10.3 0.8 pad_add_fusion
  11.1 1.3 broadcast_in_dim.73
  12.4 11.5 %all-to-all-start = ((bf16[64,64,128]{2,1,0:T(8,128)(2,1)}), bf16[64,64,128]{2,1,0:T(8,128)(2,1)S(1)}, u32[]{:S(2)}, u32[]{:S(2)}) async-start(bf16[64,64,128]{2,1,0:T(8,128)(2,1)} %broadcast_in_dim.73), calls=%async_computation | async-start | bytes 2097152 | tf_op jit(solution)/shard_map/all_to_all | solution.py:52
  23.9 19.8 %all-to-all-done = bf16[64,64,128]{2,1,0:T(8,128)(2,1)S(1)} async-done(((bf16[64,64,128]{2,1,0:T(8,128)(2,1)}), bf16[64,64,128]{2,1,0:T(8,128)(2,1)S(1)}, u32[]{:S(2)}, u32[]{:S(2)}) %all-to-all-start) | async-done | bytes 1048608 | tf_op jit(solution)/shard_map/all_to_all | solution.py:52
  43.7 0.0 copy-start.1
  43.7 0.0 collective-permute-start
  43.7 0.9 select_reduce_fusion.1
  44.6 0.8 fusion.5
  45.4 0.8 select_reduce_fusion
  46.2 1.2 multiply_sine_fusion
  47.4 0.0 collective-permute-done.peer
  47.4 0.0 copy-start.4
  47.4 0.0 copy-done.1
  47.4 1.0 copy-done.4
  48.4 0.0 copy-start.2
  48.4 9.4 %shard_map.246 = (f32[256,1536]{1,0:T(8,128)}, bf16[256,1024]{1,0:T(8,128)(2,1)}, bf16[256,512]{1,0:T(8,128)(2,1)}, f32[8,640]{1,0:T(8,128)}, f32[8,256]{1,0:T(8,128)}, /*index=5*/bf16[2,320,1536]{2,1,0:T(8,128)(2,1)}) custom-call(s32[1]{0:T(128)} %bitcast.core_ref, bf16[256,640]{1,0:T(8,128)(2,1)} %tok.5, bf16[4096,128]{1,0:T(8,128)(2,1)} %bitcast.40, ...), custom_call_target="tpu_custom_call" | custom-call | flops 4000000000 | bytes 8000000 | tf_op jit(solution)/shard_map/pallas_call | solution.py:68
  57.7 2.3 collective-permute-start.2
  60.1 2.7 %collective-permute-start.1 = (bf16[256,512]{1,0:T(8,128)(2,1)}, bf16[256,512]{1,0:T(8,128)(2,1)S(1)}, u32[]{:S(2)}, u32[]{:S(2)}) collective-permute-start(bf16[256,512]{1,0:T(8,128)(2,1)} %get-tuple-element.41.kv_own), channel_id=1, source_target_pairs={{0,2},{1,3},{2,4},{3,5},{4,6},{5,7},{6,8},{7,9},{8,10},{9,11},{10,... | collective-permute-start | bytes 786440 | tf_op jit(solution)/shard_map/ppermute | solution.py:19
  62.7 0.0 copy-done.2
  62.8 0.0 copy-done.3
  62.8 0.1 fusion.10
  62.9 0.6 select_n.54.k_seq
  63.5 0.8 copy.32.q_seq
  64.3 0.8 copy.33.live
  65.1 0.0 collective-permute-done.2.kv_near
  65.1 4.5 %collective-permute-done.1.kv_far = bf16[256,512]{1,0:T(8,128)(2,1)S(1)} collective-permute-done((bf16[256,512]{1,0:T(8,128)(2,1)}, bf16[256,512]{1,0:T(8,128)(2,1)S(1)}, u32[]{:S(2)}, u32[]{:S(2)}) %collective-permute-start.1) | collective-permute-done | bytes 262176 | tf_op jit(solution)/shard_map/ppermute | solution.py:19
  69.6 0.0 copy-done.5
  69.6 0.7 copy-done.6
  70.3 4.0 %shard_map.247 = (bf16[256,1024]{1,0:T(8,128)(2,1)}, f32[256,128]{1,0:T(8,128)}) custom-call(bf16[256,1024]{1,0:T(8,128)(2,1)} %get-tuple-element.40.query_low, bf16[256,512]{1,0:T(8,128)(2,1)} %copy-done.6, bf16[256,512]{1,0:T(8,128)(2,1)} %copy-done.5, bf16[256,512]{1,0:T(8,128)(2,1)} %get-tuple-element.41.kv_own, s32[256,1]{1,0:T(8,128)} %copy.32.q_seq, ...), custom_call_target="tpu_custom_call" | custom-call | flops 20000000000 | bytes 8000000 | tf_op jit(solution)/shard_map/pallas_call | solution.py:68
  74.3 19.4 %all-gather.2.cloned.1.call-done.full = bf16[1024,6016]{1,0:T(8,128)(2,1)} async-done(((bf16[8,6016]{1,0:T(8,128)(2,1)}), bf16[1024,6016]{1,0:T(8,128)(2,1)}) %all-gather.2.cloned.1.call-update) | async-done | bytes 12320784 | tf_op jit(solution)/shard_map/all_gather | solution.py:514
  93.7 32.7 %shard_map.248 = (bf16[256,640]{1,0:T(8,128)(2,1)}, f32[256,640]{1,0:T(8,128)}, bf16[256,1024]{1,0:T(8,128)(2,1)}, f32[8,640]{1,0:T(8,128)}, bf16[8,8,288,128]{3...) custom-call(s32[1]{0:T(128)} %bitcast.core_ref, bf16[256,640]{1,0:T(8,128)(2,1)} %tok.5, bf16[256,640]{1,0:T(8,128)(2,1)} %out_grad.1, ...), custom_call_target="tpu_custom_call" | custom-call | flops 12000000000 | bytes 8000000 | tf_op jit(solution)/shard_map/pallas_call | solution.py:68
  126.4 0.6 collective-permute-start.3
  126.9 6.3 %shard_map.249 = (f32[256,1024]{1,0:T(8,128)}, f32[256,512]{1,0:T(8,128)}, bf16[256,512]{1,0:T(8,128)(2,1)}, bf16[256,512]{1,0:T(8,128)(2,1)}) custom-call(bf16[256,1024]{1,0:T(8,128)(2,1)} %get-tuple-element.40.query_low, bf16[256,512]{1,0:T(8,128)(2,1)} %copy-done.6, bf16[256,512]{1,0:T(8,128)(2,1)} %copy-done.5, ...), custom_call_target="tpu_custom_call" | custom-call | flops 20000000000 | bytes 8000000 | tf_op jit(solution)/shard_map/pallas_call | solution.py:68
  133.2 1.3 collective-permute-start.4
  134.5 1.3 collective-permute-start.5
  135.8 0.0 collective-permute-done.3
  135.8 0.0 copy-done
  135.8 5.8 %add_convert_fusion = bf16[8,8,288,128]{3,2,1,0:T(8,128)(2,1)} fusion(bf16[8,8,288,128]{3,2,1,0:T(8,128)(2,1)} %collective-permute-done.3, bf16[8,8,288,128]{3,2,1,0:T(8,128)(2,1)S(1)} %copy-done), kind=kLoop, calls=%fused_computation.1 | loop fusion | flops 9437184 | bytes 14155776 | tf_op jit(solution)/shard_map/convert_element_type | solution.py:625
  141.6 0.0 collective-permute-done.4.near
  141.6 5.5 %collective-permute-done.5.far = bf16[256,512]{1,0:T(8,128)(2,1)S(1)} collective-permute-done((bf16[256,512]{1,0:T(8,128)(2,1)}, bf16[256,512]{1,0:T(8,128)(2,1)S(1)}, u32[]{:S(2)}, u32[]{:S(2)}) %collective-permute-start.5) | collective-permute-done | bytes 262176 | tf_op jit(solution)/shard_map/ppermute | solution.py:19
  147.2 0.0 copy-done.7
  147.2 0.7 copy-done.8
  147.9 12.4 %all-to-all-start.1 = ((bf16[64,288,128]{2,1,0:T(8,128)(2,1)}), bf16[64,288,128]{2,1,0:T(8,128)(2,1)}, u32[]{:S(2)}, u32[]{:S(2)}) async-start(bf16[64,288,128]{2,1,0:T(8,128)(2,1)} %bitcast.38), calls=%async_computation.1 | async-start | bytes 9437184 | tf_op jit(solution)/shard_map/all_to_all | solution.py:52
  160.3 10.5 %shard_map.250 = (bf16[256,640]{1,0:T(8,128)(2,1)}, bf16[4096,128]{1,0:T(8,128)(2,1)}, bf16[4096,128]{1,0:T(8,128)(2,1)}) custom-call(s32[1]{0:T(128)} %bitcast.core_ref, f32[256,1536]{1,0:T(8,128)} %get-tuple-element.44.raw, f32[256,1024]{1,0:T(8,128)} %get-tuple-element.47.d_query, f32[256,512]{1,0:T(8,128)} %get-tuple-element.48.d_own, ...), custom_call_target="tpu_custom_call" | custom-call | flops 20000000000 | bytes 8000000 | tf_op jit(solution)/shard_map/pallas_call | solution.py:68
  170.8 0.0 collective-permute-start.6
  170.8 2.9 %collective-permute-done.6 = bf16[4096,128]{1,0:T(8,128)(2,1)S(1)} collective-permute-done((bf16[4096,128]{1,0:T(8,128)(2,1)}, bf16[4096,128]{1,0:T(8,128)(2,1)S(1)}, u32[]{:S(2)}, u32[]{:S(2)}) %collective-permute-start.6) | collective-permute-done | bytes 1048608 | tf_op jit(solution)/shard_map/ppermute | solution.py:48
  173.7 2.5 add_convert_fusion.1
  176.2 42.8 %all-to-all-done.1 = bf16[64,288,128]{2,1,0:T(8,128)(2,1)} async-done(((bf16[64,288,128]{2,1,0:T(8,128)(2,1)}), bf16[64,288,128]{2,1,0:T(8,128)(2,1)}, u32[]{:S(2)}, u32[]{:S(2)}) %all-to-all-start.1) | async-done | bytes 4718624 | tf_op jit(solution)/shard_map/all_to_all | solution.py:52
  218.9 9.2 %all-to-all-start.2 = ((bf16[64,64,128]{2,1,0:T(8,128)(2,1)}), bf16[64,64,128]{2,1,0:T(8,128)(2,1)S(1)}, u32[]{:S(2)}, u32[]{:S(2)}) async-start(bf16[64,64,128]{2,1,0:T(8,128)(2,1)} %bitcast.11), calls=%async_computation.2 | async-start | bytes 2097152 | tf_op jit(solution)/shard_map/all_to_all | solution.py:52
  228.1 3.0 %convert_reduce_fusion = f32[288,128]{1,0:T(8,128)S(1)} fusion(bf16[64,288,128]{2,1,0:T(8,128)(2,1)} %all-to-all-done.1), kind=kLoop, calls=%fused_computation | loop fusion | flops 4681728 | bytes 4866048 | tf_op jit(solution)/shard_map/reduce_sum | solution.py:671
  231.1 0.6 copy.38
  231.8 0.7 reshape.127
  232.4 0.6 slice_bitcast_fusion
  233.0 14.1 %all-to-all-done.2 = bf16[64,64,128]{2,1,0:T(8,128)(2,1)S(1)} async-done(((bf16[64,64,128]{2,1,0:T(8,128)(2,1)}), bf16[64,64,128]{2,1,0:T(8,128)(2,1)S(1)}, u32[]{:S(2)}, u32[]{:S(2)}) %all-to-all-start.2) | async-done | bytes 1048608 | tf_op jit(solution)/shard_map/all_to_all | solution.py:52
  247.1 0.2 convert_reduce_fusion.1
  247.3 0.6 slice_bitcast_fusion.1
  247.9 0.6 slice_bitcast_fusion.3
  248.5 0.6 slice.89
  249.1 0.6 slice.88
  (18 shorter events, 0.1 us)
Async XLA Ops:
  7.2 86.5 %all-gather.2.cloned.1.call-start = ((), (), s32[]{:S(2)}) async-start(), calls=%async_computation.3 | async-start | bytes 12417024 | tf_op jit(solution)/shard_map/all_gather | solution.py:514
  12.4 31.3 %all-to-all-start = ((bf16[64,64,128]{2,1,0:T(8,128)(2,1)}), bf16[64,64,128]{2,1,0:T(8,128)(2,1)S(1)}, u32[]{:S(2)}, u32[]{:S(2)}) async-start(bf16[64,64,128]{2,1,0:T(8,128)(2,1)} %broadcast_in_dim.73), calls=%async_computation | async-start | bytes 2097152 | tf_op jit(solution)/shard_map/all_to_all | solution.py:52
  43.7 3.7 %copy-start.1 = (bf16[64,64,128]{2,1,0:T(8,128)(2,1)}, bf16[64,64,128]{2,1,0:T(8,128)(2,1)S(1)}, u32[]{:S(2)}) copy-start(bf16[64,64,128]{2,1,0:T(8,128)(2,1)S(1)} %all-to-all-done) | copy-start | bytes 3145732
  43.7 3.7 %collective-permute-start = (bf16[4096,128]{1,0:T(8,128)(2,1)S(1)}, bf16[4096,128]{1,0:T(8,128)(2,1)S(1)}, u32[]{:S(2)}, u32[]{:S(2)}) collective-permute-start(bf16[4096,128]{1,0:T(8,128)(2,1)S(1)} %bitcast.39), channel_id=1, source_target_pairs={{0,1},{1,0},{2,3},{3,2},{4,5},{5,4},{6,7},{7,6},{8,9},{9,8},{10,11... | collective-permute-start | bytes 3145736 | tf_op jit(solution)/shard_map/ppermute | solution.py:48
  47.4 1.0 copy-start.4
  48.4 14.4 %copy-start.2 = (s32[25]{0:T(128)S(1)}, s32[25]{0:T(128)}, u32[]{:S(2)}) copy-start(s32[25]{0:T(128)} %param.18) | copy-start | bytes 304
  48.4 14.4 %copy-start.3 = (s32[25]{0:T(128)S(1)}, s32[25]{0:T(128)}, u32[]{:S(2)}) copy-start(s32[25]{0:T(128)} %param.17) | copy-start | bytes 304
  57.7 7.3 %collective-permute-start.2 = (bf16[256,512]{1,0:T(8,128)(2,1)}, bf16[256,512]{1,0:T(8,128)(2,1)S(1)}, u32[]{:S(2)}, u32[]{:S(2)}) collective-permute-start(bf16[256,512]{1,0:T(8,128)(2,1)} %get-tuple-element.41.kv_own), channel_id=1, source_target_pairs={{0,1},{1,2},{2,3},{3,4},{4,5},{5,6},{6,7},{7,8},{8,9},{9,10},{10,1... | collective-permute-start | bytes 786440 | tf_op jit(solution)/shard_map/ppermute | solution.py:19
  60.1 9.5 %collective-permute-start.1 = (bf16[256,512]{1,0:T(8,128)(2,1)}, bf16[256,512]{1,0:T(8,128)(2,1)S(1)}, u32[]{:S(2)}, u32[]{:S(2)}) collective-permute-start(bf16[256,512]{1,0:T(8,128)(2,1)} %get-tuple-element.41.kv_own), channel_id=1, source_target_pairs={{0,2},{1,3},{2,4},{3,5},{4,6},{5,7},{6,8},{7,9},{8,10},{9,11},{10,... | collective-permute-start | bytes 786440 | tf_op jit(solution)/shard_map/ppermute | solution.py:19
  65.1 4.6 %copy-start.5 = (bf16[256,512]{1,0:T(8,128)(2,1)}, bf16[256,512]{1,0:T(8,128)(2,1)S(1)}, u32[]{:S(2)}) copy-start(bf16[256,512]{1,0:T(8,128)(2,1)S(1)} %collective-permute-done.2.kv_near) | copy-start | bytes 786436
  69.6 0.7 copy-start.6
  126.4 9.4 %collective-permute-start.3 = (bf16[8,8,288,128]{3,2,1,0:T(8,128)(2,1)}, bf16[8,8,288,128]{3,2,1,0:T(8,128)(2,1)}, u32[]{:S(2)}, u32[]{:S(2)}) collective-permute-start(bf16[8,8,288,128]{3,2,1,0:T(8,128)(2,1)} %get-tuple-element.50), channel_id=1, source_target_pairs={{0,1},{1,0},{2,3},{3,2},{4,5},{5,4},{6,7},{7,6},{8,9},{9,8},{10,11... | collective-permute-start | bytes 14155784 | tf_op jit(solution)/shard_map/ppermute | solution.py:48
  126.9 8.9 %copy-start = (bf16[8,8,288,128]{3,2,1,0:T(8,128)(2,1)S(1)}, bf16[8,8,288,128]{3,2,1,0:T(8,128)(2,1)}, u32[]{:S(2)}) copy-start(bf16[8,8,288,128]{3,2,1,0:T(8,128)(2,1)} %get-tuple-element.49) | copy-start | bytes 14155780
  133.2 8.4 %collective-permute-start.4 = (bf16[256,512]{1,0:T(8,128)(2,1)}, bf16[256,512]{1,0:T(8,128)(2,1)S(1)}, u32[]{:S(2)}, u32[]{:S(2)}) collective-permute-start(bf16[256,512]{1,0:T(8,128)(2,1)} %get-tuple-element.51), channel_id=1, source_target_pairs={{1,0},{2,1},{3,2},{4,3},{5,4},{6,5},{7,6},{8,7},{9,8},{10,9},{11,1... | collective-permute-start | bytes 786440 | tf_op jit(solution)/shard_map/ppermute | solution.py:19
  134.5 12.6 %collective-permute-start.5 = (bf16[256,512]{1,0:T(8,128)(2,1)}, bf16[256,512]{1,0:T(8,128)(2,1)S(1)}, u32[]{:S(2)}, u32[]{:S(2)}) collective-permute-start(bf16[256,512]{1,0:T(8,128)(2,1)} %get-tuple-element.52), channel_id=1, source_target_pairs={{2,0},{3,1},{4,2},{5,3},{6,4},{7,5},{8,6},{9,7},{10,8},{11,9},{12,... | collective-permute-start | bytes 786440 | tf_op jit(solution)/shard_map/ppermute | solution.py:19
  141.6 5.5 %copy-start.7 = (bf16[256,512]{1,0:T(8,128)(2,1)}, bf16[256,512]{1,0:T(8,128)(2,1)S(1)}, u32[]{:S(2)}) copy-start(bf16[256,512]{1,0:T(8,128)(2,1)S(1)} %collective-permute-done.4.near) | copy-start | bytes 786436
  147.2 0.7 copy-start.8
  147.9 71.0 %all-to-all-start.1 = ((bf16[64,288,128]{2,1,0:T(8,128)(2,1)}), bf16[64,288,128]{2,1,0:T(8,128)(2,1)}, u32[]{:S(2)}, u32[]{:S(2)}) async-start(bf16[64,288,128]{2,1,0:T(8,128)(2,1)} %bitcast.38), calls=%async_computation.1 | async-start | bytes 9437184 | tf_op jit(solution)/shard_map/all_to_all | solution.py:52
  170.8 2.9 %collective-permute-start.6 = (bf16[4096,128]{1,0:T(8,128)(2,1)}, bf16[4096,128]{1,0:T(8,128)(2,1)S(1)}, u32[]{:S(2)}, u32[]{:S(2)}) collective-permute-start(bf16[4096,128]{1,0:T(8,128)(2,1)} %get-tuple-element.61), channel_id=1, source_target_pairs={{0,1},{1,0},{2,3},{3,2},{4,5},{5,4},{6,7},{7,6},{8,9},{9,8},{10,11... | collective-permute-start | bytes 3145736 | tf_op jit(solution)/shard_map/ppermute | solution.py:48
  218.9 28.2 %all-to-all-start.2 = ((bf16[64,64,128]{2,1,0:T(8,128)(2,1)}), bf16[64,64,128]{2,1,0:T(8,128)(2,1)S(1)}, u32[]{:S(2)}, u32[]{:S(2)}) async-start(bf16[64,64,128]{2,1,0:T(8,128)(2,1)} %bitcast.11), calls=%async_computation.2 | async-start | bytes 2097152 | tf_op jit(solution)/shard_map/all_to_all | solution.py:52
Sparse Core Ops, SparseCore 0:
  11.7 81.9 all-gather.1

commit v3 on v2

--- a/solution.py
+++ b/solution.py
@@ -35,6 +35,7 @@
 F32 = jnp.float32
 SLOTS = 8
 MASKED = -1e30
+ODD = 1
 VMEM_BYTES = 56 * 1024 * 1024
 LANES = 128
 
@@ -64,11 +65,12 @@
     return exchange(jnp.broadcast_to(block[None], (chips,) + block.shape))
 
 
-def call(kernel, outs, ins, scratch=(), specs=None, flops=4e9):
+def call(kernel, outs, ins, scratch=(), specs=None, flops=4e9, out_specs=None):
     return pl.pallas_call(
         kernel,
         out_shape=outs,
         in_specs=specs,
+        **({} if out_specs is None else {"out_specs": out_specs}),
         scratch_shapes=list(scratch),
         compiler_params=pltpu.CompilerParams(vmem_limit_bytes=VMEM_BYTES),
         cost_estimate=pl.CostEstimate(
@@ -125,13 +127,6 @@
     row, chip = lax.div(place, chips), lax.rem(place, chips)
     source = (2 * chip + core) * per + row
     return ones_where(lax.broadcasted_iota(jnp.int32, (rows, chips * per), 0) == source)
-
-
-def pick_out(rows, count, core):
-    place = lax.broadcasted_iota(jnp.int32, (1, count), 1)
-    chip, row = lax.shift_right_logical(place, 3), place & (SLOTS - 1)
-    source = (2 * chip + core) * SLOTS + row
-    return ones_where(lax.broadcasted_iota(jnp.int32, (rows, count), 0) == source)
 
 
 def pick_chip(rows, chips, per, core):
@@ -167,14 +162,18 @@
     chunk = own.shape[0] // chips
     wide = jnp.zeros((width, LANES), F32)
     narrow = jnp.zeros((head, LANES), F32)
+    stride = chunk + ODD
     for which, (block, parity) in enumerate(((own, core), (peer, 1 - core))):
-        loose[...] = block[...].astype(F32)
+        for chip in range(chips):
+            loose[chip * stride : chip * stride + chunk, :] = block[
+                chip * chunk : (chip + 1) * chunk, :
+            ].astype(F32)
         for row in range(per):
             for tile in range(tiles):
                 weights[
                     which, row * chips : (row + 1) * chips, tile * LANES : (tile + 1) * LANES
-                ] = loose[pl.ds(row * tiles + tile, chips, stride=chunk), :].astype(BF16)
-        found = loose[pl.ds(per * tiles, chips, stride=chunk), :].astype(BF16)
+                ] = loose[pl.ds(row * tiles + tile, chips, stride=stride), :].astype(BF16)
+        found = loose[pl.ds(per * tiles, chips, stride=stride), :].astype(BF16)
         wide += dot(pick_chip(width, chips, per, parity), found)
         narrow += dot(pick_chip(head, chips, per_head, parity), found)
     wide, narrow = jnp.transpose(wide)[:32], jnp.transpose(narrow)[:32]
@@ -227,9 +226,10 @@
 
 def feed_forward(
     core_ref, tok, out_grad, live, gains, heads_low, full,
-    mixed, d_state, d_heads, gain_grads, keep, send,
-    weights, rest, down, act, act_slope, hidden, proj, state, total, back, low_flat, low, low_core,
-    low_branch, loose, loose_out, turn_down, weight_sem, rest_sem,
+    mixed, d_state, d_heads, gain_grads, low_own, d_gate_up_out, own_down_out, own_out_out, send_out,
+    weights, rest, down, act, act_slope, hidden, proj, state, total, back, low_flat, low, turned_low,
+    low_branch, loose, loose_out, turn_down, d_gate_up, own_down, own_out, send,
+    weight_sem, rest_sem, out_sem,
 ):
     core = core_ref[0]
     tiles, tile = weights.shape[0], weights.shape[2]
@@ -237,7 +237,7 @@
     width = state.shape[1]
     q_cols = heads_low.shape[1]
     per = width // LANES
-    blocks, strips, down_rows = keep.shape[0], keep.shape[1], turn_down.shape[3]
+    blocks, strips, down_rows = send.shape[0], send.shape[1], turn_down.shape[3]
     chips = blocks * strips
     tile_chips = tile // (2 * down_rows)
     tile_rows = tile // down_rows * SLOTS
@@ -250,16 +250,23 @@
             weight_sem.at[index],
         )
 
-    rest_copy = pltpu.make_async_copy(
-        full.at[:, columns_at : columns_at + rest.shape[1]], rest, rest_sem
-    )
-    rest_copy.start()
+    def rest_copy(which, first, last):
+        return pltpu.make_async_copy(
+            full.at[:, columns_at + first : columns_at + last],
+            rest.at[:, first:last],
+            rest_sem.at[which],
+        )
+
+    out_copy = rest_copy(0, 2 * width, 3 * width)
+    down_copy = rest_copy(1, 0, 2 * width)
+    out_copy.start()
+    down_copy.start()
     for index in range(half):
         weight_copy(index).start()
         weight_copy(half + index).start()
 
     spread_flat = pick_flat(width, weights.shape[1], per)
-    rest_copy.wait()
+    out_copy.wait()
     w_out = rest[:, 2 * width :]
     proj[...] = dot(heads_low[...], w_out)
     unit, _ = normed(proj[...])
@@ -267,9 +274,12 @@
     unit, scale = normed(state[...])
     low[...] = (unit * gains[2:3, :]).astype(BF16)
     low_flat[...] = dot(low[...], spread_flat).astype(BF16)
-    low_core[0] = dot(low[...], pick_core(width, chips, per, core)).astype(BF16)
-    low_core[1] = dot(low[...], pick_core(width, chips, per, 1 - core)).astype(BF16)
+    low_own[...] = dot(low[...], pick_core(width, chips, per, core)).astype(BF16)
+    turned_low[...] = jnp.transpose(
+        dot(low[...], pick_core(width, chips, per, 1 - core))
+    ).astype(BF16)
     total[...] = jnp.zeros_like(total)
+    down_copy.wait()
 
     def down_tile(index):
         return down[pl.ds(pl.multiple_of(index * tile, tile), tile)]
@@ -315,13 +325,7 @@
     chunk = per * row_tiles
 
     def place(start, grad):
-        for which in range(2):
-            block = dot_tn(low_core[which], grad)
-            for row in range(per):
-                for part in range(tile // LANES):
-                    loose[which, pl.ds(row * row_tiles + start + part, chips, stride=chunk), :] = (
-                        block[row * chips : (row + 1) * chips, part * LANES : (part + 1) * LANES]
-                    )
+        place_rows(loose, dot(turned_low[...], grad), start, per, chips, row_tiles)
 
     down_at = chunk
     out_at = down_at + down_rows * (width // LANES)
@@ -331,6 +335,8 @@
         d_hidden = dot_nt(low_branch[...], down_tile(index))
         d_gate = (d_hidden * act_slope[:, columns]).astype(BF16)
         d_up = (d_hidden * act[:, columns]).astype(BF16)
+        d_gate_up[:, columns] = d_gate
+        d_gate_up[:, pl.ds(pl.multiple_of((half + index) * tile, tile), tile)] = d_up
         back[...] += dot_nt(d_gate, weights[index]) + dot_nt(d_up, weights[half + index])
         place(index * (tile // LANES), d_gate)
         place((half + index) * (tile // LANES), d_up)
@@ -340,25 +346,37 @@
             .reshape(tile_chips // strips, strips, 2, down_rows, width)
         )
         tall = pl.ds(index * (tile_chips // strips), tile_chips // strips)
-        for target, parity in ((keep, core), (send, 1 - core)):
-            for part in range(width // LANES):
-                top = down_at + part * down_rows
-                target[tall, :, top : top + down_rows, :] = turn_down[
-                    :, :, parity, :, part * LANES : (part + 1) * LANES
-                ]
+        for part in range(width // LANES):
+            top = part * down_rows
+            lanes = slice(part * LANES, (part + 1) * LANES)
+            own_down[tall, :, top : top + down_rows, :] = turn_down[:, :, core, :, lanes]
+            send[tall, :, down_at + top : down_at + top + down_rows, :] = turn_down[
+                :, :, 1 - core, :, lanes
+            ]
         return carry
 
     lax.fori_loop(0, half, backward, 0)
+    copies = [
+        pltpu.make_async_copy(d_gate_up, d_gate_up_out, out_sem.at[0]),
+        pltpu.make_async_copy(own_down, own_down_out, out_sem.at[1]),
+    ]
+    for copy in copies:
+        copy.start()
 
     def pack(block, carry):
-        rows = pl.ds(pl.multiple_of(block * strips * chunk, strips * chunk), strips * chunk)
-        for which, target in enumerate((keep, send)):
-            target[block, :, :chunk, :] = (
-                loose[which, rows, :].reshape(strips, chunk, LANES).astype(BF16)
+        for strip in range(strips):
+            send[block, strip, :chunk, :] = loose_chunk(loose, block * strips + strip, chunk).astype(
+                BF16
             )
         return carry
 
     lax.fori_loop(0, blocks, pack, 0)
+    copies.append(
+        pltpu.make_async_copy(
+            send.at[:, :, :out_at, :], send_out.at[:, :, :out_at, :], out_sem.at[2]
+        )
+    )
+    copies[-1].start()
 
     high = back[...].astype(BF16)
     rounding = (back[...] - high.astype(F32)).astype(BF16)
@@ -369,18 +387,90 @@
     d_proj, gain_grads[1:2, :] = normed_back(d_state[...], proj_unit, proj_scale, gains[1:2, :])
     proj_low = d_proj.astype(BF16)
     d_heads[...] = dot_nt(proj_low, w_out).astype(BF16)
+    loose_out[...] = dot_tn(heads_low[...], proj_low).reshape(blocks, strips, 2, SLOTS, width)
     out_tiles = width // LANES
-    loose_out[:, :, out_tiles * SLOTS :, :] = jnp.zeros(
-        (blocks, strips, loose_out.shape[2] - out_tiles * SLOTS, LANES), F32
-    )
-    for target, parity in ((keep, core), (send, 1 - core)):
-        heads = dot(heads_low[...], pick_out(q_cols, chips * SLOTS, parity)).astype(BF16)
-        block = dot_tn(heads, proj_low)
-        for part in range(out_tiles):
-            loose_out[:, :, part * SLOTS : (part + 1) * SLOTS, :] = block[
-                :, part * LANES : (part + 1) * LANES
-            ].reshape(blocks, strips, SLOTS, LANES)
-        target[:, :, out_at:, :] = loose_out[...].astype(BF16)
+    for target, parity, start in ((own_out, core, 0), (send, 1 - core, out_at)):
+        for part in range(out_tiles // 2 + 1):
+            lanes = [slice(i * LANES, (i + 1) * LANES) for i in (2 * part, 2 * part + 1)]
+            pair = [
+                loose_out[:, :, parity, :, lane]
+                if lane.stop <= width
+                else jnp.zeros((blocks, strips, SLOTS, LANES), F32)
+                for lane in lanes
+            ]
+            top = start + 2 * part * SLOTS
+            target[:, :, top : top + 2 * SLOTS, :] = jnp.concatenate(pair, axis=2).astype(BF16)
+    copies += [
+        pltpu.make_async_copy(own_out, own_out_out, out_sem.at[3]),
+        pltpu.make_async_copy(
+            send.at[:, :, out_at:, :], send_out.at[:, :, out_at:, :], out_sem.at[4]
+        ),
+    ]
+    for copy in copies[-2:]:
+        copy.start()
+    for copy in copies:
+        copy.wait()
+
+
+def place_rows(loose, block, start, per, chips, row_tiles):
+    stride = per * row_tiles + ODD
+    for row in range(per):
+        for part in range(block.shape[1] // LANES):
+            loose[pl.ds(row * row_tiles + start + part, chips, stride=stride), :] = block[
+                row * chips : (row + 1) * chips, part * LANES : (part + 1) * LANES
+            ]
+
+
+def loose_chunk(loose, chip, chunk):
+    return loose[pl.ds(chip * (chunk + ODD), chunk), :]
+
+
+def own_gradients(
+    d_gate_up, low_own, own_down, own_out, arrived, both_out,
+    both, other, turned_low, loose, arrived_sem, both_sem,
+):
+    copy = pltpu.make_async_copy(arrived, other, arrived_sem)
+    copy.start()
+    blocks, strips, down_size = own_down.shape[:3]
+    chips = blocks * strips
+    per = low_own.shape[1] // chips
+    tile = 512
+    steps = d_gate_up.shape[1] // tile
+    row_tiles = d_gate_up.shape[1] // LANES
+    chunk = per * row_tiles
+    turned_low[...] = jnp.transpose(low_own[...].astype(F32)).astype(BF16)
+
+    def place(index, carry):
+        grad = d_gate_up[:, pl.ds(pl.multiple_of(index * tile, tile), tile)]
+        block = dot(turned_low[...], grad)
+        place_rows(loose, block, index * (tile // LANES), per, chips, row_tiles)
+        return carry
+
+    lax.fori_loop(0, steps, place, 0)
+    copy.wait()
+
+    def leave(block):
+        return pltpu.make_async_copy(both.at[block], both_out.at[block], both_sem.at[block])
+
+    def pack(block, carry):
+        for strip in range(strips):
+            both[block, strip, :chunk, :] = (
+                loose_chunk(loose, block * strips + strip, chunk)
+                + other[block, strip, :chunk, :].astype(F32)
+            ).astype(BF16)
+        low, high = chunk, chunk + down_size
+        both[block, :, low:high, :] = (
+            own_down[block].astype(F32) + other[block, :, low:high, :].astype(F32)
+        ).astype(BF16)
+        both[block, :, high:, :] = (
+            own_out[block].astype(F32) + other[block, :, high:, :].astype(F32)
+        ).astype(BF16)
+        leave(block).start()
+        return carry
+
+    lax.fori_loop(0, blocks, pack, 0)
+    for block in range(blocks):
+        leave(block).wait()
 
 
 def attention_back(
@@ -464,20 +554,22 @@
         narrow = jnp.where(mask, vector, narrow)
     wide, narrow = wide.astype(BF16), narrow.astype(BF16)
     attn_low = (unit * gains[0:1, :]).astype(BF16)
+    stride = chunk + ODD
     for row in range(per * tiles + 1, chunk):
-        loose[pl.ds(row, chips, stride=chunk), :] = jnp.zeros((chips, LANES), F32)
+        loose[pl.ds(row, chips, stride=stride), :] = jnp.zeros((chips, LANES), F32)
     for target, selector, parity in ((keep, selectors[0], core), (send, selectors[1], 1 - core)):
         extra = dot(wide, pick_chip(width, chips, per, parity)) + dot(
             narrow, pick_chip(head, chips, per_head, parity)
         )
-        loose[pl.ds(per * tiles, chips, stride=chunk), :] = jnp.transpose(extra)
+        loose[pl.ds(per * tiles, chips, stride=stride), :] = jnp.transpose(extra)
         block = dot_tn(dot(attn_low, selector).astype(BF16), low[...])
         for row in range(per):
             for tile in range(tiles):
-                loose[pl.ds(row * tiles + tile, chips, stride=chunk), :] = block[
+                loose[pl.ds(row * tiles + tile, chips, stride=stride), :] = block[
                     row * chips : (row + 1) * chips, tile * LANES : (tile + 1) * LANES
                 ]
-        target[...] = loose[...].astype(BF16)
+        for chip in range(chips):
+            target[chip * chunk : (chip + 1) * chunk, :] = loose_chunk(loose, chip, chunk).astype(BF16)
 
 
 def on_device(
@@ -567,7 +659,7 @@
             shape((2, chips * shard, qkv_cols), BF16),
         ),
         (core_arg, tokens, own, peer, cos_vals, sin_vals),
-        scratch=(pltpu.VMEM((chips * chunk, LANES), F32),),
+        scratch=(pltpu.VMEM((chips * (chunk + ODD), LANES), F32),),
         specs=[SCALAR] + [WHOLE] * 5,
     )
     kv_near = shifted(own_kv, "fsdp", 1)
@@ -585,19 +677,21 @@
     down_at = shard * gu_cols // LANES
     out_at = down_at + down_rows * (width // LANES)
     chunk_rows = out_at + 6 * SLOTS
-    mixed, d_state, d_heads, gain_grads, keep, send = call(
+    chunk_shape = (blocks, strips, chunk_rows, LANES)
+    mixed, d_state, d_heads, gain_grads, low_own, d_gate_up, own_down, own_out, send = call(
         feed_forward,
         (
             shape((tok_rows, width), BF16),
             shape((tok_rows, width), F32),
             shape((tok_rows, q_cols), BF16),
             shape((8, width), F32),
-            shape((blocks, strips, chunk_rows, LANES), BF16),
-            shape((blocks, strips, chunk_rows, LANES), BF16),
-        ),
-        (
-            core_arg, tokens, out_grad, live, gains, heads_low, mlp_full,
-        ),
+            shape((tok_rows, width // 2), BF16),
+            shape((tok_rows, gu_cols), BF16),
+            shape((blocks, strips, out_at - down_at, LANES), BF16),
+            shape((blocks, strips, 6 * SLOTS, LANES), BF16),
+            shape(chunk_shape, BF16),
+        ),
+        (core_arg, tokens, out_grad, live, gains, heads_low, mlp_full),
         scratch=(
             pltpu.VMEM((gu_cols // tile, size * SLOTS, tile), BF16),
             pltpu.VMEM((size * SLOTS, 3 * width), BF16),
@@ -611,18 +705,24 @@
             pltpu.VMEM((tok_rows, size * SLOTS), F32),
             pltpu.VMEM((tok_rows, size * SLOTS), BF16),
             pltpu.VMEM((tok_rows, width), BF16),
-            pltpu.VMEM((2, tok_rows, width // 2), BF16),
+            pltpu.VMEM((width // 2, tok_rows), BF16),
             pltpu.VMEM((tok_rows, width), BF16),
-            pltpu.VMEM((2, chips * down_at, LANES), F32),
-            pltpu.VMEM((blocks, strips, 6 * SLOTS, LANES), F32),
+            pltpu.VMEM((chips * (down_at + ODD), LANES), F32),
+            pltpu.VMEM((blocks, strips, 2, SLOTS, width), F32),
             pltpu.VMEM((tile // (2 * down_rows) // strips, strips, 2, down_rows, width), BF16),
+            pltpu.VMEM((tok_rows, gu_cols), BF16),
+            pltpu.VMEM((blocks, strips, out_at - down_at, LANES), BF16),
+            pltpu.VMEM((blocks, strips, 6 * SLOTS, LANES), BF16),
+            pltpu.VMEM(chunk_shape, BF16),
             pltpu.SemaphoreType.DMA((gu_cols // tile,)),
-            pltpu.SemaphoreType.DMA,
+            pltpu.SemaphoreType.DMA((2,)),
+            pltpu.SemaphoreType.DMA((5,)),
         ),
         specs=[SCALAR] + [WHOLE] * 5 + [AWAY],
+        out_specs=(WHOLE,) * 5 + (AWAY,) * 4,
         flops=12e9,
     )
-    both_mlp = (keep.astype(F32) + swap_cores(send).astype(F32)).astype(BF16)
+    arrived = swap_cores(send)
 
     d_query, d_own, d_near, d_far = call(
         attention_back,
@@ -642,6 +742,23 @@
     )
     near = shifted(d_near, "fsdp", -1)
     far = shifted(d_far, "fsdp", -2)
+    arrived, far_started = lax.optimization_barrier((arrived, d_far))
+    both_mlp = call(
+        own_gradients,
+        shape(chunk_shape, BF16),
+        (d_gate_up, low_own, own_down, own_out, arrived),
+        scratch=(
+            pltpu.VMEM(chunk_shape, BF16),
+            pltpu.VMEM(chunk_shape, BF16),
+            pltpu.VMEM((width // 2, tok_rows), BF16),
+            pltpu.VMEM((chips * (down_at + ODD), LANES), F32),
+            pltpu.SemaphoreType.DMA,
+            pltpu.SemaphoreType.DMA((blocks,)),
+        ),
+        specs=[WHOLE] * 4 + [AWAY],
+        out_specs=AWAY,
+        flops=12e9,
+    )
     both_mlp, near, far = lax.optimization_barrier((both_mlp, near, far))
     mlp_parts = exchange(both_mlp.reshape(chips, chunk_rows, LANES))
     tokens_grad, keep, send = call(
@@ -657,7 +774,7 @@
         ),
         scratch=(
             pltpu.VMEM((tok_rows, qkv_cols), BF16),
-            pltpu.VMEM((chips * chunk, LANES), F32),
+            pltpu.VMEM((chips * (chunk + ODD), LANES), F32),
         ),
         specs=[SCALAR] + [WHOLE] * 13,
         flops=20e9,

time: 257 us -> 249 us (0.969)
  other arithmetic: 18.3 us -> 10.4 us
  Pallas kernels: 62.8 us -> 56 us
  waiting for transfers between devices: 109 us -> 113 us
    pallas_call x5 -> x6, Pallas kernels: 62.8 us -> 56 us  [call(): pl.pallas_call(kernel, out_shape=outs, in_specs=specs, **{} if out_specs...]
    convert_element_type x1 -> x0, other arithmetic: 5.8 us -> none  [on_device(): both_mlp = (keep.astype(F32) + swap_cores(send).astype(F32)).astype(BF16)]
    all_gather x1, waiting for transfers between devices: 19.4 us -> 23.2 us  [on_device(): lax.all_gather(jnp.concatenate([jnp.pad(w_gate_up, ((0, SLOTS - shard), (...]
  transfers between devices with their start and end apart: 11 -> 11, of which waited for: 7 -> 8; matrix products, arithmetic and copies ran while one was open for 9% -> 6% of each run, Pallas kernels for 12% -> 13%
where the time goes in v3:
time: 249 us; the launch traced here: 248 us
  waiting for transfers between devices  113 us (45%)
  Pallas kernels  56 us (22%)
  starting transfers between devices  40.8 us (16%)
  between operations  14.3 us (6%)
  local copies, waits for them, and re-layouts  13.1 us (5%)
  other arithmetic  10.4 us (4%)
    all_to_all x3, waiting for transfers between devices, exchange(): lax.all_to_all(blocks, 'fsdp', split_axis=0, concat_axis=0, tiled=True, a...  78.6 us
    pallas_call x6, Pallas kernels, call(): pl.pallas_call(kernel, out_shape=outs, in_specs=specs, **{} if out_specs...  56 us
    all_to_all x3, starting transfers between devices, exchange(): lax.all_to_all(blocks, 'fsdp', split_axis=0, concat_axis=0, tiled=True, a...  32.9 us
    all_gather x1, waiting for transfers between devices, on_device(): lax.all_gather(jnp.concatenate([jnp.pad(w_gate_up, ((0, SLOTS - shard), (...  23.2 us
    ppermute x4, waiting for transfers between devices, shifted(): return lax.ppermute(block, axis, route)  7.67 us
    ppermute x4, starting transfers between devices, shifted(): return lax.ppermute(block, axis, route)  7.28 us
  transfers between devices with their start and end apart: 11, of which 8 were waited for; matrix products, arithmetic and copies ran while one was open for 6% of the time, Pallas kernels for 13%

profile of v3, /device:TPU:0, one launch (start us, length us, event | category | flops | bytes accessed | tf_op | source)
XLA Modules:
  0.0 248.0 jit_solution(16398822962261493782)
XLA Ops:
  7.2 0.0 copy-start.1
  7.2 0.0 copy-start.2
  7.2 0.0 all-gather.2.cloned.1.call-start
  7.2 0.7 fusion.11
  8.0 1.5 fusion.4
  9.5 0.0 all-gather.2.cloned.1.call-update
  9.5 0.7 pad_maximum_fusion
  10.3 0.8 pad_add_fusion
  11.1 1.3 broadcast_in_dim.73
  12.4 11.5 %all-to-all-start = ((bf16[64,64,128]{2,1,0:T(8,128)(2,1)}), bf16[64,64,128]{2,1,0:T(8,128)(2,1)S(1)}, u32[]{:S(2)}, u32[]{:S(2)}) async-start(bf16[64,64,128]{2,1,0:T(8,128)(2,1)} %broadcast_in_dim.73), calls=%async_computation | async-start | bytes 2097152 | tf_op jit(solution)/shard_map/all_to_all | solution.py:53
  23.9 19.8 %all-to-all-done = bf16[64,64,128]{2,1,0:T(8,128)(2,1)S(1)} async-done(((bf16[64,64,128]{2,1,0:T(8,128)(2,1)}), bf16[64,64,128]{2,1,0:T(8,128)(2,1)S(1)}, u32[]{:S(2)}, u32[]{:S(2)}) %all-to-all-start) | async-done | bytes 1048608 | tf_op jit(solution)/shard_map/all_to_all | solution.py:53
  43.7 0.0 collective-permute-start
  43.7 0.0 copy-done.1
  43.7 0.0 copy-done.2
  43.7 0.1 select_reduce_fusion.1
  43.9 0.1 fusion.5
  44.0 0.1 select_reduce_fusion
  44.1 1.3 multiply_sine_fusion
  45.4 1.0 collective-permute-done.peer
  46.4 0.0 copy-done
  46.4 1.0 copy-done.4
  47.3 6.4 %shard_map.246 = (f32[256,1536]{1,0:T(8,128)}, bf16[256,1024]{1,0:T(8,128)(2,1)}, bf16[256,512]{1,0:T(8,128)(2,1)}, f32[8,640]{1,0:T(8,128)}, f32[8,256]{1,0:T(8,128)}, /*index=5*/bf16[2,320,1536]{2,1,0:T(8,128)(2,1)}) custom-call(s32[1]{0:T(128)} %bitcast.core_ref, bf16[256,640]{1,0:T(8,128)(2,1)} %tok.5, bf16[4096,128]{1,0:T(8,128)(2,1)} %bitcast.40, ...), custom_call_target="tpu_custom_call" | custom-call | flops 4000000000 | bytes 8000000 | tf_op jit(solution)/shard_map/pallas_call | solution.py:69
  53.7 2.1 collective-permute-start.2
  55.8 2.7 %collective-permute-start.1 = (bf16[256,512]{1,0:T(8,128)(2,1)}, bf16[256,512]{1,0:T(8,128)(2,1)S(1)}, u32[]{:S(2)}, u32[]{:S(2)}) collective-permute-start(bf16[256,512]{1,0:T(8,128)(2,1)} %get-tuple-element.45.kv_own), channel_id=1, source_target_pairs={{0,2},{1,3},{2,4},{3,5},{4,6},{5,7},{6,8},{7,9},{8,10},{9,11},{10,... | collective-permute-start | bytes 786440 | tf_op jit(solution)/shard_map/ppermute | solution.py:19
  58.4 0.1 fusion.10
  58.5 0.6 select_n.54.k_seq
  59.1 0.8 copy.32.q_seq
  59.9 0.8 copy.33.live
  60.7 0.0 collective-permute-done.2.kv_near
  60.7 5.5 %collective-permute-done.1.kv_far = bf16[256,512]{1,0:T(8,128)(2,1)S(1)} collective-permute-done((bf16[256,512]{1,0:T(8,128)(2,1)}, bf16[256,512]{1,0:T(8,128)(2,1)S(1)}, u32[]{:S(2)}, u32[]{:S(2)}) %collective-permute-start.1) | collective-permute-done | bytes 262176 | tf_op jit(solution)/shard_map/ppermute | solution.py:19
  66.2 0.0 copy-done.5
  66.2 0.7 copy-done.6
  66.9 4.1 %shard_map.247 = (bf16[256,1024]{1,0:T(8,128)(2,1)}, f32[256,128]{1,0:T(8,128)}) custom-call(bf16[256,1024]{1,0:T(8,128)(2,1)} %get-tuple-element.44.query_low, bf16[256,512]{1,0:T(8,128)(2,1)} %copy-done.6, bf16[256,512]{1,0:T(8,128)(2,1)} %copy-done.5, bf16[256,512]{1,0:T(8,128)(2,1)} %get-tuple-element.45.kv_own, s32[256,1]{1,0:T(8,128)} %copy.32.q_seq, ...), custom_call_target="tpu_custom_call" | custom-call | flops 20000000000 | bytes 8000000 | tf_op jit(solution)/shard_map/pallas_call | solution.py:69
  71.0 23.2 %all-gather.2.cloned.1.call-done.full = bf16[1024,6016]{1,0:T(8,128)(2,1)} async-done(((bf16[8,6016]{1,0:T(8,128)(2,1)}), bf16[1024,6016]{1,0:T(8,128)(2,1)}) %all-gather.2.cloned.1.call-update) | async-done | bytes 12320784 | tf_op jit(solution)/shard_map/all_gather | solution.py:606
  94.2 23.8 %shard_map.248 = (bf16[256,640]{1,0:T(8,128)(2,1)}, f32[256,640]{1,0:T(8,128)}, bf16[256,1024]{1,0:T(8,128)(2,1)}, f32[8,640]{1,0:T(8,128)}, bf16[256,320]{1,0:T...) custom-call(s32[1]{0:T(128)} %bitcast.core_ref, ...), custom_call_target="tpu_custom_call" | custom-call | flops 12000000000 | bytes 8000000 | tf_op jit(solution)/shard_map/pallas_call | solution.py:69
  118.0 0.6 collective-permute-start.3
  118.5 6.2 %shard_map.249 = (f32[256,1024]{1,0:T(8,128)}, f32[256,512]{1,0:T(8,128)}, bf16[256,512]{1,0:T(8,128)(2,1)}, bf16[256,512]{1,0:T(8,128)(2,1)}) custom-call(bf16[256,1024]{1,0:T(8,128)(2,1)} %get-tuple-element.44.query_low, bf16[256,512]{1,0:T(8,128)(2,1)} %copy-done.6, bf16[256,512]{1,0:T(8,128)(2,1)} %copy-done.5, ...), custom_call_target="tpu_custom_call" | custom-call | flops 20000000000 | bytes 8000000 | tf_op jit(solution)/shard_map/pallas_call | solution.py:69
  124.7 1.3 collective-permute-start.4
  126.0 1.3 collective-permute-start.5
  127.3 0.0 collective-permute-done.3.arrived
  127.3 0.0 copy-start.3
  127.3 2.2 copy-done.3
  129.5 6.9 %shard_map.250 = bf16[8,8,288,128]{3,2,1,0:T(8,128)(2,1)} custom-call(bf16[256,4096]{1,0:T(8,128)(2,1)} %get-tuple-element.53.d_gate_up, bf16[256,320]{1,0:T(8,128)(2,1)} %get-tuple-element.54.low_own, bf16[8,8,80,128]{3,2,1,0:T(8,128)(2,1)} %get-tuple-element.55.own_down, bf16[8,8,48,128]{3,2,1,0:T(8,128)(2,1)} %get-tuple-element.56.own_out, ...), custom_call_target="tpu_custom_call" | custom-call | flops 12000000000 | bytes 8000000 | tf_op jit(solution)/shard_map/pallas_call | solution.py:69
  136.5 0.0 collective-permute-done.4.near
  136.5 0.0 copy-start.7
  136.5 2.2 collective-permute-done.5.far
  138.7 0.7 copy-done.8
  139.4 12.4 %all-to-all-start.1 = ((bf16[64,288,128]{2,1,0:T(8,128)(2,1)}), bf16[64,288,128]{2,1,0:T(8,128)(2,1)}, u32[]{:S(2)}, u32[]{:S(2)}) async-start(bf16[64,288,128]{2,1,0:T(8,128)(2,1)} %bitcast.38), calls=%async_computation.1 | async-start | bytes 9437184 | tf_op jit(solution)/shard_map/all_to_all | solution.py:53
  151.8 8.7 %shard_map.251 = (bf16[256,640]{1,0:T(8,128)(2,1)}, bf16[4096,128]{1,0:T(8,128)(2,1)}, bf16[4096,128]{1,0:T(8,128)(2,1)}) custom-call(s32[1]{0:T(128)} %bitcast.core_ref, f32[256,1536]{1,0:T(8,128)} %get-tuple-element.48.raw, f32[256,1024]{1,0:T(8,128)} %get-tuple-element.51.d_query, f32[256,512]{1,0:T(8,128)} %get-tuple-element.52.d_own, ...), custom_call_target="tpu_custom_call" | custom-call | flops 20000000000 | bytes 8000000 | tf_op jit(solution)/shard_map/pallas_call | solution.py:69
  160.5 0.0 collective-permute-start.6
  160.5 2.9 %collective-permute-done.6 = bf16[4096,128]{1,0:T(8,128)(2,1)S(1)} collective-permute-done((bf16[4096,128]{1,0:T(8,128)(2,1)}, bf16[4096,128]{1,0:T(8,128)(2,1)S(1)}, u32[]{:S(2)}, u32[]{:S(2)}) %collective-permute-start.6) | collective-permute-done | bytes 1048608 | tf_op jit(solution)/shard_map/ppermute | solution.py:49
  163.3 2.5 add_convert_fusion
  165.8 44.7 %all-to-all-done.1 = bf16[64,288,128]{2,1,0:T(8,128)(2,1)} async-done(((bf16[64,288,128]{2,1,0:T(8,128)(2,1)}), bf16[64,288,128]{2,1,0:T(8,128)(2,1)}, u32[]{:S(2)}, u32[]{:S(2)}) %all-to-all-start.1) | async-done | bytes 4718624 | tf_op jit(solution)/shard_map/all_to_all | solution.py:53
  210.5 9.0 %all-to-all-start.2 = ((bf16[64,64,128]{2,1,0:T(8,128)(2,1)}), bf16[64,64,128]{2,1,0:T(8,128)(2,1)S(1)}, u32[]{:S(2)}, u32[]{:S(2)}) async-start(bf16[64,64,128]{2,1,0:T(8,128)(2,1)} %bitcast.11), calls=%async_computation.2 | async-start | bytes 2097152 | tf_op jit(solution)/shard_map/all_to_all | solution.py:53
  219.6 3.0 %convert_reduce_fusion = f32[288,128]{1,0:T(8,128)S(1)} fusion(bf16[64,288,128]{2,1,0:T(8,128)(2,1)} %all-to-all-done.1), kind=kLoop, calls=%fused_computation | loop fusion | flops 4681728 | bytes 4866048 | tf_op jit(solution)/shard_map/reduce_sum | solution.py:788
  222.6 0.6 copy.38
  223.2 0.7 reshape.127
  223.9 0.6 slice_bitcast_fusion
  224.5 14.1 %all-to-all-done.2 = bf16[64,64,128]{2,1,0:T(8,128)(2,1)S(1)} async-done(((bf16[64,64,128]{2,1,0:T(8,128)(2,1)}), bf16[64,64,128]{2,1,0:T(8,128)(2,1)S(1)}, u32[]{:S(2)}, u32[]{:S(2)}) %all-to-all-start.2) | async-done | bytes 1048608 | tf_op jit(solution)/shard_map/all_to_all | solution.py:53
  238.6 0.2 convert_reduce_fusion.1
  238.8 0.6 slice_bitcast_fusion.1
  239.3 0.6 slice_bitcast_fusion.3
  239.9 0.6 slice.89
  240.5 0.6 slice.88
  (18 shorter events, 0.1 us)
Async XLA Ops:
  7.2 36.5 %copy-start.1 = (s32[25]{0:T(128)S(1)}, s32[25]{0:T(128)}, u32[]{:S(2)}) copy-start(s32[25]{0:T(128)} %param.18) | copy-start | bytes 304
  7.2 36.5 %copy-start.2 = (s32[25]{0:T(128)S(1)}, s32[25]{0:T(128)}, u32[]{:S(2)}) copy-start(s32[25]{0:T(128)} %param.17) | copy-start | bytes 304
  7.2 87.0 %all-gather.2.cloned.1.call-start = ((), (), s32[]{:S(2)}) async-start(), calls=%async_computation.3 | async-start | bytes 12417024 | tf_op jit(solution)/shard_map/all_gather | solution.py:606
  12.4 31.3 %all-to-all-start = ((bf16[64,64,128]{2,1,0:T(8,128)(2,1)}), bf16[64,64,128]{2,1,0:T(8,128)(2,1)S(1)}, u32[]{:S(2)}, u32[]{:S(2)}) async-start(bf16[64,64,128]{2,1,0:T(8,128)(2,1)} %broadcast_in_dim.73), calls=%async_computation | async-start | bytes 2097152 | tf_op jit(solution)/shard_map/all_to_all | solution.py:53
  43.7 2.7 %copy-start = (bf16[64,64,128]{2,1,0:T(8,128)(2,1)}, bf16[64,64,128]{2,1,0:T(8,128)(2,1)S(1)}, u32[]{:S(2)}) copy-start(bf16[64,64,128]{2,1,0:T(8,128)(2,1)S(1)} %all-to-all-done) | copy-start | bytes 3145732
  43.7 2.7 %collective-permute-start = (bf16[4096,128]{1,0:T(8,128)(2,1)S(1)}, bf16[4096,128]{1,0:T(8,128)(2,1)S(1)}, u32[]{:S(2)}, u32[]{:S(2)}) collective-permute-start(bf16[4096,128]{1,0:T(8,128)(2,1)S(1)} %bitcast.39), channel_id=1, source_target_pairs={{0,1},{1,0},{2,3},{3,2},{4,5},{5,4},{6,7},{7,6},{8,9},{9,8},{10,11... | collective-permute-start | bytes 3145736 | tf_op jit(solution)/shard_map/ppermute | solution.py:49
  46.4 1.0 copy-start.4
  53.7 7.0 %collective-permute-start.2 = (bf16[256,512]{1,0:T(8,128)(2,1)}, bf16[256,512]{1,0:T(8,128)(2,1)S(1)}, u32[]{:S(2)}, u32[]{:S(2)}) collective-permute-start(bf16[256,512]{1,0:T(8,128)(2,1)} %get-tuple-element.45.kv_own), channel_id=1, source_target_pairs={{0,1},{1,2},{2,3},{3,4},{4,5},{5,6},{6,7},{7,8},{8,9},{9,10},{10,1... | collective-permute-start | bytes 786440 | tf_op jit(solution)/shard_map/ppermute | solution.py:19
  55.8 10.4 %collective-permute-start.1 = (bf16[256,512]{1,0:T(8,128)(2,1)}, bf16[256,512]{1,0:T(8,128)(2,1)S(1)}, u32[]{:S(2)}, u32[]{:S(2)}) collective-permute-start(bf16[256,512]{1,0:T(8,128)(2,1)} %get-tuple-element.45.kv_own), channel_id=1, source_target_pairs={{0,2},{1,3},{2,4},{3,5},{4,6},{5,7},{6,8},{7,9},{8,10},{9,11},{10,... | collective-permute-start | bytes 786440 | tf_op jit(solution)/shard_map/ppermute | solution.py:19
  60.7 5.5 %copy-start.5 = (bf16[256,512]{1,0:T(8,128)(2,1)}, bf16[256,512]{1,0:T(8,128)(2,1)S(1)}, u32[]{:S(2)}) copy-start(bf16[256,512]{1,0:T(8,128)(2,1)S(1)} %collective-permute-done.2.kv_near) | copy-start | bytes 786436
  66.2 0.7 copy-start.6
  118.0 9.4 %collective-permute-start.3 = (bf16[8,8,288,128]{3,2,1,0:T(8,128)(2,1)}, bf16[8,8,288,128]{3,2,1,0:T(8,128)(2,1)S(1)}, u32[]{:S(2)}, u32[]{:S(2)}) collective-permute-start(bf16[8,8,288,128]{3,2,1,0:T(8,128)(2,1)} %get-tuple-element.57), channel_id=1, source_target_pairs={{0,1},{1,0},{2,3},{3,2},{4,5},{5,4},{6,7},{7,6},{8,9},{9,8},{10,11... | collective-permute-start | bytes 14155784 | tf_op jit(solution)/shard_map/ppermute | solution.py:49
  124.7 11.7 %collective-permute-start.4 = (bf16[256,512]{1,0:T(8,128)(2,1)}, bf16[256,512]{1,0:T(8,128)(2,1)S(1)}, u32[]{:S(2)}, u32[]{:S(2)}) collective-permute-start(bf16[256,512]{1,0:T(8,128)(2,1)} %get-tuple-element.60), channel_id=1, source_target_pairs={{1,0},{2,1},{3,2},{4,3},{5,4},{6,5},{7,6},{8,7},{9,8},{10,9},{11,1... | collective-permute-start | bytes 786440 | tf_op jit(solution)/shard_map/ppermute | solution.py:19
  126.0 12.7 %collective-permute-start.5 = (bf16[256,512]{1,0:T(8,128)(2,1)}, bf16[256,512]{1,0:T(8,128)(2,1)S(1)}, u32[]{:S(2)}, u32[]{:S(2)}) collective-permute-start(bf16[256,512]{1,0:T(8,128)(2,1)} %get-tuple-element.58), channel_id=1, source_target_pairs={{2,0},{3,1},{4,2},{5,3},{6,4},{7,5},{8,6},{9,7},{10,8},{11,9},{12,... | collective-permute-start | bytes 786440 | tf_op jit(solution)/shard_map/ppermute | solution.py:19
  127.3 2.2 copy-start.3
  136.5 2.2 copy-start.7
  138.7 0.7 copy-start.8
  139.4 71.1 %all-to-all-start.1 = ((bf16[64,288,128]{2,1,0:T(8,128)(2,1)}), bf16[64,288,128]{2,1,0:T(8,128)(2,1)}, u32[]{:S(2)}, u32[]{:S(2)}) async-start(bf16[64,288,128]{2,1,0:T(8,128)(2,1)} %bitcast.38), calls=%async_computation.1 | async-start | bytes 9437184 | tf_op jit(solution)/shard_map/all_to_all | solution.py:53
  160.5 2.9 %collective-permute-start.6 = (bf16[4096,128]{1,0:T(8,128)(2,1)}, bf16[4096,128]{1,0:T(8,128)(2,1)S(1)}, u32[]{:S(2)}, u32[]{:S(2)}) collective-permute-start(bf16[4096,128]{1,0:T(8,128)(2,1)} %get-tuple-element.69), channel_id=1, source_target_pairs={{0,1},{1,0},{2,3},{3,2},{4,5},{5,4},{6,7},{7,6},{8,9},{9,8},{10,11... | collective-permute-start | bytes 3145736 | tf_op jit(solution)/shard_map/ppermute | solution.py:49
  210.5 28.1 %all-to-all-start.2 = ((bf16[64,64,128]{2,1,0:T(8,128)(2,1)}), bf16[64,64,128]{2,1,0:T(8,128)(2,1)S(1)}, u32[]{:S(2)}, u32[]{:S(2)}) async-start(bf16[64,64,128]{2,1,0:T(8,128)(2,1)} %bitcast.11), calls=%async_computation.2 | async-start | bytes 2097152 | tf_op jit(solution)/shard_map/all_to_all | solution.py:53
Sparse Core Ops, SparseCore 0:
  11.7 82.4 all-gather.1

commit v4 on v3

--- a/solution.py
+++ b/solution.py
@@ -65,14 +65,14 @@
     return exchange(jnp.broadcast_to(block[None], (chips,) + block.shape))
 
 
-def call(kernel, outs, ins, scratch=(), specs=None, flops=4e9, out_specs=None):
+def call(kernel, outs, ins, scratch=(), specs=None, flops=4e9, out_specs=None, vmem=VMEM_BYTES):
     return pl.pallas_call(
         kernel,
         out_shape=outs,
         in_specs=specs,
         **({} if out_specs is None else {"out_specs": out_specs}),
         scratch_shapes=list(scratch),
-        compiler_params=pltpu.CompilerParams(vmem_limit_bytes=VMEM_BYTES),
+        compiler_params=pltpu.CompilerParams(vmem_limit_bytes=vmem),
         cost_estimate=pl.CostEstimate(
             flops=int(flops), bytes_accessed=8_000_000, transcendentals=0
         ),
@@ -206,7 +206,16 @@
     return (same & (distance >= 0) & (distance < WINDOW)) | (distance == 0)
 
 
-def attention(query_low, kv_far, kv_near, kv_own, q_seq, k_seq, heads_low, log_total):
+def attention(
+    core_ref, query_low, kv_far, kv_near, kv_own, q_seq, k_seq,
+    heads_low, log_total, spread_flat, spread_core,
+):
+    core = core_ref[0]
+    width, per_core = spread_core.shape[1:]
+    per = width // LANES
+    spread_flat[...] = pick_flat(width, spread_flat.shape[1], per)
+    for which, parity in enumerate((core, 1 - core)):
+        spread_core[which] = pick_core(width, per_core // per, per, parity)
     head = kv_own.shape[1] // 2
     parts = (kv_far, kv_near, kv_own)
     keys = jnp.concatenate([part[:, :head] for part in parts], axis=0)
@@ -225,11 +234,12 @@
 
 
 def feed_forward(
-    core_ref, tok, out_grad, live, gains, heads_low, full,
-    mixed, d_state, d_heads, gain_grads, low_own, d_gate_up_out, own_down_out, own_out_out, send_out,
+    core_ref, tok, out_grad, live, gains, heads_low, spread_flat_in, spread_core_in, full,
+    gain_grads, mixed_out, d_state_out, d_heads_out, low_own_out, d_gate_up_out, own_down_out,
+    own_out_out, send_out,
     weights, rest, down, act, act_slope, hidden, proj, state, total, back, low_flat, low, turned_low,
-    low_branch, loose, loose_out, turn_down, d_gate_up, own_down, own_out, send,
-    weight_sem, rest_sem, out_sem,
+    low_branch, loose, loose_out, turn_down, spread_flat, spread_core, mixed, d_state, d_heads,
+    low_own, d_gate_up, own_down, own_out, send, weight_sem, rest_sem, out_sem,
 ):
     core = core_ref[0]
     tiles, tile = weights.shape[0], weights.shape[2]
@@ -259,13 +269,21 @@
 
     out_copy = rest_copy(0, 2 * width, 3 * width)
     down_copy = rest_copy(1, 0, 2 * width)
+    flat_copy = pltpu.make_async_copy(spread_flat_in, spread_flat, rest_sem.at[2])
+    core_copy = pltpu.make_async_copy(spread_core_in, spread_core, rest_sem.at[3])
     out_copy.start()
+    flat_copy.start()
     down_copy.start()
     for index in range(half):
         weight_copy(index).start()
         weight_copy(half + index).start()
-
-    spread_flat = pick_flat(width, weights.shape[1], per)
+    core_copy.start()
+    leaving = []
+
+    def leave(source, target):
+        leaving.append(pltpu.make_async_copy(source, target, out_sem.at[len(leaving)]))
+        leaving[-1].start()
+
     out_copy.wait()
     w_out = rest[:, 2 * width :]
     proj[...] = dot(heads_low[...], w_out)
@@ -273,11 +291,8 @@
     state[...] = tok[...].astype(F32) + unit * gains[1:2, :]
     unit, scale = normed(state[...])
     low[...] = (unit * gains[2:3, :]).astype(BF16)
-    low_flat[...] = dot(low[...], spread_flat).astype(BF16)
-    low_own[...] = dot(low[...], pick_core(width, chips, per, core)).astype(BF16)
-    turned_low[...] = jnp.transpose(
-        dot(low[...], pick_core(width, chips, per, 1 - core))
-    ).astype(BF16)
+    flat_copy.wait()
+    low_flat[...] = dot(low[...], spread_flat[...]).astype(BF16)
     total[...] = jnp.zeros_like(total)
     down_copy.wait()
 
@@ -311,9 +326,14 @@
         return carry
 
     lax.fori_loop(0, half, forward, 0)
+    core_copy.wait()
+    low_own[...] = dot(low[...], spread_core[0]).astype(BF16)
+    turned_low[...] = jnp.transpose(dot(low[...], spread_core[1])).astype(BF16)
+    leave(low_own, low_own_out)
 
     branch_unit, branch_scale = normed(total[...])
     mixed[...] = ((state[...] + branch_unit * gains[3:4, :]) * live[...]).astype(BF16)
+    leave(mixed, mixed_out)
     cotangent = out_grad[...].astype(F32) * live[...]
     d_branch, gain_grads[3:4, :] = normed_back(
         cotangent, branch_unit, branch_scale, gains[3:4, :]
@@ -356,12 +376,8 @@
         return carry
 
     lax.fori_loop(0, half, backward, 0)
-    copies = [
-        pltpu.make_async_copy(d_gate_up, d_gate_up_out, out_sem.at[0]),
-        pltpu.make_async_copy(own_down, own_down_out, out_sem.at[1]),
-    ]
-    for copy in copies:
-        copy.start()
+    leave(d_gate_up, d_gate_up_out)
+    leave(own_down, own_down_out)
 
     def pack(block, carry):
         for strip in range(strips):
@@ -371,22 +387,15 @@
         return carry
 
     lax.fori_loop(0, blocks, pack, 0)
-    copies.append(
-        pltpu.make_async_copy(
-            send.at[:, :, :out_at, :], send_out.at[:, :, :out_at, :], out_sem.at[2]
-        )
-    )
-    copies[-1].start()
-
-    high = back[...].astype(BF16)
-    rounding = (back[...] - high.astype(F32)).astype(BF16)
-    d_low = dot_nt(high, spread_flat) + dot_nt(rounding, spread_flat)
+    leave(send.at[:, :, :out_at, :], send_out.at[:, :, :out_at, :])
+
+    d_low = dot_nt(back[...].astype(BF16), spread_flat[...])
     d_norm, gain_grads[2:3, :] = normed_back(d_low, unit, scale, gains[2:3, :])
     d_state[...] = cotangent + d_norm
+    leave(d_state, d_state_out)
     proj_unit, proj_scale = normed(proj[...])
     d_proj, gain_grads[1:2, :] = normed_back(d_state[...], proj_unit, proj_scale, gains[1:2, :])
     proj_low = d_proj.astype(BF16)
-    d_heads[...] = dot_nt(proj_low, w_out).astype(BF16)
     loose_out[...] = dot_tn(heads_low[...], proj_low).reshape(blocks, strips, 2, SLOTS, width)
     out_tiles = width // LANES
     for target, parity, start in ((own_out, core, 0), (send, 1 - core, out_at)):
@@ -400,15 +409,11 @@
             ]
             top = start + 2 * part * SLOTS
             target[:, :, top : top + 2 * SLOTS, :] = jnp.concatenate(pair, axis=2).astype(BF16)
-    copies += [
-        pltpu.make_async_copy(own_out, own_out_out, out_sem.at[3]),
-        pltpu.make_async_copy(
-            send.at[:, :, out_at:, :], send_out.at[:, :, out_at:, :], out_sem.at[4]
-        ),
-    ]
-    for copy in copies[-2:]:
-        copy.start()
-    for copy in copies:
+    leave(own_out, own_out_out)
+    leave(send.at[:, :, out_at:, :], send_out.at[:, :, out_at:, :])
+    d_heads[...] = dot_nt(proj_low, w_out).astype(BF16)
+    leave(d_heads, d_heads_out)
+    for copy in leaving:
         copy.wait()
 
 
@@ -664,11 +669,16 @@
     )
     kv_near = shifted(own_kv, "fsdp", 1)
     kv_far = shifted(own_kv, "fsdp", 2)
-    heads_low, log_total = call(
+    heads_low, log_total, spread_flat, spread_core = call(
         attention,
-        (shape((tok_rows, q_cols), BF16), shape((tok_rows, LANES), F32)),
-        (query_low, kv_far, kv_near, own_kv, q_seq, k_seq),
-        specs=[WHOLE] * 6,
+        (
+            shape((tok_rows, q_cols), BF16),
+            shape((tok_rows, LANES), F32),
+            shape((width, size * SLOTS), BF16),
+            shape((2, width, width // 2), BF16),
+        ),
+        (core_arg, query_low, kv_far, kv_near, own_kv, q_seq, k_seq),
+        specs=[SCALAR] + [WHOLE] * 6,
         flops=20e9,
     )
 
@@ -678,20 +688,22 @@
     out_at = down_at + down_rows * (width // LANES)
     chunk_rows = out_at + 6 * SLOTS
     chunk_shape = (blocks, strips, chunk_rows, LANES)
-    mixed, d_state, d_heads, gain_grads, low_own, d_gate_up, own_down, own_out, send = call(
+    gain_grads, mixed, d_state, d_heads, low_own, d_gate_up, own_down, own_out, send = call(
         feed_forward,
         (
+            shape((8, width), F32),
             shape((tok_rows, width), BF16),
             shape((tok_rows, width), F32),
             shape((tok_rows, q_cols), BF16),
-            shape((8, width), F32),
             shape((tok_rows, width // 2), BF16),
             shape((tok_rows, gu_cols), BF16),
             shape((blocks, strips, out_at - down_at, LANES), BF16),
             shape((blocks, strips, 6 * SLOTS, LANES), BF16),
             shape(chunk_shape, BF16),
         ),
-        (core_arg, tokens, out_grad, live, gains, heads_low, mlp_full),
+        (
+            core_arg, tokens, out_grad, live, gains, heads_low, spread_flat, spread_core, mlp_full,
+        ),
         scratch=(
             pltpu.VMEM((gu_cols // tile, size * SLOTS, tile), BF16),
             pltpu.VMEM((size * SLOTS, 3 * width), BF16),
@@ -710,16 +722,22 @@
             pltpu.VMEM((chips * (down_at + ODD), LANES), F32),
             pltpu.VMEM((blocks, strips, 2, SLOTS, width), F32),
             pltpu.VMEM((tile // (2 * down_rows) // strips, strips, 2, down_rows, width), BF16),
+            pltpu.VMEM((width, size * SLOTS), BF16),
+            pltpu.VMEM((2, width, width // 2), BF16),
+            pltpu.VMEM((tok_rows, width), BF16),
+            pltpu.VMEM((tok_rows, width), F32),
+            pltpu.VMEM((tok_rows, q_cols), BF16),
+            pltpu.VMEM((tok_rows, width // 2), BF16),
             pltpu.VMEM((tok_rows, gu_cols), BF16),
             pltpu.VMEM((blocks, strips, out_at - down_at, LANES), BF16),
             pltpu.VMEM((blocks, strips, 6 * SLOTS, LANES), BF16),
             pltpu.VMEM(chunk_shape, BF16),
             pltpu.SemaphoreType.DMA((gu_cols // tile,)),
-            pltpu.SemaphoreType.DMA((2,)),
-            pltpu.SemaphoreType.DMA((5,)),
-        ),
-        specs=[SCALAR] + [WHOLE] * 5 + [AWAY],
-        out_specs=(WHOLE,) * 5 + (AWAY,) * 4,
+            pltpu.SemaphoreType.DMA((4,)),
+            pltpu.SemaphoreType.DMA((9,)),
+        ),
+        specs=[SCALAR] + [WHOLE] * 5 + [AWAY] * 3,
+        out_specs=(WHOLE,) + (AWAY,) * 8,
         flops=12e9,
     )
     arrived = swap_cores(send)
@@ -758,6 +776,7 @@
         specs=[WHOLE] * 4 + [AWAY],
         out_specs=AWAY,
         flops=12e9,
+        vmem=62 * 1024 * 1024,
     )
     both_mlp, near, far = lax.optimization_barrier((both_mlp, near, far))
     mlp_parts = exchange(both_mlp.reshape(chips, chunk_rows, LANES))

time: 249 us -> 247 us (level)
  no operation moved by 1% of the time
where the time goes in v4:
time: 247 us; the launch traced here: 246 us
  waiting for transfers between devices  115 us (47%)
  Pallas kernels  55 us (22%)
  starting transfers between devices  40.9 us (17%)
  between operations  14.3 us (6%)
  local copies, waits for them, and re-layouts  10.9 us (4%)
  other arithmetic  10.4 us (4%)
    all_to_all x3, waiting for transfers between devices, exchange(): lax.all_to_all(blocks, 'fsdp', split_axis=0, concat_axis=0, tiled=True, a...  78.7 us
    pallas_call x6, Pallas kernels, call(): pl.pallas_call(kernel, out_shape=outs, in_specs=specs, **{} if out_specs...  55 us
    all_to_all x3, starting transfers between devices, exchange(): lax.all_to_all(blocks, 'fsdp', split_axis=0, concat_axis=0, tiled=True, a...  33 us
    all_gather x1, waiting for transfers between devices, on_device(): lax.all_gather(jnp.concatenate([jnp.pad(w_gate_up, ((0, SLOTS - shard), (...  22.3 us
    ppermute x4, waiting for transfers between devices, shifted(): return lax.ppermute(block, axis, route)  9.82 us
    ppermute x4, starting transfers between devices, shifted(): return lax.ppermute(block, axis, route)  7.29 us
  transfers between devices with their start and end apart: 11, of which 8 were waited for; matrix products, arithmetic and copies ran while one was open for 6% of the time, Pallas kernels for 13%

profile of v4, /device:TPU:0, one launch (start us, length us, event | category | flops | bytes accessed | tf_op | source)
XLA Modules:
  0.0 246.2 jit_solution(9414206384668848855)
XLA Ops:
  7.2 0.0 copy-start.1
  7.2 0.0 copy-start.2
  7.2 0.0 all-gather.2.cloned.1.call-start
  7.2 0.7 fusion.11
  8.0 1.5 fusion.4
  9.5 0.0 all-gather.2.cloned.1.call-update
  9.5 0.7 pad_maximum_fusion
  10.3 0.8 pad_add_fusion
  11.1 1.3 broadcast_in_dim.73
  12.4 11.5 %all-to-all-start = ((bf16[64,64,128]{2,1,0:T(8,128)(2,1)}), bf16[64,64,128]{2,1,0:T(8,128)(2,1)S(1)}, u32[]{:S(2)}, u32[]{:S(2)}) async-start(bf16[64,64,128]{2,1,0:T(8,128)(2,1)} %broadcast_in_dim.73), calls=%async_computation | async-start | bytes 2097152 | tf_op jit(solution)/shard_map/all_to_all | solution.py:53
  23.9 19.8 %all-to-all-done = bf16[64,64,128]{2,1,0:T(8,128)(2,1)S(1)} async-done(((bf16[64,64,128]{2,1,0:T(8,128)(2,1)}), bf16[64,64,128]{2,1,0:T(8,128)(2,1)S(1)}, u32[]{:S(2)}, u32[]{:S(2)}) %all-to-all-start) | async-done | bytes 1048608 | tf_op jit(solution)/shard_map/all_to_all | solution.py:53
  43.7 0.0 copy-start
  43.7 0.0 collective-permute-start
  43.7 0.0 copy-done.1
  43.7 0.0 copy-done.2
  43.7 0.1 select_reduce_fusion.1
  43.9 0.1 fusion.5
  44.0 0.1 select_reduce_fusion
  44.1 1.2 multiply_sine_fusion
  45.3 1.0 collective-permute-done.peer
  46.4 0.0 copy-done
  46.4 1.0 copy-done.3
  47.3 6.4 %shard_map.246 = (f32[256,1536]{1,0:T(8,128)}, bf16[256,1024]{1,0:T(8,128)(2,1)}, bf16[256,512]{1,0:T(8,128)(2,1)}, f32[8,640]{1,0:T(8,128)}, f32[8,256]{1,0:T(8,128)}, /*index=5*/bf16[2,320,1536]{2,1,0:T(8,128)(2,1)}) custom-call(s32[1]{0:T(128)} %bitcast.core_ref, bf16[256,640]{1,0:T(8,128)(2,1)} %tok.5, bf16[4096,128]{1,0:T(8,128)(2,1)} %bitcast.40, ...), custom_call_target="tpu_custom_call" | custom-call | flops 4000000000 | bytes 8000000 | tf_op jit(solution)/shard_map/pallas_call | solution.py:69
  53.7 2.0 collective-permute-start.2
  55.8 2.7 %collective-permute-start.1 = (bf16[256,512]{1,0:T(8,128)(2,1)}, bf16[256,512]{1,0:T(8,128)(2,1)S(1)}, u32[]{:S(2)}, u32[]{:S(2)}) collective-permute-start(bf16[256,512]{1,0:T(8,128)(2,1)} %get-tuple-element.47.kv_own), channel_id=1, source_target_pairs={{0,2},{1,3},{2,4},{3,5},{4,6},{5,7},{6,8},{7,9},{8,10},{9,11},{10,... | collective-permute-start | bytes 786440 | tf_op jit(solution)/shard_map/ppermute | solution.py:19
  58.4 0.1 fusion.10
  58.5 0.6 select_n.54.k_seq
  59.1 0.8 copy.32.q_seq
  59.9 0.8 copy.33.live
  60.7 0.0 collective-permute-done.2.kv_near
  60.7 5.5 %collective-permute-done.1.kv_far = bf16[256,512]{1,0:T(8,128)(2,1)S(1)} collective-permute-done((bf16[256,512]{1,0:T(8,128)(2,1)}, bf16[256,512]{1,0:T(8,128)(2,1)S(1)}, u32[]{:S(2)}, u32[]{:S(2)}) %collective-permute-start.1) | collective-permute-done | bytes 262176 | tf_op jit(solution)/shard_map/ppermute | solution.py:19
  66.2 0.0 copy-done.4
  66.2 0.7 copy-done.5
  66.9 5.0 %shard_map.247 = (bf16[256,1024]{1,0:T(8,128)(2,1)}, f32[256,128]{1,0:T(8,128)}, bf16[640,1024]{1,0:T(8,128)(2,1)}, bf16[2,640,320]{2,1,0:T(8,128)(2,1)}) custom-call(s32[1]{0:T(128)} %bitcast.core_ref, bf16[256,1024]{1,0:T(8,128)(2,1)} %get-tuple-element.46.query_low, bf16[256,512]{1,0:T(8,128)(2,1)} %copy-done.5, bf16[256,512]{1,0:T(8,128)(2,1)} %copy-done.4, ...), custom_call_target="tpu_custom_call" | custom-call | flops 20000000000 | bytes 8000000 | tf_op jit(solution)/shard_map/pallas_call | solution.py:69
  71.9 22.3 %all-gather.2.cloned.1.call-done.full = bf16[1024,6016]{1,0:T(8,128)(2,1)} async-done(((bf16[8,6016]{1,0:T(8,128)(2,1)}), bf16[1024,6016]{1,0:T(8,128)(2,1)}) %all-gather.2.cloned.1.call-update) | async-done | bytes 12320784 | tf_op jit(solution)/shard_map/all_gather | solution.py:611
  94.2 22.0 %shard_map.248 = (f32[8,640]{1,0:T(8,128)}, bf16[256,640]{1,0:T(8,128)(2,1)}, f32[256,640]{1,0:T(8,128)}, bf16[256,1024]{1,0:T(8,128)(2,1)}, bf16[256,320]{1,0:T...) custom-call(s32[1]{0:T(128)} %bitcast.core_ref, ...), custom_call_target="tpu_custom_call" | custom-call | flops 12000000000 | bytes 8000000 | tf_op jit(solution)/shard_map/pallas_call | solution.py:69
  116.2 0.6 collective-permute-start.3
  116.8 6.1 %shard_map.249 = (f32[256,1024]{1,0:T(8,128)}, f32[256,512]{1,0:T(8,128)}, bf16[256,512]{1,0:T(8,128)(2,1)}, bf16[256,512]{1,0:T(8,128)(2,1)}) custom-call(bf16[256,1024]{1,0:T(8,128)(2,1)} %get-tuple-element.46.query_low, bf16[256,512]{1,0:T(8,128)(2,1)} %copy-done.5, bf16[256,512]{1,0:T(8,128)(2,1)} %copy-done.4, ...), custom_call_target="tpu_custom_call" | custom-call | flops 20000000000 | bytes 8000000 | tf_op jit(solution)/shard_map/pallas_call | solution.py:69
  122.9 1.3 collective-permute-start.4
  124.2 1.3 collective-permute-start.5
  125.5 0.0 collective-permute-done.3.arrived
  125.5 6.9 %shard_map.250 = bf16[8,8,288,128]{3,2,1,0:T(8,128)(2,1)} custom-call(bf16[256,4096]{1,0:T(8,128)(2,1)} %get-tuple-element.57.d_gate_up, bf16[256,320]{1,0:T(8,128)(2,1)} %get-tuple-element.58.low_own, bf16[8,8,80,128]{3,2,1,0:T(8,128)(2,1)} %get-tuple-element.59.own_down, bf16[8,8,48,128]{3,2,1,0:T(8,128)(2,1)} %get-tuple-element.60.own_out, ...), custom_call_target="tpu_custom_call" | custom-call | flops 12000000000 | bytes 8000000 | tf_op jit(solution)/shard_map/pallas_call | solution.py:69
  132.4 0.0 collective-permute-done.4.near
  132.4 0.0 copy-start.6
  132.5 4.4 %collective-permute-done.5.far = bf16[256,512]{1,0:T(8,128)(2,1)S(1)} collective-permute-done((bf16[256,512]{1,0:T(8,128)(2,1)}, bf16[256,512]{1,0:T(8,128)(2,1)S(1)}, u32[]{:S(2)}, u32[]{:S(2)}) %collective-permute-start.5) | collective-permute-done | bytes 262176 | tf_op jit(solution)/shard_map/ppermute | solution.py:19
  136.8 0.0 copy-done.6
  136.8 0.7 copy-done.7
  137.5 12.4 %all-to-all-start.1 = ((bf16[64,288,128]{2,1,0:T(8,128)(2,1)}), bf16[64,288,128]{2,1,0:T(8,128)(2,1)}, u32[]{:S(2)}, u32[]{:S(2)}) async-start(bf16[64,288,128]{2,1,0:T(8,128)(2,1)} %bitcast.38), calls=%async_computation.1 | async-start | bytes 9437184 | tf_op jit(solution)/shard_map/all_to_all | solution.py:53
  149.9 8.5 %shard_map.251 = (bf16[256,640]{1,0:T(8,128)(2,1)}, bf16[4096,128]{1,0:T(8,128)(2,1)}, bf16[4096,128]{1,0:T(8,128)(2,1)}) custom-call(s32[1]{0:T(128)} %bitcast.core_ref, f32[256,1536]{1,0:T(8,128)} %get-tuple-element.52.raw, f32[256,1024]{1,0:T(8,128)} %get-tuple-element.55.d_query, f32[256,512]{1,0:T(8,128)} %get-tuple-element.56.d_own, ...), custom_call_target="tpu_custom_call" | custom-call | flops 20000000000 | bytes 8000000 | tf_op jit(solution)/shard_map/pallas_call | solution.py:69
  158.5 0.0 collective-permute-start.6
  158.5 2.9 %collective-permute-done.6 = bf16[4096,128]{1,0:T(8,128)(2,1)S(1)} collective-permute-done((bf16[4096,128]{1,0:T(8,128)(2,1)}, bf16[4096,128]{1,0:T(8,128)(2,1)S(1)}, u32[]{:S(2)}, u32[]{:S(2)}) %collective-permute-start.6) | collective-permute-done | bytes 1048608 | tf_op jit(solution)/shard_map/ppermute | solution.py:49
  161.4 2.5 add_convert_fusion
  163.8 44.9 %all-to-all-done.1 = bf16[64,288,128]{2,1,0:T(8,128)(2,1)} async-done(((bf16[64,288,128]{2,1,0:T(8,128)(2,1)}), bf16[64,288,128]{2,1,0:T(8,128)(2,1)}, u32[]{:S(2)}, u32[]{:S(2)}) %all-to-all-start.1) | async-done | bytes 4718624 | tf_op jit(solution)/shard_map/all_to_all | solution.py:53
  208.7 9.0 %all-to-all-start.2 = ((bf16[64,64,128]{2,1,0:T(8,128)(2,1)}), bf16[64,64,128]{2,1,0:T(8,128)(2,1)S(1)}, u32[]{:S(2)}, u32[]{:S(2)}) async-start(bf16[64,64,128]{2,1,0:T(8,128)(2,1)} %bitcast.11), calls=%async_computation.2 | async-start | bytes 2097152 | tf_op jit(solution)/shard_map/all_to_all | solution.py:53
  217.7 3.0 %convert_reduce_fusion = f32[288,128]{1,0:T(8,128)S(1)} fusion(bf16[64,288,128]{2,1,0:T(8,128)(2,1)} %all-to-all-done.1), kind=kLoop, calls=%fused_computation | loop fusion | flops 4681728 | bytes 4866048 | tf_op jit(solution)/shard_map/reduce_sum | solution.py:807
  220.8 0.6 copy.38
  221.4 0.7 reshape.127
  222.0 0.6 slice_bitcast_fusion
  222.6 14.1 %all-to-all-done.2 = bf16[64,64,128]{2,1,0:T(8,128)(2,1)S(1)} async-done(((bf16[64,64,128]{2,1,0:T(8,128)(2,1)}), bf16[64,64,128]{2,1,0:T(8,128)(2,1)S(1)}, u32[]{:S(2)}, u32[]{:S(2)}) %all-to-all-start.2) | async-done | bytes 1048608 | tf_op jit(solution)/shard_map/all_to_all | solution.py:53
  236.7 0.2 convert_reduce_fusion.1
  236.9 0.6 slice_bitcast_fusion.1
  237.5 0.6 slice_bitcast_fusion.3
  238.1 0.6 slice.89
  238.7 0.6 slice.88
  (16 shorter events, 0.1 us)
Async XLA Ops:
  7.2 36.5 %copy-start.1 = (s32[25]{0:T(128)S(1)}, s32[25]{0:T(128)}, u32[]{:S(2)}) copy-start(s32[25]{0:T(128)} %param.18) | copy-start | bytes 304
  7.2 36.5 %copy-start.2 = (s32[25]{0:T(128)S(1)}, s32[25]{0:T(128)}, u32[]{:S(2)}) copy-start(s32[25]{0:T(128)} %param.17) | copy-start | bytes 304
  7.2 87.0 %all-gather.2.cloned.1.call-start = ((), (), s32[]{:S(2)}) async-start(), calls=%async_computation.3 | async-start | bytes 12417024 | tf_op jit(solution)/shard_map/all_gather | solution.py:611
  12.4 31.3 %all-to-all-start = ((bf16[64,64,128]{2,1,0:T(8,128)(2,1)}), bf16[64,64,128]{2,1,0:T(8,128)(2,1)S(1)}, u32[]{:S(2)}, u32[]{:S(2)}) async-start(bf16[64,64,128]{2,1,0:T(8,128)(2,1)} %broadcast_in_dim.73), calls=%async_computation | async-start | bytes 2097152 | tf_op jit(solution)/shard_map/all_to_all | solution.py:53
  43.7 2.7 %copy-start = (bf16[64,64,128]{2,1,0:T(8,128)(2,1)}, bf16[64,64,128]{2,1,0:T(8,128)(2,1)S(1)}, u32[]{:S(2)}) copy-start(bf16[64,64,128]{2,1,0:T(8,128)(2,1)S(1)} %all-to-all-done) | copy-start | bytes 3145732
  43.7 2.7 %collective-permute-start = (bf16[4096,128]{1,0:T(8,128)(2,1)S(1)}, bf16[4096,128]{1,0:T(8,128)(2,1)S(1)}, u32[]{:S(2)}, u32[]{:S(2)}) collective-permute-start(bf16[4096,128]{1,0:T(8,128)(2,1)S(1)} %bitcast.39), channel_id=1, source_target_pairs={{0,1},{1,0},{2,3},{3,2},{4,5},{5,4},{6,7},{7,6},{8,9},{9,8},{10,11... | collective-permute-start | bytes 3145736 | tf_op jit(solution)/shard_map/ppermute | solution.py:49
  46.4 1.0 copy-start.3
  53.7 7.0 %collective-permute-start.2 = (bf16[256,512]{1,0:T(8,128)(2,1)}, bf16[256,512]{1,0:T(8,128)(2,1)S(1)}, u32[]{:S(2)}, u32[]{:S(2)}) collective-permute-start(bf16[256,512]{1,0:T(8,128)(2,1)} %get-tuple-element.47.kv_own), channel_id=1, source_target_pairs={{0,1},{1,2},{2,3},{3,4},{4,5},{5,6},{6,7},{7,8},{8,9},{9,10},{10,1... | collective-permute-start | bytes 786440 | tf_op jit(solution)/shard_map/ppermute | solution.py:19
  55.8 10.4 %collective-permute-start.1 = (bf16[256,512]{1,0:T(8,128)(2,1)}, bf16[256,512]{1,0:T(8,128)(2,1)S(1)}, u32[]{:S(2)}, u32[]{:S(2)}) collective-permute-start(bf16[256,512]{1,0:T(8,128)(2,1)} %get-tuple-element.47.kv_own), channel_id=1, source_target_pairs={{0,2},{1,3},{2,4},{3,5},{4,6},{5,7},{6,8},{7,9},{8,10},{9,11},{10,... | collective-permute-start | bytes 786440 | tf_op jit(solution)/shard_map/ppermute | solution.py:19
  60.7 5.5 %copy-start.4 = (bf16[256,512]{1,0:T(8,128)(2,1)}, bf16[256,512]{1,0:T(8,128)(2,1)S(1)}, u32[]{:S(2)}) copy-start(bf16[256,512]{1,0:T(8,128)(2,1)S(1)} %collective-permute-done.2.kv_near) | copy-start | bytes 786436
  66.2 0.7 copy-start.5
  116.2 9.3 %collective-permute-start.3 = (bf16[8,8,288,128]{3,2,1,0:T(8,128)(2,1)}, bf16[8,8,288,128]{3,2,1,0:T(8,128)(2,1)}, u32[]{:S(2)}, u32[]{:S(2)}) collective-permute-start(bf16[8,8,288,128]{3,2,1,0:T(8,128)(2,1)} %get-tuple-element.61), channel_id=1, source_target_pairs={{0,1},{1,0},{2,3},{3,2},{4,5},{5,4},{6,7},{7,6},{8,9},{9,8},{10,11... | collective-permute-start | bytes 14155784 | tf_op jit(solution)/shard_map/ppermute | solution.py:49
  122.9 9.5 %collective-permute-start.4 = (bf16[256,512]{1,0:T(8,128)(2,1)}, bf16[256,512]{1,0:T(8,128)(2,1)S(1)}, u32[]{:S(2)}, u32[]{:S(2)}) collective-permute-start(bf16[256,512]{1,0:T(8,128)(2,1)} %get-tuple-element.64), channel_id=1, source_target_pairs={{1,0},{2,1},{3,2},{4,3},{5,4},{6,5},{7,6},{8,7},{9,8},{10,9},{11,1... | collective-permute-start | bytes 786440 | tf_op jit(solution)/shard_map/ppermute | solution.py:19
  124.2 12.6 %collective-permute-start.5 = (bf16[256,512]{1,0:T(8,128)(2,1)}, bf16[256,512]{1,0:T(8,128)(2,1)S(1)}, u32[]{:S(2)}, u32[]{:S(2)}) collective-permute-start(bf16[256,512]{1,0:T(8,128)(2,1)} %get-tuple-element.62), channel_id=1, source_target_pairs={{2,0},{3,1},{4,2},{5,3},{6,4},{7,5},{8,6},{9,7},{10,8},{11,9},{12,... | collective-permute-start | bytes 786440 | tf_op jit(solution)/shard_map/ppermute | solution.py:19
  132.4 4.4 %copy-start.6 = (bf16[256,512]{1,0:T(8,128)(2,1)}, bf16[256,512]{1,0:T(8,128)(2,1)S(1)}, u32[]{:S(2)}) copy-start(bf16[256,512]{1,0:T(8,128)(2,1)S(1)} %collective-permute-done.4.near) | copy-start | bytes 786436
  136.8 0.7 copy-start.7
  137.5 71.2 %all-to-all-start.1 = ((bf16[64,288,128]{2,1,0:T(8,128)(2,1)}), bf16[64,288,128]{2,1,0:T(8,128)(2,1)}, u32[]{:S(2)}, u32[]{:S(2)}) async-start(bf16[64,288,128]{2,1,0:T(8,128)(2,1)} %bitcast.38), calls=%async_computation.1 | async-start | bytes 9437184 | tf_op jit(solution)/shard_map/all_to_all | solution.py:53
  158.5 2.9 %collective-permute-start.6 = (bf16[4096,128]{1,0:T(8,128)(2,1)}, bf16[4096,128]{1,0:T(8,128)(2,1)S(1)}, u32[]{:S(2)}, u32[]{:S(2)}) collective-permute-start(bf16[4096,128]{1,0:T(8,128)(2,1)} %get-tuple-element.73), channel_id=1, source_target_pairs={{0,1},{1,0},{2,3},{3,2},{4,5},{5,4},{6,7},{7,6},{8,9},{9,8},{10,11... | collective-permute-start | bytes 3145736 | tf_op jit(solution)/shard_map/ppermute | solution.py:49
  208.7 28.1 %all-to-all-start.2 = ((bf16[64,64,128]{2,1,0:T(8,128)(2,1)}), bf16[64,64,128]{2,1,0:T(8,128)(2,1)S(1)}, u32[]{:S(2)}, u32[]{:S(2)}) async-start(bf16[64,64,128]{2,1,0:T(8,128)(2,1)} %bitcast.11), calls=%async_computation.2 | async-start | bytes 2097152 | tf_op jit(solution)/shard_map/all_to_all | solution.py:53
Sparse Core Ops, SparseCore 0:
  11.7 82.4 all-gather.1

commit v5 on v4

--- a/solution.py
+++ b/solution.py
@@ -234,12 +234,13 @@
 
 
 def feed_forward(
-    core_ref, tok, out_grad, live, gains, heads_low, spread_flat_in, spread_core_in, full,
+    core_ref, live, gains, tok_in, out_grad_in, heads_in, spread_flat_in, spread_core_in, full,
     gain_grads, mixed_out, d_state_out, d_heads_out, low_own_out, d_gate_up_out, own_down_out,
     own_out_out, send_out,
     weights, rest, down, act, act_slope, hidden, proj, state, total, back, low_flat, low, turned_low,
     low_branch, loose, loose_out, turn_down, spread_flat, spread_core, mixed, d_state, d_heads,
-    low_own, d_gate_up, own_down, own_out, send, weight_sem, rest_sem, out_sem,
+    low_own, d_gate_up, own_down, own_out, send, tok, out_grad, heads_low,
+    weight_sem, rest_sem, out_sem,
 ):
     core = core_ref[0]
     tiles, tile = weights.shape[0], weights.shape[2]
@@ -271,22 +272,30 @@
     down_copy = rest_copy(1, 0, 2 * width)
     flat_copy = pltpu.make_async_copy(spread_flat_in, spread_flat, rest_sem.at[2])
     core_copy = pltpu.make_async_copy(spread_core_in, spread_core, rest_sem.at[3])
+    heads_copy = pltpu.make_async_copy(heads_in, heads_low, rest_sem.at[4])
+    tok_copy = pltpu.make_async_copy(tok_in, tok, rest_sem.at[5])
+    grad_copy = pltpu.make_async_copy(out_grad_in, out_grad, rest_sem.at[6])
+    heads_copy.start()
     out_copy.start()
+    tok_copy.start()
     flat_copy.start()
     down_copy.start()
     for index in range(half):
         weight_copy(index).start()
         weight_copy(half + index).start()
     core_copy.start()
+    grad_copy.start()
     leaving = []
 
     def leave(source, target):
         leaving.append(pltpu.make_async_copy(source, target, out_sem.at[len(leaving)]))
         leaving[-1].start()
 
+    heads_copy.wait()
     out_copy.wait()
     w_out = rest[:, 2 * width :]
     proj[...] = dot(heads_low[...], w_out)
+    tok_copy.wait()
     unit, _ = normed(proj[...])
     state[...] = tok[...].astype(F32) + unit * gains[1:2, :]
     unit, scale = normed(state[...])
@@ -325,7 +334,7 @@
         total[...] += dot(hidden[:, columns], down_tile(index))
         return carry
 
-    lax.fori_loop(0, half, forward, 0)
+    lax.fori_loop(0, half, forward, 0, unroll=True)
     core_copy.wait()
     low_own[...] = dot(low[...], spread_core[0]).astype(BF16)
     turned_low[...] = jnp.transpose(dot(low[...], spread_core[1])).astype(BF16)
@@ -334,6 +343,7 @@
     branch_unit, branch_scale = normed(total[...])
     mixed[...] = ((state[...] + branch_unit * gains[3:4, :]) * live[...]).astype(BF16)
     leave(mixed, mixed_out)
+    grad_copy.wait()
     cotangent = out_grad[...].astype(F32) * live[...]
     d_branch, gain_grads[3:4, :] = normed_back(
         cotangent, branch_unit, branch_scale, gains[3:4, :]
@@ -375,7 +385,7 @@
             ]
         return carry
 
-    lax.fori_loop(0, half, backward, 0)
+    lax.fori_loop(0, half, backward, 0, unroll=True)
     leave(d_gate_up, d_gate_up_out)
     leave(own_down, own_down_out)
 
@@ -431,33 +441,55 @@
 
 
 def own_gradients(
-    d_gate_up, low_own, own_down, own_out, arrived, both_out,
-    both, other, turned_low, loose, arrived_sem, both_sem,
+    low_own, d_gate_up_in, own_down_in, own_out_in, arrived, both_out,
+    both, other, d_gate_up, own_down, own_out, turned_low, loose, tile_sem, in_sem, arrived_sem, both_sem,
 ):
-    copy = pltpu.make_async_copy(arrived, other, arrived_sem)
-    copy.start()
+    tile = 512
+    steps = d_gate_up.shape[1] // tile
+
+    def tile_copy(index):
+        span = pl.ds(pl.multiple_of(index * tile, tile), tile)
+        return pltpu.make_async_copy(
+            d_gate_up_in.at[:, span], d_gate_up.at[:, span], tile_sem.at[index]
+        )
+
+    for index in range(steps):
+        tile_copy(index).start()
+    copies = [
+        pltpu.make_async_copy(own_down_in, own_down, in_sem.at[0]),
+        pltpu.make_async_copy(own_out_in, own_out, in_sem.at[1]),
+    ]
+
+    def arrival(block):
+        return pltpu.make_async_copy(arrived.at[block], other.at[block], arrived_sem.at[block])
+
+    for copy in copies:
+        copy.start()
     blocks, strips, down_size = own_down.shape[:3]
+    for block in range(blocks):
+        arrival(block).start()
     chips = blocks * strips
     per = low_own.shape[1] // chips
-    tile = 512
-    steps = d_gate_up.shape[1] // tile
     row_tiles = d_gate_up.shape[1] // LANES
     chunk = per * row_tiles
     turned_low[...] = jnp.transpose(low_own[...].astype(F32)).astype(BF16)
 
     def place(index, carry):
+        tile_copy(index).wait()
         grad = d_gate_up[:, pl.ds(pl.multiple_of(index * tile, tile), tile)]
         block = dot(turned_low[...], grad)
         place_rows(loose, block, index * (tile // LANES), per, chips, row_tiles)
         return carry
 
     lax.fori_loop(0, steps, place, 0)
-    copy.wait()
+    for copy in copies:
+        copy.wait()
 
     def leave(block):
         return pltpu.make_async_copy(both.at[block], both_out.at[block], both_sem.at[block])
 
     def pack(block, carry):
+        arrival(block).wait()
         for strip in range(strips):
             both[block, strip, :chunk, :] = (
                 loose_chunk(loose, block * strips + strip, chunk)
@@ -608,20 +640,16 @@
     head = kv_cols // 2
     hshard = norm_query.shape[0]
 
-    mlp_full = lax.all_gather(
-        jnp.concatenate(
-            [
-                jnp.pad(w_gate_up, ((0, SLOTS - shard), (0, 0))),
-                w_down[:SLOTS],
-                w_down[SLOTS:],
-                w_output,
-            ],
-            axis=1,
-        ),
-        "fsdp",
-        axis=0,
-        tiled=True,
-    )
+    gathered = jnp.zeros((SLOTS, gu_cols + 3 * width), BF16)
+    column = 0
+    zero = jnp.zeros((), BF16)
+    for part, first in ((w_gate_up, 0), (w_down, 0), (w_down, SLOTS), (w_output, 0)):
+        high, wide = part.shape
+        after = gathered.shape[1] - column - wide
+        rows = (-first, SLOTS - high + first, 0)
+        gathered = gathered + lax.pad(part, zero, (rows, (column, after, 0)))
+        column += wide
+    mlp_full = lax.all_gather(gathered, "fsdp", axis=0, tiled=True)
 
     tiles = qkv_cols // LANES
     chunk = 64
@@ -702,7 +730,7 @@
             shape(chunk_shape, BF16),
         ),
         (
-            core_arg, tokens, out_grad, live, gains, heads_low, spread_flat, spread_core, mlp_full,
+            core_arg, live, gains, tokens, out_grad, heads_low, spread_flat, spread_core, mlp_full,
         ),
         scratch=(
             pltpu.VMEM((gu_cols // tile, size * SLOTS, tile), BF16),
@@ -732,11 +760,14 @@
             pltpu.VMEM((blocks, strips, out_at - down_at, LANES), BF16),
             pltpu.VMEM((blocks, strips, 6 * SLOTS, LANES), BF16),
             pltpu.VMEM(chunk_shape, BF16),
+            pltpu.VMEM((tok_rows, width), BF16),
+            pltpu.VMEM((tok_rows, width), BF16),
+            pltpu.VMEM((tok_rows, q_cols), BF16),
             pltpu.SemaphoreType.DMA((gu_cols // tile,)),
-            pltpu.SemaphoreType.DMA((4,)),
+            pltpu.SemaphoreType.DMA((7,)),
             pltpu.SemaphoreType.DMA((9,)),
         ),
-        specs=[SCALAR] + [WHOLE] * 5 + [AWAY] * 3,
+        specs=[SCALAR] + [WHOLE] * 2 + [AWAY] * 6,
         out_specs=(WHOLE,) + (AWAY,) * 8,
         flops=12e9,
     )
@@ -764,16 +795,21 @@
     both_mlp = call(
         own_gradients,
         shape(chunk_shape, BF16),
-        (d_gate_up, low_own, own_down, own_out, arrived),
+        (low_own, d_gate_up, own_down, own_out, arrived),
         scratch=(
             pltpu.VMEM(chunk_shape, BF16),
             pltpu.VMEM(chunk_shape, BF16),
+            pltpu.VMEM((tok_rows, gu_cols), BF16),
+            pltpu.VMEM((blocks, strips, out_at - down_at, LANES), BF16),
+            pltpu.VMEM((blocks, strips, 6 * SLOTS, LANES), BF16),
             pltpu.VMEM((width // 2, tok_rows), BF16),
             pltpu.VMEM((chips * (down_at + ODD), LANES), F32),
-            pltpu.SemaphoreType.DMA,
+            pltpu.SemaphoreType.DMA((gu_cols // tile,)),
+            pltpu.SemaphoreType.DMA((2,)),
             pltpu.SemaphoreType.DMA((blocks,)),
-        ),
-        specs=[WHOLE] * 4 + [AWAY],
+            pltpu.SemaphoreType.DMA((blocks,)),
+        ),
+        specs=[WHOLE] + [AWAY] * 4,
         out_specs=AWAY,
         flops=12e9,
         vmem=62 * 1024 * 1024,

time: 247 us -> 245 us (level)
  no operation moved by 1% of the time
where the time goes in v5:
time: 245 us; the launch traced here: 244 us
  waiting for transfers between devices  114 us (47%)
  Pallas kernels  53.6 us (22%)
  starting transfers between devices  41 us (17%)
  between operations  14.3 us (6%)
  other arithmetic  10.5 us (4%)
  local copies, waits for them, and re-layouts  10.2 us (4%)
    all_to_all x3, waiting for transfers between devices, exchange(): lax.all_to_all(blocks, 'fsdp', split_axis=0, concat_axis=0, tiled=True, a...  78.3 us
    pallas_call x6, Pallas kernels, call(): pl.pallas_call(kernel, out_shape=outs, in_specs=specs, **{} if out_specs...  53.6 us
    all_to_all x3, starting transfers between devices, exchange(): lax.all_to_all(blocks, 'fsdp', split_axis=0, concat_axis=0, tiled=True, a...  33.3 us
    all_gather x1, waiting for transfers between devices, on_device(): mlp_full = lax.all_gather(gathered, 'fsdp', axis=0, tiled=True)  22.3 us
    ppermute x4, waiting for transfers between devices, shifted(): return lax.ppermute(block, axis, route)  9.95 us
    ppermute x4, starting transfers between devices, shifted(): return lax.ppermute(block, axis, route)  7.33 us
  transfers between devices with their start and end apart: 11, of which 8 were waited for; matrix products, arithmetic and copies ran while one was open for 6% of the time, Pallas kernels for 13%

profile of v5, /device:TPU:0, one launch (start us, length us, event | category | flops | bytes accessed | tf_op | source)
XLA Modules:
  0.0 244.0 jit_solution(5808819087277935123)
XLA Ops:
  7.2 0.0 copy-start.1
  7.2 0.0 copy-start.2
  7.2 0.0 all-gather.2.cloned.1.call-start
  7.2 1.5 fusion.3
  8.8 0.0 all-gather.2.cloned.1.call-update
  8.8 0.7 pad_maximum_fusion
  9.6 0.8 pad_add_fusion
  10.4 1.3 broadcast_in_dim.73
  11.7 11.5 %all-to-all-start = ((bf16[64,64,128]{2,1,0:T(8,128)(2,1)}), bf16[64,64,128]{2,1,0:T(8,128)(2,1)S(1)}, u32[]{:S(2)}, u32[]{:S(2)}) async-start(bf16[64,64,128]{2,1,0:T(8,128)(2,1)} %broadcast_in_dim.73), calls=%async_computation | async-start | bytes 2097152 | tf_op jit(solution)/shard_map/all_to_all | solution.py:53
  23.2 19.7 %all-to-all-done = bf16[64,64,128]{2,1,0:T(8,128)(2,1)S(1)} async-done(((bf16[64,64,128]{2,1,0:T(8,128)(2,1)}), bf16[64,64,128]{2,1,0:T(8,128)(2,1)S(1)}, u32[]{:S(2)}, u32[]{:S(2)}) %all-to-all-start) | async-done | bytes 1048608 | tf_op jit(solution)/shard_map/all_to_all | solution.py:53
  43.0 0.0 copy-start
  43.0 0.0 collective-permute-start
  43.0 0.0 copy-done.1
  43.0 0.0 copy-done.2
  43.0 0.1 select_reduce_fusion.1
  43.1 0.1 fusion.4
  43.3 0.1 select_reduce_fusion
  43.4 1.3 multiply_sine_fusion
  44.6 1.0 collective-permute-done.peer
  45.6 0.0 copy-start.3
  45.6 0.0 copy-done
  45.6 1.0 copy-done.3
  46.6 6.4 %shard_map.246 = (f32[256,1536]{1,0:T(8,128)}, bf16[256,1024]{1,0:T(8,128)(2,1)}, bf16[256,512]{1,0:T(8,128)(2,1)}, f32[8,640]{1,0:T(8,128)}, f32[8,256]{1,0:T(8,128)}, /*index=5*/bf16[2,320,1536]{2,1,0:T(8,128)(2,1)}) custom-call(s32[1]{0:T(128)} %bitcast.core_ref, bf16[256,640]{1,0:T(8,128)(2,1)} %tok.3, bf16[4096,128]{1,0:T(8,128)(2,1)} %bitcast.40, ...), custom_call_target="tpu_custom_call" | custom-call | flops 4000000000 | bytes 8000000 | tf_op jit(solution)/shard_map/pallas_call | solution.py:69
  53.0 2.1 collective-permute-start.2
  55.1 2.7 %collective-permute-start.1 = (bf16[256,512]{1,0:T(8,128)(2,1)}, bf16[256,512]{1,0:T(8,128)(2,1)S(1)}, u32[]{:S(2)}, u32[]{:S(2)}) collective-permute-start(bf16[256,512]{1,0:T(8,128)(2,1)} %get-tuple-element.47.kv_own), channel_id=1, source_target_pairs={{0,2},{1,3},{2,4},{3,5},{4,6},{5,7},{6,8},{7,9},{8,10},{9,11},{10,... | collective-permute-start | bytes 786440 | tf_op jit(solution)/shard_map/ppermute | solution.py:19
  57.8 0.1 fusion.9
  57.9 0.6 select_n.54.k_seq
  58.5 0.8 copy.32.q_seq
  59.3 0.8 copy.33.live
  60.1 0.0 collective-permute-done.2.kv_near
  60.1 5.4 %collective-permute-done.1.kv_far = bf16[256,512]{1,0:T(8,128)(2,1)S(1)} collective-permute-done((bf16[256,512]{1,0:T(8,128)(2,1)}, bf16[256,512]{1,0:T(8,128)(2,1)S(1)}, u32[]{:S(2)}, u32[]{:S(2)}) %collective-permute-start.1) | collective-permute-done | bytes 262176 | tf_op jit(solution)/shard_map/ppermute | solution.py:19
  65.5 0.0 copy-done.4
  65.5 0.7 copy-done.5
  66.2 5.0 %shard_map.247 = (bf16[256,1024]{1,0:T(8,128)(2,1)}, f32[256,128]{1,0:T(8,128)}, bf16[640,1024]{1,0:T(8,128)(2,1)}, bf16[2,640,320]{2,1,0:T(8,128)(2,1)}) custom-call(s32[1]{0:T(128)} %bitcast.core_ref, bf16[256,1024]{1,0:T(8,128)(2,1)} %get-tuple-element.46.query_low, bf16[256,512]{1,0:T(8,128)(2,1)} %copy-done.5, bf16[256,512]{1,0:T(8,128)(2,1)} %copy-done.4, ...), custom_call_target="tpu_custom_call" | custom-call | flops 20000000000 | bytes 8000000 | tf_op jit(solution)/shard_map/pallas_call | solution.py:69
  71.2 22.3 %all-gather.2.cloned.1.call-done.full = bf16[1024,6016]{1,0:T(8,128)(2,1)} async-done(((bf16[8,6016]{1,0:T(8,128)(2,1)}), bf16[1024,6016]{1,0:T(8,128)(2,1)}) %all-gather.2.cloned.1.call-update) | async-done | bytes 12320784 | tf_op jit(solution)/shard_map/all_gather | solution.py:652
  93.5 20.8 %shard_map.248 = (f32[8,640]{1,0:T(8,128)}, bf16[256,640]{1,0:T(8,128)(2,1)}, f32[256,640]{1,0:T(8,128)}, bf16[256,1024]{1,0:T(8,128)(2,1)}, bf16[256,320]{1,0:T...) custom-call(s32[1]{0:T(128)} %bitcast.core_ref, ...), custom_call_target="tpu_custom_call" | custom-call | flops 12000000000 | bytes 8000000 | tf_op jit(solution)/shard_map/pallas_call | solution.py:69
  114.2 0.3 collective-permute-start.3
  114.6 6.1 %shard_map.249 = (f32[256,1024]{1,0:T(8,128)}, f32[256,512]{1,0:T(8,128)}, bf16[256,512]{1,0:T(8,128)(2,1)}, bf16[256,512]{1,0:T(8,128)(2,1)}) custom-call(bf16[256,1024]{1,0:T(8,128)(2,1)} %get-tuple-element.46.query_low, bf16[256,512]{1,0:T(8,128)(2,1)} %copy-done.5, bf16[256,512]{1,0:T(8,128)(2,1)} %copy-done.4, ...), custom_call_target="tpu_custom_call" | custom-call | flops 20000000000 | bytes 8000000 | tf_op jit(solution)/shard_map/pallas_call | solution.py:69
  120.7 1.3 collective-permute-start.4
  122.0 1.3 collective-permute-start.5
  123.3 0.0 collective-permute-done.3.arrived
  123.3 6.8 %shard_map.250 = bf16[8,8,288,128]{3,2,1,0:T(8,128)(2,1)} custom-call(bf16[256,320]{1,0:T(8,128)(2,1)} %get-tuple-element.57.low_own, bf16[256,4096]{1,0:T(8,128)(2,1)} %get-tuple-element.58.d_gate_up_in, bf16[8,8,80,128]{3,2,1,0:T(8,128)(2,1)} %get-tuple-element.59.own_down_in, bf16[8,8,48,128]{3,2,1,0:T(8,128)(2,1)} %get-tuple-element.60.own_out_in, ...), custom_call_target="tpu_custom_call" | custom-call | flops 12000000000 | bytes 8000000 | tf_op jit(solution)/shard_map/pallas_call | solution.py:69
  130.1 0.0 collective-permute-done.4.near
  130.1 0.0 copy-start.6
  130.2 4.5 %collective-permute-done.5.far = bf16[256,512]{1,0:T(8,128)(2,1)S(1)} collective-permute-done((bf16[256,512]{1,0:T(8,128)(2,1)}, bf16[256,512]{1,0:T(8,128)(2,1)S(1)}, u32[]{:S(2)}, u32[]{:S(2)}) %collective-permute-start.5) | collective-permute-done | bytes 262176 | tf_op jit(solution)/shard_map/ppermute | solution.py:19
  134.7 0.0 copy-done.6
  134.7 0.7 copy-done.7
  135.4 12.4 %all-to-all-start.1 = ((bf16[64,288,128]{2,1,0:T(8,128)(2,1)}), bf16[64,288,128]{2,1,0:T(8,128)(2,1)}, u32[]{:S(2)}, u32[]{:S(2)}) async-start(bf16[64,288,128]{2,1,0:T(8,128)(2,1)} %bitcast.38), calls=%async_computation.1 | async-start | bytes 9437184 | tf_op jit(solution)/shard_map/all_to_all | solution.py:53
  147.8 8.5 %shard_map.251 = (bf16[256,640]{1,0:T(8,128)(2,1)}, bf16[4096,128]{1,0:T(8,128)(2,1)}, bf16[4096,128]{1,0:T(8,128)(2,1)}) custom-call(s32[1]{0:T(128)} %bitcast.core_ref, f32[256,1536]{1,0:T(8,128)} %get-tuple-element.52.raw, f32[256,1024]{1,0:T(8,128)} %get-tuple-element.55.d_query, f32[256,512]{1,0:T(8,128)} %get-tuple-element.56.d_own, ...), custom_call_target="tpu_custom_call" | custom-call | flops 20000000000 | bytes 8000000 | tf_op jit(solution)/shard_map/pallas_call | solution.py:69
  156.3 0.0 collective-permute-start.6
  156.3 2.9 %collective-permute-done.6 = bf16[4096,128]{1,0:T(8,128)(2,1)S(1)} collective-permute-done((bf16[4096,128]{1,0:T(8,128)(2,1)}, bf16[4096,128]{1,0:T(8,128)(2,1)S(1)}, u32[]{:S(2)}, u32[]{:S(2)}) %collective-permute-start.6) | collective-permute-done | bytes 1048608 | tf_op jit(solution)/shard_map/ppermute | solution.py:49
  159.2 2.5 %add_convert_fusion = bf16[4096,128]{1,0:T(8,128)(2,1)} fusion(bf16[4096,128]{1,0:T(8,128)(2,1)S(1)} %collective-permute-done.6, bf16[4096,128]{1,0:T(8,128)(2,1)} %get-tuple-element.72), kind=kLoop, calls=%fused_computation.2 | loop fusion | flops 2097152 | bytes 3145728 | tf_op jit(solution)/shard_map/convert_element_type | solution.py:837
  161.7 44.5 %all-to-all-done.1 = bf16[64,288,128]{2,1,0:T(8,128)(2,1)} async-done(((bf16[64,288,128]{2,1,0:T(8,128)(2,1)}), bf16[64,288,128]{2,1,0:T(8,128)(2,1)}, u32[]{:S(2)}, u32[]{:S(2)}) %all-to-all-start.1) | async-done | bytes 4718624 | tf_op jit(solution)/shard_map/all_to_all | solution.py:53
  206.2 9.4 %all-to-all-start.2 = ((bf16[64,64,128]{2,1,0:T(8,128)(2,1)}), bf16[64,64,128]{2,1,0:T(8,128)(2,1)S(1)}, u32[]{:S(2)}, u32[]{:S(2)}) async-start(bf16[64,64,128]{2,1,0:T(8,128)(2,1)} %bitcast.11), calls=%async_computation.2 | async-start | bytes 2097152 | tf_op jit(solution)/shard_map/all_to_all | solution.py:53
  215.6 3.0 %convert_reduce_fusion = f32[288,128]{1,0:T(8,128)S(1)} fusion(bf16[64,288,128]{2,1,0:T(8,128)(2,1)} %all-to-all-done.1), kind=kLoop, calls=%fused_computation | loop fusion | flops 4681728 | bytes 4866048 | tf_op jit(solution)/shard_map/reduce_sum | solution.py:843
  218.6 0.6 copy.38
  219.2 0.7 reshape.127
  219.9 0.6 slice_bitcast_fusion
  220.5 14.1 %all-to-all-done.2 = bf16[64,64,128]{2,1,0:T(8,128)(2,1)S(1)} async-done(((bf16[64,64,128]{2,1,0:T(8,128)(2,1)}), bf16[64,64,128]{2,1,0:T(8,128)(2,1)S(1)}, u32[]{:S(2)}, u32[]{:S(2)}) %all-to-all-start.2) | async-done | bytes 1048608 | tf_op jit(solution)/shard_map/all_to_all | solution.py:53
  234.6 0.2 convert_reduce_fusion.1
  234.7 0.6 slice_bitcast_fusion.1
  235.3 0.6 slice_bitcast_fusion.3
  235.9 0.6 slice.83
  236.5 0.6 slice.82
  (15 shorter events, 0.1 us)
Async XLA Ops:
  7.2 35.8 %copy-start.1 = (s32[25]{0:T(128)S(1)}, s32[25]{0:T(128)}, u32[]{:S(2)}) copy-start(s32[25]{0:T(128)} %param.18) | copy-start | bytes 304
  7.2 35.8 %copy-start.2 = (s32[25]{0:T(128)S(1)}, s32[25]{0:T(128)}, u32[]{:S(2)}) copy-start(s32[25]{0:T(128)} %param.17) | copy-start | bytes 304
  7.2 86.3 %all-gather.2.cloned.1.call-start = ((), (), s32[]{:S(2)}) async-start(), calls=%async_computation.3 | async-start | bytes 12417024 | tf_op jit(solution)/shard_map/all_gather | solution.py:652
  11.7 31.2 %all-to-all-start = ((bf16[64,64,128]{2,1,0:T(8,128)(2,1)}), bf16[64,64,128]{2,1,0:T(8,128)(2,1)S(1)}, u32[]{:S(2)}, u32[]{:S(2)}) async-start(bf16[64,64,128]{2,1,0:T(8,128)(2,1)} %broadcast_in_dim.73), calls=%async_computation | async-start | bytes 2097152 | tf_op jit(solution)/shard_map/all_to_all | solution.py:53
  43.0 2.7 %copy-start = (bf16[64,64,128]{2,1,0:T(8,128)(2,1)}, bf16[64,64,128]{2,1,0:T(8,128)(2,1)S(1)}, u32[]{:S(2)}) copy-start(bf16[64,64,128]{2,1,0:T(8,128)(2,1)S(1)} %all-to-all-done) | copy-start | bytes 3145732
  43.0 2.7 %collective-permute-start = (bf16[4096,128]{1,0:T(8,128)(2,1)S(1)}, bf16[4096,128]{1,0:T(8,128)(2,1)S(1)}, u32[]{:S(2)}, u32[]{:S(2)}) collective-permute-start(bf16[4096,128]{1,0:T(8,128)(2,1)S(1)} %bitcast.39), channel_id=1, source_target_pairs={{0,1},{1,0},{2,3},{3,2},{4,5},{5,4},{6,7},{7,6},{8,9},{9,8},{10,11... | collective-permute-start | bytes 3145736 | tf_op jit(solution)/shard_map/ppermute | solution.py:49
  45.6 1.0 copy-start.3
  53.0 7.1 %collective-permute-start.2 = (bf16[256,512]{1,0:T(8,128)(2,1)}, bf16[256,512]{1,0:T(8,128)(2,1)S(1)}, u32[]{:S(2)}, u32[]{:S(2)}) collective-permute-start(bf16[256,512]{1,0:T(8,128)(2,1)} %get-tuple-element.47.kv_own), channel_id=1, source_target_pairs={{0,1},{1,2},{2,3},{3,4},{4,5},{5,6},{6,7},{7,8},{8,9},{9,10},{10,1... | collective-permute-start | bytes 786440 | tf_op jit(solution)/shard_map/ppermute | solution.py:19
  55.1 10.4 %collective-permute-start.1 = (bf16[256,512]{1,0:T(8,128)(2,1)}, bf16[256,512]{1,0:T(8,128)(2,1)S(1)}, u32[]{:S(2)}, u32[]{:S(2)}) collective-permute-start(bf16[256,512]{1,0:T(8,128)(2,1)} %get-tuple-element.47.kv_own), channel_id=1, source_target_pairs={{0,2},{1,3},{2,4},{3,5},{4,6},{5,7},{6,8},{7,9},{8,10},{9,11},{10,... | collective-permute-start | bytes 786440 | tf_op jit(solution)/shard_map/ppermute | solution.py:19
  60.1 5.4 %copy-start.4 = (bf16[256,512]{1,0:T(8,128)(2,1)}, bf16[256,512]{1,0:T(8,128)(2,1)S(1)}, u32[]{:S(2)}) copy-start(bf16[256,512]{1,0:T(8,128)(2,1)S(1)} %collective-permute-done.2.kv_near) | copy-start | bytes 786436
  65.5 0.7 copy-start.5
  114.2 9.1 %collective-permute-start.3 = (bf16[8,8,288,128]{3,2,1,0:T(8,128)(2,1)}, bf16[8,8,288,128]{3,2,1,0:T(8,128)(2,1)}, u32[]{:S(2)}, u32[]{:S(2)}) collective-permute-start(bf16[8,8,288,128]{3,2,1,0:T(8,128)(2,1)} %get-tuple-element.61), channel_id=1, source_target_pairs={{0,1},{1,0},{2,3},{3,2},{4,5},{5,4},{6,7},{7,6},{8,9},{9,8},{10,11... | collective-permute-start | bytes 14155784 | tf_op jit(solution)/shard_map/ppermute | solution.py:49
  120.7 9.4 %collective-permute-start.4 = (bf16[256,512]{1,0:T(8,128)(2,1)}, bf16[256,512]{1,0:T(8,128)(2,1)S(1)}, u32[]{:S(2)}, u32[]{:S(2)}) collective-permute-start(bf16[256,512]{1,0:T(8,128)(2,1)} %get-tuple-element.64), channel_id=1, source_target_pairs={{1,0},{2,1},{3,2},{4,3},{5,4},{6,5},{7,6},{8,7},{9,8},{10,9},{11,1... | collective-permute-start | bytes 786440 | tf_op jit(solution)/shard_map/ppermute | solution.py:19
  122.0 12.6 %collective-permute-start.5 = (bf16[256,512]{1,0:T(8,128)(2,1)}, bf16[256,512]{1,0:T(8,128)(2,1)S(1)}, u32[]{:S(2)}, u32[]{:S(2)}) collective-permute-start(bf16[256,512]{1,0:T(8,128)(2,1)} %get-tuple-element.62), channel_id=1, source_target_pairs={{2,0},{3,1},{4,2},{5,3},{6,4},{7,5},{8,6},{9,7},{10,8},{11,9},{12,... | collective-permute-start | bytes 786440 | tf_op jit(solution)/shard_map/ppermute | solution.py:19
  130.1 4.5 %copy-start.6 = (bf16[256,512]{1,0:T(8,128)(2,1)}, bf16[256,512]{1,0:T(8,128)(2,1)S(1)}, u32[]{:S(2)}) copy-start(bf16[256,512]{1,0:T(8,128)(2,1)S(1)} %collective-permute-done.4.near) | copy-start | bytes 786436
  134.7 0.7 copy-start.7
  135.4 70.8 %all-to-all-start.1 = ((bf16[64,288,128]{2,1,0:T(8,128)(2,1)}), bf16[64,288,128]{2,1,0:T(8,128)(2,1)}, u32[]{:S(2)}, u32[]{:S(2)}) async-start(bf16[64,288,128]{2,1,0:T(8,128)(2,1)} %bitcast.38), calls=%async_computation.1 | async-start | bytes 9437184 | tf_op jit(solution)/shard_map/all_to_all | solution.py:53
  156.3 2.9 %collective-permute-start.6 = (bf16[4096,128]{1,0:T(8,128)(2,1)}, bf16[4096,128]{1,0:T(8,128)(2,1)S(1)}, u32[]{:S(2)}, u32[]{:S(2)}) collective-permute-start(bf16[4096,128]{1,0:T(8,128)(2,1)} %get-tuple-element.73), channel_id=1, source_target_pairs={{0,1},{1,0},{2,3},{3,2},{4,5},{5,4},{6,7},{7,6},{8,9},{9,8},{10,11... | collective-permute-start | bytes 3145736 | tf_op jit(solution)/shard_map/ppermute | solution.py:49
  206.2 28.3 %all-to-all-start.2 = ((bf16[64,64,128]{2,1,0:T(8,128)(2,1)}), bf16[64,64,128]{2,1,0:T(8,128)(2,1)S(1)}, u32[]{:S(2)}, u32[]{:S(2)}) async-start(bf16[64,64,128]{2,1,0:T(8,128)(2,1)} %bitcast.11), calls=%async_computation.2 | async-start | bytes 2097152 | tf_op jit(solution)/shard_map/all_to_all | solution.py:53
Sparse Core Ops, SparseCore 0:
  11.7 81.6 all-gather.1

commit v6 on v5

--- a/solution.py
+++ b/solution.py
@@ -44,6 +44,32 @@
     return [[2 * chip + core for chip in range(size // 2)] for core in range(2)]
 
 
+LINE = 4
+
+
+def line_groups(size):
+    planes = size // 2 // LINE
+    return [
+        [2 * (plane * LINE + x) + core for x in range(LINE)]
+        for plane in range(planes)
+        for core in range(2)
+    ]
+
+
+def plane_groups(size):
+    planes = size // 2 // LINE
+    return [
+        [2 * (plane * LINE + x) + core for plane in range(planes)]
+        for x in range(LINE)
+        for core in range(2)
+    ]
+
+
+def line_first(place, chips):
+    planes = chips // LINE
+    return lax.rem(place, planes) * LINE + lax.div(place, planes)
+
+
 def swap_cores(block):
     size = lax.axis_size("fsdp")
     return lax.ppermute(block, "fsdp", [(i, i ^ 1) for i in range(size)])
@@ -122,15 +148,20 @@
     return ones_where(lax.broadcasted_iota(jnp.int32, (rows, count), 0) == source)
 
 
-def pick_core(rows, chips, per, core):
+def pick_core(rows, chips, per, core, lines=False):
     place = lax.broadcasted_iota(jnp.int32, (1, chips * per), 1)
     row, chip = lax.div(place, chips), lax.rem(place, chips)
+    if lines:
+        chip = line_first(chip, chips)
     source = (2 * chip + core) * per + row
     return ones_where(lax.broadcasted_iota(jnp.int32, (rows, chips * per), 0) == source)
 
 
-def pick_chip(rows, chips, per, core):
-    low = (2 * lax.broadcasted_iota(jnp.int32, (1, chips), 1) + core) * per
+def pick_chip(rows, chips, per, core, lines=False):
+    chip = lax.broadcasted_iota(jnp.int32, (1, chips), 1)
+    if lines:
+        chip = line_first(chip, chips)
+    low = (2 * chip + core) * per
     natural = lax.broadcasted_iota(jnp.int32, (rows, chips), 0)
     return ones_where((natural >= low) & (natural < low + per))
 
@@ -594,10 +625,11 @@
     stride = chunk + ODD
     for row in range(per * tiles + 1, chunk):
         loose[pl.ds(row, chips, stride=stride), :] = jnp.zeros((chips, LANES), F32)
-    for target, selector, parity in ((keep, selectors[0], core), (send, selectors[1], 1 - core)):
-        extra = dot(wide, pick_chip(width, chips, per, parity)) + dot(
-            narrow, pick_chip(head, chips, per_head, parity)
+    for target, parity in ((keep, core), (send, 1 - core)):
+        extra = dot(wide, pick_chip(width, chips, per, parity, lines=True)) + dot(
+            narrow, pick_chip(head, chips, per_head, parity, lines=True)
         )
+        selector = pick_core(width, chips, per, parity, lines=True)
         loose[pl.ds(per * tiles, chips, stride=stride), :] = jnp.transpose(extra)
         block = dot_tn(dot(attn_low, selector).astype(BF16), low[...])
         for row in range(per):
@@ -833,10 +865,22 @@
         ),
         specs=[SCALAR] + [WHOLE] * 13,
         flops=20e9,
+        vmem=62 * 1024 * 1024,
     )
     both = (keep.astype(F32) + swap_cores(send).astype(F32)).astype(BF16)
-    both, mlp_parts = lax.optimization_barrier((both, mlp_parts))
-    share_attn = jnp.sum(exchange(both.reshape(chips, chunk, LANES)).astype(F32), axis=0)
+    line = lax.psum_scatter(
+        both, "fsdp", scatter_dimension=0, axis_index_groups=line_groups(size), tiled=True
+    )
+    line, mlp_parts = lax.optimization_barrier((line, mlp_parts))
+    attn_parts = lax.all_to_all(
+        line.reshape(chips // LINE, chunk, LANES),
+        "fsdp",
+        split_axis=0,
+        concat_axis=0,
+        tiled=True,
+        axis_index_groups=plane_groups(size),
+    )
+    share_attn = jnp.sum(attn_parts.astype(F32), axis=0)
     share_qkv = share_attn[: shard * tiles].reshape(shard, tiles * LANES)
     share_gains = share_attn[shard * tiles, :gain_count]
 

time: 245 us -> 237 us (0.967)
  starting transfers between devices: 41 us -> 35.2 us
    all_to_all x3 -> x2, waiting for transfers between devices: 78.3 us -> 32.6 us  [exchange(): lax.all_to_all(blocks, 'fsdp', split_axis=0, concat_axis=0, tiled=True, a...]
    reduce_scatter x0 -> x1, waiting for transfers between devices: none -> 39.6 us  [on_device(): lax.psum_scatter(both, 'fsdp', scatter_dimension=0, axis_index_groups=lin...]
    all_to_all x3 -> x2, starting transfers between devices: 33.3 us -> 23.9 us  [exchange(): lax.all_to_all(blocks, 'fsdp', split_axis=0, concat_axis=0, tiled=True, a...]
    all_to_all x0 -> x1, waiting for transfers between devices: none -> 3.72 us  [on_device(): lax.all_to_all(line.reshape(chips // LINE, chunk, LANES), 'fsdp', split_a...]
    all_to_all x0 -> x1, starting transfers between devices: none -> 3.53 us  [on_device(): lax.all_to_all(line.reshape(chips // LINE, chunk, LANES), 'fsdp', split_a...]
  transfers between devices with their start and end apart: 11 -> 12, of which waited for: 8 -> 9; matrix products, arithmetic and copies ran while one was open for 6% -> 6% of each run, Pallas kernels for 13% -> 14%
where the time goes in v6:
time: 237 us; the launch traced here: 236 us
  waiting for transfers between devices  112 us (47%)
  Pallas kernels  53.6 us (23%)
  starting transfers between devices  35.2 us (15%)
  between operations  14.3 us (6%)
  other arithmetic  10.3 us (4%)
  local copies, waits for them, and re-layouts  10.2 us (4%)
    pallas_call x6, Pallas kernels, call(): pl.pallas_call(kernel, out_shape=outs, in_specs=specs, **{} if out_specs...  53.6 us
    reduce_scatter x1, waiting for transfers between devices, on_device(): lax.psum_scatter(both, 'fsdp', scatter_dimension=0, axis_index_groups=lin...  39.6 us
    all_to_all x2, waiting for transfers between devices, exchange(): lax.all_to_all(blocks, 'fsdp', split_axis=0, concat_axis=0, tiled=True, a...  32.6 us
    all_to_all x2, starting transfers between devices, exchange(): lax.all_to_all(blocks, 'fsdp', split_axis=0, concat_axis=0, tiled=True, a...  23.9 us
    all_gather x1, waiting for transfers between devices, on_device(): mlp_full = lax.all_gather(gathered, 'fsdp', axis=0, tiled=True)  22.3 us
    ppermute x4, waiting for transfers between devices, shifted(): return lax.ppermute(block, axis, route)  9.95 us
    ppermute x4, starting transfers between devices, shifted(): return lax.ppermute(block, axis, route)  7.33 us
  transfers between devices with their start and end apart: 12, of which 9 were waited for; matrix products, arithmetic and copies ran while one was open for 6% of the time, Pallas kernels for 14%

profile of v6, /device:TPU:0, one launch (start us, length us, event | category | flops | bytes accessed | tf_op | source)
XLA Modules:
  0.0 235.7 jit_solution(2837596641131320175)
XLA Ops:
  7.2 0.0 copy-start.1
  7.2 0.0 copy-start.2
  7.2 0.0 all-gather.2.cloned.1.call-start
  7.2 1.5 fusion.3
  8.8 0.0 all-gather.2.cloned.1.call-update
  8.8 0.7 pad_maximum_fusion
  9.6 0.8 pad_add_fusion
  10.4 1.3 broadcast_in_dim.73
  11.7 11.5 %all-to-all-start = ((bf16[64,64,128]{2,1,0:T(8,128)(2,1)}), bf16[64,64,128]{2,1,0:T(8,128)(2,1)S(1)}, u32[]{:S(2)}, u32[]{:S(2)}) async-start(bf16[64,64,128]{2,1,0:T(8,128)(2,1)} %broadcast_in_dim.73), calls=%async_computation | async-start | bytes 2097152 | tf_op jit(solution)/shard_map/all_to_all | solution.py:79
  23.2 19.7 %all-to-all-done = bf16[64,64,128]{2,1,0:T(8,128)(2,1)S(1)} async-done(((bf16[64,64,128]{2,1,0:T(8,128)(2,1)}), bf16[64,64,128]{2,1,0:T(8,128)(2,1)S(1)}, u32[]{:S(2)}, u32[]{:S(2)}) %all-to-all-start) | async-done | bytes 1048608 | tf_op jit(solution)/shard_map/all_to_all | solution.py:79
  43.0 0.0 collective-permute-start
  43.0 0.0 copy-done.1
  43.0 0.0 copy-done.2
  43.0 0.1 select_reduce_fusion.1
  43.1 0.1 fusion.4
  43.3 0.1 select_reduce_fusion
  43.4 1.3 multiply_sine_fusion
  44.6 1.0 collective-permute-done.peer
  45.6 0.0 copy-done
  45.6 1.0 copy-done.3
  46.6 6.4 %shard_map.246 = (f32[256,1536]{1,0:T(8,128)}, bf16[256,1024]{1,0:T(8,128)(2,1)}, bf16[256,512]{1,0:T(8,128)(2,1)}, f32[8,640]{1,0:T(8,128)}, f32[8,256]{1,0:T(8,128)}, /*index=5*/bf16[2,320,1536]{2,1,0:T(8,128)(2,1)}) custom-call(s32[1]{0:T(128)} %bitcast.core_ref, bf16[256,640]{1,0:T(8,128)(2,1)} %tok.3, bf16[4096,128]{1,0:T(8,128)(2,1)} %bitcast.40, ...), custom_call_target="tpu_custom_call" | custom-call | flops 4000000000 | bytes 8000000 | tf_op jit(solution)/shard_map/pallas_call | solution.py:95
  53.0 2.1 collective-permute-start.2
  55.1 2.7 %collective-permute-start.1 = (bf16[256,512]{1,0:T(8,128)(2,1)}, bf16[256,512]{1,0:T(8,128)(2,1)S(1)}, u32[]{:S(2)}, u32[]{:S(2)}) collective-permute-start(bf16[256,512]{1,0:T(8,128)(2,1)} %get-tuple-element.47.kv_own), channel_id=1, source_target_pairs={{0,2},{1,3},{2,4},{3,5},{4,6},{5,7},{6,8},{7,9},{8,10},{9,11},{10,... | collective-permute-start | bytes 786440 | tf_op jit(solution)/shard_map/ppermute | solution.py:19
  57.8 0.1 fusion.9
  57.9 0.6 select_n.54.k_seq
  58.5 0.8 copy.32.q_seq
  59.3 0.8 copy.33.live
  60.1 0.0 collective-permute-done.2.kv_near
  60.1 5.4 %collective-permute-done.1.kv_far = bf16[256,512]{1,0:T(8,128)(2,1)S(1)} collective-permute-done((bf16[256,512]{1,0:T(8,128)(2,1)}, bf16[256,512]{1,0:T(8,128)(2,1)S(1)}, u32[]{:S(2)}, u32[]{:S(2)}) %collective-permute-start.1) | collective-permute-done | bytes 262176 | tf_op jit(solution)/shard_map/ppermute | solution.py:19
  65.5 0.0 copy-done.4
  65.5 0.7 copy-done.5
  66.2 5.0 %shard_map.247 = (bf16[256,1024]{1,0:T(8,128)(2,1)}, f32[256,128]{1,0:T(8,128)}, bf16[640,1024]{1,0:T(8,128)(2,1)}, bf16[2,640,320]{2,1,0:T(8,128)(2,1)}) custom-call(s32[1]{0:T(128)} %bitcast.core_ref, bf16[256,1024]{1,0:T(8,128)(2,1)} %get-tuple-element.46.query_low, bf16[256,512]{1,0:T(8,128)(2,1)} %copy-done.5, bf16[256,512]{1,0:T(8,128)(2,1)} %copy-done.4, ...), custom_call_target="tpu_custom_call" | custom-call | flops 20000000000 | bytes 8000000 | tf_op jit(solution)/shard_map/pallas_call | solution.py:95
  71.2 22.3 %all-gather.2.cloned.1.call-done.full = bf16[1024,6016]{1,0:T(8,128)(2,1)} async-done(((bf16[8,6016]{1,0:T(8,128)(2,1)}), bf16[1024,6016]{1,0:T(8,128)(2,1)}) %all-gather.2.cloned.1.call-update) | async-done | bytes 12320784 | tf_op jit(solution)/shard_map/all_gather | solution.py:684
  93.5 20.8 %shard_map.248 = (f32[8,640]{1,0:T(8,128)}, bf16[256,640]{1,0:T(8,128)(2,1)}, f32[256,640]{1,0:T(8,128)}, bf16[256,1024]{1,0:T(8,128)(2,1)}, bf16[256,320]{1,0:T...) custom-call(s32[1]{0:T(128)} %bitcast.core_ref, ...), custom_call_target="tpu_custom_call" | custom-call | flops 12000000000 | bytes 8000000 | tf_op jit(solution)/shard_map/pallas_call | solution.py:95
  114.2 0.3 collective-permute-start.3
  114.6 6.1 %shard_map.249 = (f32[256,1024]{1,0:T(8,128)}, f32[256,512]{1,0:T(8,128)}, bf16[256,512]{1,0:T(8,128)(2,1)}, bf16[256,512]{1,0:T(8,128)(2,1)}) custom-call(bf16[256,1024]{1,0:T(8,128)(2,1)} %get-tuple-element.46.query_low, bf16[256,512]{1,0:T(8,128)(2,1)} %copy-done.5, bf16[256,512]{1,0:T(8,128)(2,1)} %copy-done.4, ...), custom_call_target="tpu_custom_call" | custom-call | flops 20000000000 | bytes 8000000 | tf_op jit(solution)/shard_map/pallas_call | solution.py:95
  120.7 1.3 collective-permute-start.4
  122.0 1.3 collective-permute-start.5
  123.3 0.0 collective-permute-done.3.arrived
  123.3 6.8 %shard_map.250 = bf16[8,8,288,128]{3,2,1,0:T(8,128)(2,1)} custom-call(bf16[256,320]{1,0:T(8,128)(2,1)} %get-tuple-element.57.low_own, bf16[256,4096]{1,0:T(8,128)(2,1)} %get-tuple-element.58.d_gate_up_in, bf16[8,8,80,128]{3,2,1,0:T(8,128)(2,1)} %get-tuple-element.59.own_down_in, bf16[8,8,48,128]{3,2,1,0:T(8,128)(2,1)} %get-tuple-element.60.own_out_in, ...), custom_call_target="tpu_custom_call" | custom-call | flops 12000000000 | bytes 8000000 | tf_op jit(solution)/shard_map/pallas_call | solution.py:95
  130.1 0.0 collective-permute-done.4.near
  130.1 0.0 copy-start.6
  130.2 4.5 %collective-permute-done.5.far = bf16[256,512]{1,0:T(8,128)(2,1)S(1)} collective-permute-done((bf16[256,512]{1,0:T(8,128)(2,1)}, bf16[256,512]{1,0:T(8,128)(2,1)S(1)}, u32[]{:S(2)}, u32[]{:S(2)}) %collective-permute-start.5) | collective-permute-done | bytes 262176 | tf_op jit(solution)/shard_map/ppermute | solution.py:19
  134.7 0.0 copy-done.6
  134.7 0.7 copy-done.7
  135.4 12.4 %all-to-all-start.1 = ((bf16[64,288,128]{2,1,0:T(8,128)(2,1)}), bf16[64,288,128]{2,1,0:T(8,128)(2,1)}, u32[]{:S(2)}, u32[]{:S(2)}) async-start(bf16[64,288,128]{2,1,0:T(8,128)(2,1)} %bitcast.38), calls=%async_computation.2 | async-start | bytes 9437184 | tf_op jit(solution)/shard_map/all_to_all | solution.py:79
  147.8 0.0 reduce-scatter.2.cloned.1.call-start
  147.8 8.5 %shard_map.251 = (bf16[256,640]{1,0:T(8,128)(2,1)}, bf16[4096,128]{1,0:T(8,128)(2,1)}, bf16[4096,128]{1,0:T(8,128)(2,1)}) custom-call(s32[1]{0:T(128)} %bitcast.core_ref, f32[256,1536]{1,0:T(8,128)} %get-tuple-element.52.raw, f32[256,1024]{1,0:T(8,128)} %get-tuple-element.55.d_query, f32[256,512]{1,0:T(8,128)} %get-tuple-element.56.d_own, ...), custom_call_target="tpu_custom_call" | custom-call | flops 20000000000 | bytes 8000000 | tf_op jit(solution)/shard_map/pallas_call | solution.py:95
  156.4 0.0 collective-permute-start.6
  156.4 2.9 %collective-permute-done.6 = bf16[4096,128]{1,0:T(8,128)(2,1)S(1)} collective-permute-done((bf16[4096,128]{1,0:T(8,128)(2,1)}, bf16[4096,128]{1,0:T(8,128)(2,1)S(1)}, u32[]{:S(2)}, u32[]{:S(2)}) %collective-permute-start.6) | collective-permute-done | bytes 1048608 | tf_op jit(solution)/shard_map/ppermute | solution.py:75
  159.3 2.5 %add_convert_fusion = bf16[4096,128]{1,0:T(8,128)(2,1)} fusion(bf16[4096,128]{1,0:T(8,128)(2,1)S(1)} %collective-permute-done.6, bf16[4096,128]{1,0:T(8,128)(2,1)} %get-tuple-element.72), kind=kLoop, calls=%fused_computation.1 | loop fusion | flops 2097152 | bytes 3145728 | tf_op jit(solution)/shard_map/convert_element_type | solution.py:870
  161.7 0.0 reduce-scatter.2.cloned.1.call-update
  161.7 39.6 %reduce-scatter.2.cloned.1.call-done = bf16[1024,128]{1,0:T(8,128)(2,1)} async-done(((bf16[4096,128]{1,0:T(8,128)(2,1)}), bf16[1024,128]{1,0:T(8,128)(2,1)}) %reduce-scatter.2.cloned.1.call-update) | async-done | bytes 262160 | tf_op jit(solution)/shard_map/reduce_scatter | solution.py:871
  201.4 12.9 %all-to-all-done.1 = bf16[64,288,128]{2,1,0:T(8,128)(2,1)} async-done(((bf16[64,288,128]{2,1,0:T(8,128)(2,1)}), bf16[64,288,128]{2,1,0:T(8,128)(2,1)}, u32[]{:S(2)}, u32[]{:S(2)}) %all-to-all-start.1) | async-done | bytes 4718624 | tf_op jit(solution)/shard_map/all_to_all | solution.py:79
  214.2 3.5 %all-to-all-start.2 = ((bf16[16,64,128]{2,1,0:T(8,128)(2,1)}), bf16[16,64,128]{2,1,0:T(8,128)(2,1)S(1)}, u32[]{:S(2)}, u32[]{:S(2)}) async-start(bf16[16,64,128]{2,1,0:T(8,128)(2,1)} %bitcast.41), calls=%async_computation.3 | async-start | bytes 524288 | tf_op jit(solution)/shard_map/all_to_all | solution.py:875
  217.8 3.0 %convert_reduce_fusion = f32[288,128]{1,0:T(8,128)S(1)} fusion(bf16[64,288,128]{2,1,0:T(8,128)(2,1)} %all-to-all-done.1), kind=kLoop, calls=%fused_computation | loop fusion | flops 4681728 | bytes 4866048 | tf_op jit(solution)/shard_map/reduce_sum | solution.py:887
  220.8 0.6 copy.38
  221.4 0.7 reshape.127
  222.1 0.6 slice_bitcast_fusion
  222.7 3.7 %all-to-all-done.2 = bf16[16,64,128]{2,1,0:T(8,128)(2,1)S(1)} async-done(((bf16[16,64,128]{2,1,0:T(8,128)(2,1)}), bf16[16,64,128]{2,1,0:T(8,128)(2,1)S(1)}, u32[]{:S(2)}, u32[]{:S(2)}) %all-to-all-start.2) | async-done | bytes 262176 | tf_op jit(solution)/shard_map/all_to_all | solution.py:875
  226.5 0.6 slice_bitcast_fusion.1
  227.1 0.6 slice_bitcast_fusion.3
  227.7 0.6 slice.83
  228.3 0.6 slice.82
  (18 shorter events, 0.2 us)
Async XLA Ops:
  7.2 35.8 %copy-start.1 = (s32[25]{0:T(128)S(1)}, s32[25]{0:T(128)}, u32[]{:S(2)}) copy-start(s32[25]{0:T(128)} %param.18) | copy-start | bytes 304
  7.2 35.8 %copy-start.2 = (s32[25]{0:T(128)S(1)}, s32[25]{0:T(128)}, u32[]{:S(2)}) copy-start(s32[25]{0:T(128)} %param.17) | copy-start | bytes 304
  7.2 86.3 %all-gather.2.cloned.1.call-start = ((), (), s32[]{:S(2)}) async-start(), calls=%async_computation.4 | async-start | bytes 12417024 | tf_op jit(solution)/shard_map/all_gather | solution.py:684
  11.7 31.2 %all-to-all-start = ((bf16[64,64,128]{2,1,0:T(8,128)(2,1)}), bf16[64,64,128]{2,1,0:T(8,128)(2,1)S(1)}, u32[]{:S(2)}, u32[]{:S(2)}) async-start(bf16[64,64,128]{2,1,0:T(8,128)(2,1)} %broadcast_in_dim.73), calls=%async_computation | async-start | bytes 2097152 | tf_op jit(solution)/shard_map/all_to_all | solution.py:79
  43.0 2.7 %copy-start = (bf16[64,64,128]{2,1,0:T(8,128)(2,1)}, bf16[64,64,128]{2,1,0:T(8,128)(2,1)S(1)}, u32[]{:S(2)}) copy-start(bf16[64,64,128]{2,1,0:T(8,128)(2,1)S(1)} %all-to-all-done) | copy-start | bytes 3145732
  43.0 2.7 %collective-permute-start = (bf16[4096,128]{1,0:T(8,128)(2,1)S(1)}, bf16[4096,128]{1,0:T(8,128)(2,1)S(1)}, u32[]{:S(2)}, u32[]{:S(2)}) collective-permute-start(bf16[4096,128]{1,0:T(8,128)(2,1)S(1)} %bitcast.39), channel_id=1, source_target_pairs={{0,1},{1,0},{2,3},{3,2},{4,5},{5,4},{6,7},{7,6},{8,9},{9,8},{10,11... | collective-permute-start | bytes 3145736 | tf_op jit(solution)/shard_map/ppermute | solution.py:75
  45.6 1.0 copy-start.3
  53.0 7.1 %collective-permute-start.2 = (bf16[256,512]{1,0:T(8,128)(2,1)}, bf16[256,512]{1,0:T(8,128)(2,1)S(1)}, u32[]{:S(2)}, u32[]{:S(2)}) collective-permute-start(bf16[256,512]{1,0:T(8,128)(2,1)} %get-tuple-element.47.kv_own), channel_id=1, source_target_pairs={{0,1},{1,2},{2,3},{3,4},{4,5},{5,6},{6,7},{7,8},{8,9},{9,10},{10,1... | collective-permute-start | bytes 786440 | tf_op jit(solution)/shard_map/ppermute | solution.py:19
  55.1 10.4 %collective-permute-start.1 = (bf16[256,512]{1,0:T(8,128)(2,1)}, bf16[256,512]{1,0:T(8,128)(2,1)S(1)}, u32[]{:S(2)}, u32[]{:S(2)}) collective-permute-start(bf16[256,512]{1,0:T(8,128)(2,1)} %get-tuple-element.47.kv_own), channel_id=1, source_target_pairs={{0,2},{1,3},{2,4},{3,5},{4,6},{5,7},{6,8},{7,9},{8,10},{9,11},{10,... | collective-permute-start | bytes 786440 | tf_op jit(solution)/shard_map/ppermute | solution.py:19
  60.1 5.4 %copy-start.4 = (bf16[256,512]{1,0:T(8,128)(2,1)}, bf16[256,512]{1,0:T(8,128)(2,1)S(1)}, u32[]{:S(2)}) copy-start(bf16[256,512]{1,0:T(8,128)(2,1)S(1)} %collective-permute-done.2.kv_near) | copy-start | bytes 786436
  65.5 0.7 copy-start.5
  114.2 9.1 %collective-permute-start.3 = (bf16[8,8,288,128]{3,2,1,0:T(8,128)(2,1)}, bf16[8,8,288,128]{3,2,1,0:T(8,128)(2,1)}, u32[]{:S(2)}, u32[]{:S(2)}) collective-permute-start(bf16[8,8,288,128]{3,2,1,0:T(8,128)(2,1)} %get-tuple-element.61), channel_id=1, source_target_pairs={{0,1},{1,0},{2,3},{3,2},{4,5},{5,4},{6,7},{7,6},{8,9},{9,8},{10,11... | collective-permute-start | bytes 14155784 | tf_op jit(solution)/shard_map/ppermute | solution.py:75
  120.7 9.4 %collective-permute-start.4 = (bf16[256,512]{1,0:T(8,128)(2,1)}, bf16[256,512]{1,0:T(8,128)(2,1)S(1)}, u32[]{:S(2)}, u32[]{:S(2)}) collective-permute-start(bf16[256,512]{1,0:T(8,128)(2,1)} %get-tuple-element.64), channel_id=1, source_target_pairs={{1,0},{2,1},{3,2},{4,3},{5,4},{6,5},{7,6},{8,7},{9,8},{10,9},{11,1... | collective-permute-start | bytes 786440 | tf_op jit(solution)/shard_map/ppermute | solution.py:19
  122.0 12.6 %collective-permute-start.5 = (bf16[256,512]{1,0:T(8,128)(2,1)}, bf16[256,512]{1,0:T(8,128)(2,1)S(1)}, u32[]{:S(2)}, u32[]{:S(2)}) collective-permute-start(bf16[256,512]{1,0:T(8,128)(2,1)} %get-tuple-element.62), channel_id=1, source_target_pairs={{2,0},{3,1},{4,2},{5,3},{6,4},{7,5},{8,6},{9,7},{10,8},{11,9},{12,... | collective-permute-start | bytes 786440 | tf_op jit(solution)/shard_map/ppermute | solution.py:19
  130.1 4.5 %copy-start.6 = (bf16[256,512]{1,0:T(8,128)(2,1)}, bf16[256,512]{1,0:T(8,128)(2,1)S(1)}, u32[]{:S(2)}) copy-start(bf16[256,512]{1,0:T(8,128)(2,1)S(1)} %collective-permute-done.4.near) | copy-start | bytes 786436
  134.7 0.7 copy-start.7
  135.4 78.9 %all-to-all-start.1 = ((bf16[64,288,128]{2,1,0:T(8,128)(2,1)}), bf16[64,288,128]{2,1,0:T(8,128)(2,1)}, u32[]{:S(2)}, u32[]{:S(2)}) async-start(bf16[64,288,128]{2,1,0:T(8,128)(2,1)} %bitcast.38), calls=%async_computation.2 | async-start | bytes 9437184 | tf_op jit(solution)/shard_map/all_to_all | solution.py:79
  147.8 53.6 %reduce-scatter.2.cloned.1.call-start = ((), (), s32[]{:S(2)}) async-start(), calls=%async_computation.5 | async-start | bytes 1310720 | tf_op jit(solution)/shard_map/reduce_scatter | solution.py:871
  156.4 2.9 %collective-permute-start.6 = (bf16[4096,128]{1,0:T(8,128)(2,1)}, bf16[4096,128]{1,0:T(8,128)(2,1)S(1)}, u32[]{:S(2)}, u32[]{:S(2)}) collective-permute-start(bf16[4096,128]{1,0:T(8,128)(2,1)} %get-tuple-element.73), channel_id=1, source_target_pairs={{0,1},{1,0},{2,3},{3,2},{4,5},{5,4},{6,7},{7,6},{8,9},{9,8},{10,11... | collective-permute-start | bytes 3145736 | tf_op jit(solution)/shard_map/ppermute | solution.py:75
  214.2 12.2 %all-to-all-start.2 = ((bf16[16,64,128]{2,1,0:T(8,128)(2,1)}), bf16[16,64,128]{2,1,0:T(8,128)(2,1)S(1)}, u32[]{:S(2)}, u32[]{:S(2)}) async-start(bf16[16,64,128]{2,1,0:T(8,128)(2,1)} %bitcast.41), calls=%async_computation.3 | async-start | bytes 524288 | tf_op jit(solution)/shard_map/all_to_all | solution.py:875
Sparse Core Ops, SparseCore 0:
  11.7 81.6 all-gather.1
  161.9 39.4 reduce-scatter.1

commit v7 on v6

--- a/solution.py
+++ b/solution.py
@@ -467,6 +467,10 @@
             ]
 
 
+def loose_rows(chips, chunk):
+    return -(-(chips + 1) * (chunk + ODD) // SLOTS) * SLOTS
+
+
 def loose_chunk(loose, chip, chunk):
     return loose[pl.ds(chip * (chunk + ODD), chunk), :]
 
@@ -724,7 +728,7 @@
             shape((2, chips * shard, qkv_cols), BF16),
         ),
         (core_arg, tokens, own, peer, cos_vals, sin_vals),
-        scratch=(pltpu.VMEM((chips * (chunk + ODD), LANES), F32),),
+        scratch=(pltpu.VMEM((loose_rows(chips, chunk), LANES), F32),),
         specs=[SCALAR] + [WHOLE] * 5,
     )
     kv_near = shifted(own_kv, "fsdp", 1)
@@ -779,7 +783,7 @@
             pltpu.VMEM((tok_rows, width), BF16),
             pltpu.VMEM((width // 2, tok_rows), BF16),
             pltpu.VMEM((tok_rows, width), BF16),
-            pltpu.VMEM((chips * (down_at + ODD), LANES), F32),
+            pltpu.VMEM((loose_rows(chips, down_at), LANES), F32),
             pltpu.VMEM((blocks, strips, 2, SLOTS, width), F32),
             pltpu.VMEM((tile // (2 * down_rows) // strips, strips, 2, down_rows, width), BF16),
             pltpu.VMEM((width, size * SLOTS), BF16),
@@ -835,7 +839,7 @@
             pltpu.VMEM((blocks, strips, out_at - down_at, LANES), BF16),
             pltpu.VMEM((blocks, strips, 6 * SLOTS, LANES), BF16),
             pltpu.VMEM((width // 2, tok_rows), BF16),
-            pltpu.VMEM((chips * (down_at + ODD), LANES), F32),
+            pltpu.VMEM((loose_rows(chips, down_at), LANES), F32),
             pltpu.SemaphoreType.DMA((gu_cols // tile,)),
             pltpu.SemaphoreType.DMA((2,)),
             pltpu.SemaphoreType.DMA((blocks,)),
@@ -861,7 +865,7 @@
         ),
         scratch=(
             pltpu.VMEM((tok_rows, qkv_cols), BF16),
-            pltpu.VMEM((chips * (chunk + ODD), LANES), F32),
+            pltpu.VMEM((loose_rows(chips, chunk), LANES), F32),
         ),
         specs=[SCALAR] + [WHOLE] * 13,
         flops=20e9,

time: 237 us -> 237 us (level)
  no operation moved by 1% of the time
where the time goes in v7:
time: 237 us; the launch traced here: 236 us
  waiting for transfers between devices  112 us (47%)
  Pallas kernels  53.6 us (23%)
  starting transfers between devices  35.2 us (15%)
  between operations  14.3 us (6%)
  other arithmetic  10.3 us (4%)
  local copies, waits for them, and re-layouts  10.2 us (4%)
    pallas_call x6, Pallas kernels, call(): pl.pallas_call(kernel, out_shape=outs, in_specs=specs, **{} if out_specs...  53.6 us
    reduce_scatter x1, waiting for transfers between devices, on_device(): lax.psum_scatter(both, 'fsdp', scatter_dimension=0, axis_index_groups=lin...  39.6 us
    all_to_all x2, waiting for transfers between devices, exchange(): lax.all_to_all(blocks, 'fsdp', split_axis=0, concat_axis=0, tiled=True, a...  32.6 us
    all_to_all x2, starting transfers between devices, exchange(): lax.all_to_all(blocks, 'fsdp', split_axis=0, concat_axis=0, tiled=True, a...  23.9 us
    all_gather x1, waiting for transfers between devices, on_device(): mlp_full = lax.all_gather(gathered, 'fsdp', axis=0, tiled=True)  22.3 us
    ppermute x4, waiting for transfers between devices, shifted(): return lax.ppermute(block, axis, route)  9.96 us
    ppermute x4, starting transfers between devices, shifted(): return lax.ppermute(block, axis, route)  7.33 us
  transfers between devices with their start and end apart: 12, of which 9 were waited for; matrix products, arithmetic and copies ran while one was open for 6% of the time, Pallas kernels for 14%

profile of v7, /device:TPU:0, one launch (start us, length us, event | category | flops | bytes accessed | tf_op | source)
XLA Modules:
  0.0 235.8 jit_solution(443220888451379020)
XLA Ops:
  7.2 0.0 copy-start.1
  7.2 0.0 copy-start.2
  7.2 0.0 all-gather.2.cloned.1.call-start
  7.2 1.5 fusion.3
  8.8 0.0 all-gather.2.cloned.1.call-update
  8.8 0.7 pad_maximum_fusion
  9.6 0.8 pad_add_fusion
  10.4 1.3 broadcast_in_dim.73
  11.7 11.5 %all-to-all-start = ((bf16[64,64,128]{2,1,0:T(8,128)(2,1)}), bf16[64,64,128]{2,1,0:T(8,128)(2,1)S(1)}, u32[]{:S(2)}, u32[]{:S(2)}) async-start(bf16[64,64,128]{2,1,0:T(8,128)(2,1)} %broadcast_in_dim.73), calls=%async_computation | async-start | bytes 2097152 | tf_op jit(solution)/shard_map/all_to_all | solution.py:79
  23.2 19.7 %all-to-all-done = bf16[64,64,128]{2,1,0:T(8,128)(2,1)S(1)} async-done(((bf16[64,64,128]{2,1,0:T(8,128)(2,1)}), bf16[64,64,128]{2,1,0:T(8,128)(2,1)S(1)}, u32[]{:S(2)}, u32[]{:S(2)}) %all-to-all-start) | async-done | bytes 1048608 | tf_op jit(solution)/shard_map/all_to_all | solution.py:79
  43.0 0.0 collective-permute-start
  43.0 0.0 copy-done.1
  43.0 0.0 copy-done.2
  43.0 0.1 select_reduce_fusion.1
  43.1 0.1 fusion.4
  43.3 0.1 select_reduce_fusion
  43.4 1.3 multiply_sine_fusion
  44.6 1.0 collective-permute-done.peer
  45.6 0.0 copy-done
  45.6 1.0 copy-done.3
  46.6 6.4 %shard_map.246 = (f32[256,1536]{1,0:T(8,128)}, bf16[256,1024]{1,0:T(8,128)(2,1)}, bf16[256,512]{1,0:T(8,128)(2,1)}, f32[8,640]{1,0:T(8,128)}, f32[8,256]{1,0:T(8,128)}, /*index=5*/bf16[2,320,1536]{2,1,0:T(8,128)(2,1)}) custom-call(s32[1]{0:T(128)} %bitcast.core_ref, bf16[256,640]{1,0:T(8,128)(2,1)} %tok.3, bf16[4096,128]{1,0:T(8,128)(2,1)} %bitcast.40, ...), custom_call_target="tpu_custom_call" | custom-call | flops 4000000000 | bytes 8000000 | tf_op jit(solution)/shard_map/pallas_call | solution.py:95
  53.0 2.1 collective-permute-start.2
  55.0 2.7 %collective-permute-start.1 = (bf16[256,512]{1,0:T(8,128)(2,1)}, bf16[256,512]{1,0:T(8,128)(2,1)S(1)}, u32[]{:S(2)}, u32[]{:S(2)}) collective-permute-start(bf16[256,512]{1,0:T(8,128)(2,1)} %get-tuple-element.47.kv_own), channel_id=1, source_target_pairs={{0,2},{1,3},{2,4},{3,5},{4,6},{5,7},{6,8},{7,9},{8,10},{9,11},{10,... | collective-permute-start | bytes 786440 | tf_op jit(solution)/shard_map/ppermute | solution.py:19
  57.7 0.1 fusion.9
  57.9 0.6 select_n.54.k_seq
  58.4 0.8 copy.32.q_seq
  59.2 0.8 copy.33.live
  60.0 0.0 collective-permute-done.2.kv_near
  60.0 5.5 %collective-permute-done.1.kv_far = bf16[256,512]{1,0:T(8,128)(2,1)S(1)} collective-permute-done((bf16[256,512]{1,0:T(8,128)(2,1)}, bf16[256,512]{1,0:T(8,128)(2,1)S(1)}, u32[]{:S(2)}, u32[]{:S(2)}) %collective-permute-start.1) | collective-permute-done | bytes 262176 | tf_op jit(solution)/shard_map/ppermute | solution.py:19
  65.5 0.0 copy-done.4
  65.5 0.7 copy-done.5
  66.2 5.0 %shard_map.247 = (bf16[256,1024]{1,0:T(8,128)(2,1)}, f32[256,128]{1,0:T(8,128)}, bf16[640,1024]{1,0:T(8,128)(2,1)}, bf16[2,640,320]{2,1,0:T(8,128)(2,1)}) custom-call(s32[1]{0:T(128)} %bitcast.core_ref, bf16[256,1024]{1,0:T(8,128)(2,1)} %get-tuple-element.46.query_low, bf16[256,512]{1,0:T(8,128)(2,1)} %copy-done.5, bf16[256,512]{1,0:T(8,128)(2,1)} %copy-done.4, ...), custom_call_target="tpu_custom_call" | custom-call | flops 20000000000 | bytes 8000000 | tf_op jit(solution)/shard_map/pallas_call | solution.py:95
  71.2 22.3 %all-gather.2.cloned.1.call-done.full = bf16[1024,6016]{1,0:T(8,128)(2,1)} async-done(((bf16[8,6016]{1,0:T(8,128)(2,1)}), bf16[1024,6016]{1,0:T(8,128)(2,1)}) %all-gather.2.cloned.1.call-update) | async-done | bytes 12320784 | tf_op jit(solution)/shard_map/all_gather | solution.py:688
  93.5 20.8 %shard_map.248 = (f32[8,640]{1,0:T(8,128)}, bf16[256,640]{1,0:T(8,128)(2,1)}, f32[256,640]{1,0:T(8,128)}, bf16[256,1024]{1,0:T(8,128)(2,1)}, bf16[256,320]{1,0:T...) custom-call(s32[1]{0:T(128)} %bitcast.core_ref, ...), custom_call_target="tpu_custom_call" | custom-call | flops 12000000000 | bytes 8000000 | tf_op jit(solution)/shard_map/pallas_call | solution.py:95
  114.3 0.3 collective-permute-start.3
  114.6 6.1 %shard_map.249 = (f32[256,1024]{1,0:T(8,128)}, f32[256,512]{1,0:T(8,128)}, bf16[256,512]{1,0:T(8,128)(2,1)}, bf16[256,512]{1,0:T(8,128)(2,1)}) custom-call(bf16[256,1024]{1,0:T(8,128)(2,1)} %get-tuple-element.46.query_low, bf16[256,512]{1,0:T(8,128)(2,1)} %copy-done.5, bf16[256,512]{1,0:T(8,128)(2,1)} %copy-done.4, ...), custom_call_target="tpu_custom_call" | custom-call | flops 20000000000 | bytes 8000000 | tf_op jit(solution)/shard_map/pallas_call | solution.py:95
  120.8 1.3 collective-permute-start.4
  122.0 1.3 collective-permute-start.5
  123.3 0.0 collective-permute-done.3.arrived
  123.3 6.8 %shard_map.250 = bf16[8,8,288,128]{3,2,1,0:T(8,128)(2,1)} custom-call(bf16[256,320]{1,0:T(8,128)(2,1)} %get-tuple-element.57.low_own, bf16[256,4096]{1,0:T(8,128)(2,1)} %get-tuple-element.58.d_gate_up_in, bf16[8,8,80,128]{3,2,1,0:T(8,128)(2,1)} %get-tuple-element.59.own_down_in, bf16[8,8,48,128]{3,2,1,0:T(8,128)(2,1)} %get-tuple-element.60.own_out_in, ...), custom_call_target="tpu_custom_call" | custom-call | flops 12000000000 | bytes 8000000 | tf_op jit(solution)/shard_map/pallas_call | solution.py:95
  130.2 0.0 collective-permute-done.4.near
  130.2 0.0 copy-start.6
  130.2 4.5 %collective-permute-done.5.far = bf16[256,512]{1,0:T(8,128)(2,1)S(1)} collective-permute-done((bf16[256,512]{1,0:T(8,128)(2,1)}, bf16[256,512]{1,0:T(8,128)(2,1)S(1)}, u32[]{:S(2)}, u32[]{:S(2)}) %collective-permute-start.5) | collective-permute-done | bytes 262176 | tf_op jit(solution)/shard_map/ppermute | solution.py:19
  134.7 0.0 copy-done.6
  134.7 0.7 copy-done.7
  135.4 12.4 %all-to-all-start.1 = ((bf16[64,288,128]{2,1,0:T(8,128)(2,1)}), bf16[64,288,128]{2,1,0:T(8,128)(2,1)}, u32[]{:S(2)}, u32[]{:S(2)}) async-start(bf16[64,288,128]{2,1,0:T(8,128)(2,1)} %bitcast.38), calls=%async_computation.2 | async-start | bytes 9437184 | tf_op jit(solution)/shard_map/all_to_all | solution.py:79
  147.8 0.0 reduce-scatter.2.cloned.1.call-start
  147.9 8.5 %shard_map.251 = (bf16[256,640]{1,0:T(8,128)(2,1)}, bf16[4096,128]{1,0:T(8,128)(2,1)}, bf16[4096,128]{1,0:T(8,128)(2,1)}) custom-call(s32[1]{0:T(128)} %bitcast.core_ref, f32[256,1536]{1,0:T(8,128)} %get-tuple-element.52.raw, f32[256,1024]{1,0:T(8,128)} %get-tuple-element.55.d_query, f32[256,512]{1,0:T(8,128)} %get-tuple-element.56.d_own, ...), custom_call_target="tpu_custom_call" | custom-call | flops 20000000000 | bytes 8000000 | tf_op jit(solution)/shard_map/pallas_call | solution.py:95
  156.4 0.0 collective-permute-start.6
  156.4 2.9 %collective-permute-done.6 = bf16[4096,128]{1,0:T(8,128)(2,1)S(1)} collective-permute-done((bf16[4096,128]{1,0:T(8,128)(2,1)}, bf16[4096,128]{1,0:T(8,128)(2,1)S(1)}, u32[]{:S(2)}, u32[]{:S(2)}) %collective-permute-start.6) | collective-permute-done | bytes 1048608 | tf_op jit(solution)/shard_map/ppermute | solution.py:75
  159.3 2.5 %add_convert_fusion = bf16[4096,128]{1,0:T(8,128)(2,1)} fusion(bf16[4096,128]{1,0:T(8,128)(2,1)S(1)} %collective-permute-done.6, bf16[4096,128]{1,0:T(8,128)(2,1)} %get-tuple-element.72), kind=kLoop, calls=%fused_computation.1 | loop fusion | flops 2097152 | bytes 3145728 | tf_op jit(solution)/shard_map/convert_element_type | solution.py:874
  161.8 0.0 reduce-scatter.2.cloned.1.call-update
  161.8 39.6 %reduce-scatter.2.cloned.1.call-done = bf16[1024,128]{1,0:T(8,128)(2,1)} async-done(((bf16[4096,128]{1,0:T(8,128)(2,1)}), bf16[1024,128]{1,0:T(8,128)(2,1)}) %reduce-scatter.2.cloned.1.call-update) | async-done | bytes 262160 | tf_op jit(solution)/shard_map/reduce_scatter | solution.py:875
  201.4 12.8 %all-to-all-done.1 = bf16[64,288,128]{2,1,0:T(8,128)(2,1)} async-done(((bf16[64,288,128]{2,1,0:T(8,128)(2,1)}), bf16[64,288,128]{2,1,0:T(8,128)(2,1)}, u32[]{:S(2)}, u32[]{:S(2)}) %all-to-all-start.1) | async-done | bytes 4718624 | tf_op jit(solution)/shard_map/all_to_all | solution.py:79
  214.3 3.5 %all-to-all-start.2 = ((bf16[16,64,128]{2,1,0:T(8,128)(2,1)}), bf16[16,64,128]{2,1,0:T(8,128)(2,1)S(1)}, u32[]{:S(2)}, u32[]{:S(2)}) async-start(bf16[16,64,128]{2,1,0:T(8,128)(2,1)} %bitcast.41), calls=%async_computation.3 | async-start | bytes 524288 | tf_op jit(solution)/shard_map/all_to_all | solution.py:879
  217.8 3.0 %convert_reduce_fusion = f32[288,128]{1,0:T(8,128)S(1)} fusion(bf16[64,288,128]{2,1,0:T(8,128)(2,1)} %all-to-all-done.1), kind=kLoop, calls=%fused_computation | loop fusion | flops 4681728 | bytes 4866048 | tf_op jit(solution)/shard_map/reduce_sum | solution.py:891
  220.8 0.6 copy.38
  221.5 0.7 reshape.127
  222.1 0.6 slice_bitcast_fusion
  222.7 3.7 %all-to-all-done.2 = bf16[16,64,128]{2,1,0:T(8,128)(2,1)S(1)} async-done(((bf16[16,64,128]{2,1,0:T(8,128)(2,1)}), bf16[16,64,128]{2,1,0:T(8,128)(2,1)S(1)}, u32[]{:S(2)}, u32[]{:S(2)}) %all-to-all-start.2) | async-done | bytes 262176 | tf_op jit(solution)/shard_map/all_to_all | solution.py:879
  226.5 0.6 slice_bitcast_fusion.1
  227.1 0.6 slice_bitcast_fusion.3
  227.7 0.6 slice.83
  228.3 0.6 slice.82
  (18 shorter events, 0.2 us)
Async XLA Ops:
  7.2 35.8 %copy-start.1 = (s32[25]{0:T(128)S(1)}, s32[25]{0:T(128)}, u32[]{:S(2)}) copy-start(s32[25]{0:T(128)} %param.18) | copy-start | bytes 304
  7.2 35.8 %copy-start.2 = (s32[25]{0:T(128)S(1)}, s32[25]{0:T(128)}, u32[]{:S(2)}) copy-start(s32[25]{0:T(128)} %param.17) | copy-start | bytes 304
  7.2 86.3 %all-gather.2.cloned.1.call-start = ((), (), s32[]{:S(2)}) async-start(), calls=%async_computation.4 | async-start | bytes 12417024 | tf_op jit(solution)/shard_map/all_gather | solution.py:688
  11.7 31.2 %all-to-all-start = ((bf16[64,64,128]{2,1,0:T(8,128)(2,1)}), bf16[64,64,128]{2,1,0:T(8,128)(2,1)S(1)}, u32[]{:S(2)}, u32[]{:S(2)}) async-start(bf16[64,64,128]{2,1,0:T(8,128)(2,1)} %broadcast_in_dim.73), calls=%async_computation | async-start | bytes 2097152 | tf_op jit(solution)/shard_map/all_to_all | solution.py:79
  43.0 2.7 %copy-start = (bf16[64,64,128]{2,1,0:T(8,128)(2,1)}, bf16[64,64,128]{2,1,0:T(8,128)(2,1)S(1)}, u32[]{:S(2)}) copy-start(bf16[64,64,128]{2,1,0:T(8,128)(2,1)S(1)} %all-to-all-done) | copy-start | bytes 3145732
  43.0 2.7 %collective-permute-start = (bf16[4096,128]{1,0:T(8,128)(2,1)S(1)}, bf16[4096,128]{1,0:T(8,128)(2,1)S(1)}, u32[]{:S(2)}, u32[]{:S(2)}) collective-permute-start(bf16[4096,128]{1,0:T(8,128)(2,1)S(1)} %bitcast.39), channel_id=1, source_target_pairs={{0,1},{1,0},{2,3},{3,2},{4,5},{5,4},{6,7},{7,6},{8,9},{9,8},{10,11... | collective-permute-start | bytes 3145736 | tf_op jit(solution)/shard_map/ppermute | solution.py:75
  45.6 1.0 copy-start.3
  53.0 7.1 %collective-permute-start.2 = (bf16[256,512]{1,0:T(8,128)(2,1)}, bf16[256,512]{1,0:T(8,128)(2,1)S(1)}, u32[]{:S(2)}, u32[]{:S(2)}) collective-permute-start(bf16[256,512]{1,0:T(8,128)(2,1)} %get-tuple-element.47.kv_own), channel_id=1, source_target_pairs={{0,1},{1,2},{2,3},{3,4},{4,5},{5,6},{6,7},{7,8},{8,9},{9,10},{10,1... | collective-permute-start | bytes 786440 | tf_op jit(solution)/shard_map/ppermute | solution.py:19
  55.0 10.5 %collective-permute-start.1 = (bf16[256,512]{1,0:T(8,128)(2,1)}, bf16[256,512]{1,0:T(8,128)(2,1)S(1)}, u32[]{:S(2)}, u32[]{:S(2)}) collective-permute-start(bf16[256,512]{1,0:T(8,128)(2,1)} %get-tuple-element.47.kv_own), channel_id=1, source_target_pairs={{0,2},{1,3},{2,4},{3,5},{4,6},{5,7},{6,8},{7,9},{8,10},{9,11},{10,... | collective-permute-start | bytes 786440 | tf_op jit(solution)/shard_map/ppermute | solution.py:19
  60.0 5.5 %copy-start.4 = (bf16[256,512]{1,0:T(8,128)(2,1)}, bf16[256,512]{1,0:T(8,128)(2,1)S(1)}, u32[]{:S(2)}) copy-start(bf16[256,512]{1,0:T(8,128)(2,1)S(1)} %collective-permute-done.2.kv_near) | copy-start | bytes 786436
  65.5 0.7 copy-start.5
  114.3 9.1 %collective-permute-start.3 = (bf16[8,8,288,128]{3,2,1,0:T(8,128)(2,1)}, bf16[8,8,288,128]{3,2,1,0:T(8,128)(2,1)}, u32[]{:S(2)}, u32[]{:S(2)}) collective-permute-start(bf16[8,8,288,128]{3,2,1,0:T(8,128)(2,1)} %get-tuple-element.61), channel_id=1, source_target_pairs={{0,1},{1,0},{2,3},{3,2},{4,5},{5,4},{6,7},{7,6},{8,9},{9,8},{10,11... | collective-permute-start | bytes 14155784 | tf_op jit(solution)/shard_map/ppermute | solution.py:75
  120.8 9.4 %collective-permute-start.4 = (bf16[256,512]{1,0:T(8,128)(2,1)}, bf16[256,512]{1,0:T(8,128)(2,1)S(1)}, u32[]{:S(2)}, u32[]{:S(2)}) collective-permute-start(bf16[256,512]{1,0:T(8,128)(2,1)} %get-tuple-element.64), channel_id=1, source_target_pairs={{1,0},{2,1},{3,2},{4,3},{5,4},{6,5},{7,6},{8,7},{9,8},{10,9},{11,1... | collective-permute-start | bytes 786440 | tf_op jit(solution)/shard_map/ppermute | solution.py:19
  122.0 12.6 %collective-permute-start.5 = (bf16[256,512]{1,0:T(8,128)(2,1)}, bf16[256,512]{1,0:T(8,128)(2,1)S(1)}, u32[]{:S(2)}, u32[]{:S(2)}) collective-permute-start(bf16[256,512]{1,0:T(8,128)(2,1)} %get-tuple-element.62), channel_id=1, source_target_pairs={{2,0},{3,1},{4,2},{5,3},{6,4},{7,5},{8,6},{9,7},{10,8},{11,9},{12,... | collective-permute-start | bytes 786440 | tf_op jit(solution)/shard_map/ppermute | solution.py:19
  130.2 4.5 %copy-start.6 = (bf16[256,512]{1,0:T(8,128)(2,1)}, bf16[256,512]{1,0:T(8,128)(2,1)S(1)}, u32[]{:S(2)}) copy-start(bf16[256,512]{1,0:T(8,128)(2,1)S(1)} %collective-permute-done.4.near) | copy-start | bytes 786436
  134.7 0.7 copy-start.7
  135.4 78.9 %all-to-all-start.1 = ((bf16[64,288,128]{2,1,0:T(8,128)(2,1)}), bf16[64,288,128]{2,1,0:T(8,128)(2,1)}, u32[]{:S(2)}, u32[]{:S(2)}) async-start(bf16[64,288,128]{2,1,0:T(8,128)(2,1)} %bitcast.38), calls=%async_computation.2 | async-start | bytes 9437184 | tf_op jit(solution)/shard_map/all_to_all | solution.py:79
  147.8 53.6 %reduce-scatter.2.cloned.1.call-start = ((), (), s32[]{:S(2)}) async-start(), calls=%async_computation.5 | async-start | bytes 1310720 | tf_op jit(solution)/shard_map/reduce_scatter | solution.py:875
  156.4 2.9 %collective-permute-start.6 = (bf16[4096,128]{1,0:T(8,128)(2,1)}, bf16[4096,128]{1,0:T(8,128)(2,1)S(1)}, u32[]{:S(2)}, u32[]{:S(2)}) collective-permute-start(bf16[4096,128]{1,0:T(8,128)(2,1)} %get-tuple-element.73), channel_id=1, source_target_pairs={{0,1},{1,0},{2,3},{3,2},{4,5},{5,4},{6,7},{7,6},{8,9},{9,8},{10,11... | collective-permute-start | bytes 3145736 | tf_op jit(solution)/shard_map/ppermute | solution.py:75
  214.3 12.2 %all-to-all-start.2 = ((bf16[16,64,128]{2,1,0:T(8,128)(2,1)}), bf16[16,64,128]{2,1,0:T(8,128)(2,1)S(1)}, u32[]{:S(2)}, u32[]{:S(2)}) async-start(bf16[16,64,128]{2,1,0:T(8,128)(2,1)} %bitcast.41), calls=%async_computation.3 | async-start | bytes 524288 | tf_op jit(solution)/shard_map/all_to_all | solution.py:879
Sparse Core Ops, SparseCore 0:
  11.7 81.7 all-gather.1
  161.9 39.4 reduce-scatter.1

commit v8 on v7

--- a/solution.py
+++ b/solution.py
@@ -563,7 +563,7 @@
         d_probs = dot_nt(d_heads[:, span], values)
         inner = jnp.sum(probs * d_probs, axis=-1, keepdims=True)
         d_scores = (probs * (d_probs - inner)).astype(BF16)
-        d_query[:, span] = dot(d_scores, keys) * query_scale
+        d_query[:, span] = (dot(d_scores, keys) * query_scale).astype(BF16)
         key_term = dot_tn(d_scores, query_low[:, span]) * query_scale
         value_term = dot_tn(probs.astype(BF16), d_heads[:, span])
         if index == 0:
@@ -594,11 +594,11 @@
     for index in range(q_cols // head):
         span = slice(index * head, (index + 1) * head)
         unit, scale = normed(raw[:, span])
-        cot = turned(d_query[:, span], cosine, minus_sine)
+        cot = turned(d_query[:, span].astype(F32), cosine, minus_sine)
         d_raw, part = normed_back(cot, unit, scale, head_gains[0:1, :])
         query_gain_grad += part
         low[:, span] = d_raw.astype(BF16)
-    d_kv = d_own[...] + near[...].astype(F32) + far[...].astype(F32)
+    d_kv = d_own[...].astype(F32) + near[...].astype(F32) + far[...].astype(F32)
     unit, scale = normed(raw[:, q_cols : q_cols + head])
     cot = turned(d_kv[:, :head], cosine, minus_sine)
     d_raw, key_gain_grad = normed_back(cot, unit, scale, head_gains[1:2, :])
@@ -812,8 +812,8 @@
     d_query, d_own, d_near, d_far = call(
         attention_back,
         (
-            shape((tok_rows, q_cols), F32),
-            shape((tok_rows, kv_cols), F32),
+            shape((tok_rows, q_cols), BF16),
+            shape((tok_rows, kv_cols), BF16),
             shape((tok_rows, kv_cols), BF16),
             shape((tok_rows, kv_cols), BF16),
         ),

time: 237 us -> 236 us (level)
  no operation moved by 1% of the time
where the time goes in v8:
time: 236 us
  waiting for transfers between devices  112 us (47%)
  Pallas kernels  53.2 us (23%)
  starting transfers between devices  35.2 us (15%)
  between operations  14.3 us (6%)
  other arithmetic  10.4 us (4%)
  local copies, waits for them, and re-layouts  10.2 us (4%)
    pallas_call x6, Pallas kernels, call(): pl.pallas_call(kernel, out_shape=outs, in_specs=specs, **{} if out_specs...  53.2 us
    reduce_scatter x1, waiting for transfers between devices, on_device(): lax.psum_scatter(both, 'fsdp', scatter_dimension=0, axis_index_groups=lin...  39.6 us
    all_to_all x2, waiting for transfers between devices, exchange(): lax.all_to_all(blocks, 'fsdp', split_axis=0, concat_axis=0, tiled=True, a...  32.7 us
    all_to_all x2, starting transfers between devices, exchange(): lax.all_to_all(blocks, 'fsdp', split_axis=0, concat_axis=0, tiled=True, a...  23.9 us
    all_gather x1, waiting for transfers between devices, on_device(): mlp_full = lax.all_gather(gathered, 'fsdp', axis=0, tiled=True)  22.3 us
    ppermute x4, waiting for transfers between devices, shifted(): return lax.ppermute(block, axis, route)  9.96 us
    ppermute x4, starting transfers between devices, shifted(): return lax.ppermute(block, axis, route)  7.33 us
  transfers between devices with their start and end apart: 12, of which 9 were waited for; matrix products, arithmetic and copies ran while one was open for 6% of the time, Pallas kernels for 14%

profile of v8, /device:TPU:0, one launch (start us, length us, event | category | flops | bytes accessed | tf_op | source)
XLA Modules:
  0.0 235.5 jit_solution(6721642272552893900)
XLA Ops:
  7.2 0.0 copy-start.1
  7.2 0.0 copy-start.2
  7.2 0.0 all-gather.2.cloned.1.call-start
  7.2 1.5 fusion.3
  8.8 0.0 all-gather.2.cloned.1.call-update
  8.8 0.7 pad_maximum_fusion
  9.6 0.8 pad_add_fusion
  10.4 1.3 broadcast_in_dim.73
  11.7 11.5 %all-to-all-start = ((bf16[64,64,128]{2,1,0:T(8,128)(2,1)}), bf16[64,64,128]{2,1,0:T(8,128)(2,1)S(1)}, u32[]{:S(2)}, u32[]{:S(2)}) async-start(bf16[64,64,128]{2,1,0:T(8,128)(2,1)} %broadcast_in_dim.73), calls=%async_computation | async-start | bytes 2097152 | tf_op jit(solution)/shard_map/all_to_all | solution.py:79
  23.2 19.7 %all-to-all-done = bf16[64,64,128]{2,1,0:T(8,128)(2,1)S(1)} async-done(((bf16[64,64,128]{2,1,0:T(8,128)(2,1)}), bf16[64,64,128]{2,1,0:T(8,128)(2,1)S(1)}, u32[]{:S(2)}, u32[]{:S(2)}) %all-to-all-start) | async-done | bytes 1048608 | tf_op jit(solution)/shard_map/all_to_all | solution.py:79
  43.0 0.0 collective-permute-start
  43.0 0.0 copy-done.1
  43.0 0.0 copy-done.2
  43.0 0.1 select_reduce_fusion.1
  43.1 0.1 fusion.4
  43.3 0.1 select_reduce_fusion
  43.4 1.3 multiply_sine_fusion
  44.6 1.0 collective-permute-done.peer
  45.6 0.0 copy-done
  45.6 1.0 copy-done.3
  46.6 6.4 %shard_map.246 = (f32[256,1536]{1,0:T(8,128)}, bf16[256,1024]{1,0:T(8,128)(2,1)}, bf16[256,512]{1,0:T(8,128)(2,1)}, f32[8,640]{1,0:T(8,128)}, f32[8,256]{1,0:T(8,128)}, /*index=5*/bf16[2,320,1536]{2,1,0:T(8,128)(2,1)}) custom-call(s32[1]{0:T(128)} %bitcast.core_ref, bf16[256,640]{1,0:T(8,128)(2,1)} %tok.3, bf16[4096,128]{1,0:T(8,128)(2,1)} %bitcast.40, ...), custom_call_target="tpu_custom_call" | custom-call | flops 4000000000 | bytes 8000000 | tf_op jit(solution)/shard_map/pallas_call | solution.py:95
  53.0 2.1 collective-permute-start.2
  55.0 2.7 %collective-permute-start.1 = (bf16[256,512]{1,0:T(8,128)(2,1)}, bf16[256,512]{1,0:T(8,128)(2,1)S(1)}, u32[]{:S(2)}, u32[]{:S(2)}) collective-permute-start(bf16[256,512]{1,0:T(8,128)(2,1)} %get-tuple-element.47.kv_own), channel_id=1, source_target_pairs={{0,2},{1,3},{2,4},{3,5},{4,6},{5,7},{6,8},{7,9},{8,10},{9,11},{10,... | collective-permute-start | bytes 786440 | tf_op jit(solution)/shard_map/ppermute | solution.py:19
  57.7 0.1 fusion.9
  57.9 0.6 select_n.54.k_seq
  58.4 0.8 copy.32.q_seq
  59.2 0.8 copy.33.live
  60.0 0.0 collective-permute-done.2.kv_near
  60.0 5.5 %collective-permute-done.1.kv_far = bf16[256,512]{1,0:T(8,128)(2,1)S(1)} collective-permute-done((bf16[256,512]{1,0:T(8,128)(2,1)}, bf16[256,512]{1,0:T(8,128)(2,1)S(1)}, u32[]{:S(2)}, u32[]{:S(2)}) %collective-permute-start.1) | collective-permute-done | bytes 262176 | tf_op jit(solution)/shard_map/ppermute | solution.py:19
  65.5 0.0 copy-done.4
  65.5 0.7 copy-done.5
  66.2 5.0 %shard_map.247 = (bf16[256,1024]{1,0:T(8,128)(2,1)}, f32[256,128]{1,0:T(8,128)}, bf16[640,1024]{1,0:T(8,128)(2,1)}, bf16[2,640,320]{2,1,0:T(8,128)(2,1)}) custom-call(s32[1]{0:T(128)} %bitcast.core_ref, bf16[256,1024]{1,0:T(8,128)(2,1)} %get-tuple-element.46.query_low, bf16[256,512]{1,0:T(8,128)(2,1)} %copy-done.5, bf16[256,512]{1,0:T(8,128)(2,1)} %copy-done.4, ...), custom_call_target="tpu_custom_call" | custom-call | flops 20000000000 | bytes 8000000 | tf_op jit(solution)/shard_map/pallas_call | solution.py:95
  71.2 22.3 %all-gather.2.cloned.1.call-done.full = bf16[1024,6016]{1,0:T(8,128)(2,1)} async-done(((bf16[8,6016]{1,0:T(8,128)(2,1)}), bf16[1024,6016]{1,0:T(8,128)(2,1)}) %all-gather.2.cloned.1.call-update) | async-done | bytes 12320784 | tf_op jit(solution)/shard_map/all_gather | solution.py:688
  93.5 20.8 %shard_map.248 = (f32[8,640]{1,0:T(8,128)}, bf16[256,640]{1,0:T(8,128)(2,1)}, f32[256,640]{1,0:T(8,128)}, bf16[256,1024]{1,0:T(8,128)(2,1)}, bf16[256,320]{1,0:T...) custom-call(s32[1]{0:T(128)} %bitcast.core_ref, ...), custom_call_target="tpu_custom_call" | custom-call | flops 12000000000 | bytes 8000000 | tf_op jit(solution)/shard_map/pallas_call | solution.py:95
  114.3 0.3 collective-permute-start.3
  114.6 5.9 %shard_map.249 = (bf16[256,1024]{1,0:T(8,128)(2,1)}, bf16[256,512]{1,0:T(8,128)(2,1)}, bf16[256,512]{1,0:T(8,128)(2,1)}, bf16[256,512]{1,0:T(8,128)(2,1)}) custom-call(bf16[256,1024]{1,0:T(8,128)(2,1)} %get-tuple-element.46.query_low, bf16[256,512]{1,0:T(8,128)(2,1)} %copy-done.5, bf16[256,512]{1,0:T(8,128)(2,1)} %copy-done.4, ...), custom_call_target="tpu_custom_call" | custom-call | flops 20000000000 | bytes 8000000 | tf_op jit(solution)/shard_map/pallas_call | solution.py:95
  120.5 1.3 collective-permute-start.4
  121.8 1.3 collective-permute-start.5
  123.1 0.0 collective-permute-done.3.arrived
  123.1 6.8 %shard_map.250 = bf16[8,8,288,128]{3,2,1,0:T(8,128)(2,1)} custom-call(bf16[256,320]{1,0:T(8,128)(2,1)} %get-tuple-element.57.low_own, bf16[256,4096]{1,0:T(8,128)(2,1)} %get-tuple-element.58.d_gate_up_in, bf16[8,8,80,128]{3,2,1,0:T(8,128)(2,1)} %get-tuple-element.59.own_down_in, bf16[8,8,48,128]{3,2,1,0:T(8,128)(2,1)} %get-tuple-element.60.own_out_in, ...), custom_call_target="tpu_custom_call" | custom-call | flops 12000000000 | bytes 8000000 | tf_op jit(solution)/shard_map/pallas_call | solution.py:95
  129.9 0.0 collective-permute-done.4.near
  129.9 0.0 copy-start.6
  129.9 4.5 %collective-permute-done.5.far = bf16[256,512]{1,0:T(8,128)(2,1)S(1)} collective-permute-done((bf16[256,512]{1,0:T(8,128)(2,1)}, bf16[256,512]{1,0:T(8,128)(2,1)S(1)}, u32[]{:S(2)}, u32[]{:S(2)}) %collective-permute-start.5) | collective-permute-done | bytes 262176 | tf_op jit(solution)/shard_map/ppermute | solution.py:19
  134.4 0.0 copy-done.6
  134.4 0.7 copy-done.7
  135.1 12.4 %all-to-all-start.1 = ((bf16[64,288,128]{2,1,0:T(8,128)(2,1)}), bf16[64,288,128]{2,1,0:T(8,128)(2,1)}, u32[]{:S(2)}, u32[]{:S(2)}) async-start(bf16[64,288,128]{2,1,0:T(8,128)(2,1)} %bitcast.38), calls=%async_computation.2 | async-start | bytes 9437184 | tf_op jit(solution)/shard_map/all_to_all | solution.py:79
  147.6 0.0 reduce-scatter.2.cloned.1.call-start
  147.6 8.4 %shard_map.251 = (bf16[256,640]{1,0:T(8,128)(2,1)}, bf16[4096,128]{1,0:T(8,128)(2,1)}, bf16[4096,128]{1,0:T(8,128)(2,1)}) custom-call(s32[1]{0:T(128)} %bitcast.core_ref, f32[256,1536]{1,0:T(8,128)} %get-tuple-element.52.raw, bf16[256,1024]{1,0:T(8,128)(2,1)} %get-tuple-element.55.d_query, bf16[256,512]{1,0:T(8,128)(2,1)} %get-tuple-element.56.d_own, ...), custom_call_target="tpu_custom_call" | custom-call | flops 20000000000 | bytes 8000000 | tf_op jit(solution)/shard_map/pallas_call | solution.py:95
  156.0 0.0 collective-permute-start.6
  156.0 2.9 %collective-permute-done.6 = bf16[4096,128]{1,0:T(8,128)(2,1)S(1)} collective-permute-done((bf16[4096,128]{1,0:T(8,128)(2,1)}, bf16[4096,128]{1,0:T(8,128)(2,1)S(1)}, u32[]{:S(2)}, u32[]{:S(2)}) %collective-permute-start.6) | collective-permute-done | bytes 1048608 | tf_op jit(solution)/shard_map/ppermute | solution.py:75
  158.9 2.5 %add_convert_fusion = bf16[4096,128]{1,0:T(8,128)(2,1)} fusion(bf16[4096,128]{1,0:T(8,128)(2,1)S(1)} %collective-permute-done.6, bf16[4096,128]{1,0:T(8,128)(2,1)} %get-tuple-element.72), kind=kLoop, calls=%fused_computation.1 | loop fusion | flops 2097152 | bytes 3145728 | tf_op jit(solution)/shard_map/convert_element_type | solution.py:874
  161.4 0.0 reduce-scatter.2.cloned.1.call-update
  161.4 39.6 %reduce-scatter.2.cloned.1.call-done = bf16[1024,128]{1,0:T(8,128)(2,1)} async-done(((bf16[4096,128]{1,0:T(8,128)(2,1)}), bf16[1024,128]{1,0:T(8,128)(2,1)}) %reduce-scatter.2.cloned.1.call-update) | async-done | bytes 262160 | tf_op jit(solution)/shard_map/reduce_scatter | solution.py:875
  201.0 13.0 %all-to-all-done.1 = bf16[64,288,128]{2,1,0:T(8,128)(2,1)} async-done(((bf16[64,288,128]{2,1,0:T(8,128)(2,1)}), bf16[64,288,128]{2,1,0:T(8,128)(2,1)}, u32[]{:S(2)}, u32[]{:S(2)}) %all-to-all-start.1) | async-done | bytes 4718624 | tf_op jit(solution)/shard_map/all_to_all | solution.py:79
  214.0 3.5 %all-to-all-start.2 = ((bf16[16,64,128]{2,1,0:T(8,128)(2,1)}), bf16[16,64,128]{2,1,0:T(8,128)(2,1)S(1)}, u32[]{:S(2)}, u32[]{:S(2)}) async-start(bf16[16,64,128]{2,1,0:T(8,128)(2,1)} %bitcast.41), calls=%async_computation.3 | async-start | bytes 524288 | tf_op jit(solution)/shard_map/all_to_all | solution.py:879
  217.6 3.0 %convert_reduce_fusion = f32[288,128]{1,0:T(8,128)S(1)} fusion(bf16[64,288,128]{2,1,0:T(8,128)(2,1)} %all-to-all-done.1), kind=kLoop, calls=%fused_computation | loop fusion | flops 4681728 | bytes 4866048 | tf_op jit(solution)/shard_map/reduce_sum | solution.py:891
  220.6 0.6 copy.38
  221.2 0.7 reshape.127
  221.9 0.6 slice_bitcast_fusion
  222.5 3.7 %all-to-all-done.2 = bf16[16,64,128]{2,1,0:T(8,128)(2,1)S(1)} async-done(((bf16[16,64,128]{2,1,0:T(8,128)(2,1)}), bf16[16,64,128]{2,1,0:T(8,128)(2,1)S(1)}, u32[]{:S(2)}, u32[]{:S(2)}) %all-to-all-start.2) | async-done | bytes 262176 | tf_op jit(solution)/shard_map/all_to_all | solution.py:879
  226.3 0.6 slice_bitcast_fusion.1
  226.9 0.6 slice_bitcast_fusion.3
  227.5 0.6 slice.83
  228.1 0.6 slice.82
  (18 shorter events, 0.2 us)
Async XLA Ops:
  7.2 35.8 %copy-start.1 = (s32[25]{0:T(128)S(1)}, s32[25]{0:T(128)}, u32[]{:S(2)}) copy-start(s32[25]{0:T(128)} %param.18) | copy-start | bytes 304
  7.2 35.8 %copy-start.2 = (s32[25]{0:T(128)S(1)}, s32[25]{0:T(128)}, u32[]{:S(2)}) copy-start(s32[25]{0:T(128)} %param.17) | copy-start | bytes 304
  7.2 86.3 %all-gather.2.cloned.1.call-start = ((), (), s32[]{:S(2)}) async-start(), calls=%async_computation.4 | async-start | bytes 12417024 | tf_op jit(solution)/shard_map/all_gather | solution.py:688
  11.7 31.2 %all-to-all-start = ((bf16[64,64,128]{2,1,0:T(8,128)(2,1)}), bf16[64,64,128]{2,1,0:T(8,128)(2,1)S(1)}, u32[]{:S(2)}, u32[]{:S(2)}) async-start(bf16[64,64,128]{2,1,0:T(8,128)(2,1)} %broadcast_in_dim.73), calls=%async_computation | async-start | bytes 2097152 | tf_op jit(solution)/shard_map/all_to_all | solution.py:79
  43.0 2.7 %copy-start = (bf16[64,64,128]{2,1,0:T(8,128)(2,1)}, bf16[64,64,128]{2,1,0:T(8,128)(2,1)S(1)}, u32[]{:S(2)}) copy-start(bf16[64,64,128]{2,1,0:T(8,128)(2,1)S(1)} %all-to-all-done) | copy-start | bytes 3145732
  43.0 2.7 %collective-permute-start = (bf16[4096,128]{1,0:T(8,128)(2,1)S(1)}, bf16[4096,128]{1,0:T(8,128)(2,1)S(1)}, u32[]{:S(2)}, u32[]{:S(2)}) collective-permute-start(bf16[4096,128]{1,0:T(8,128)(2,1)S(1)} %bitcast.39), channel_id=1, source_target_pairs={{0,1},{1,0},{2,3},{3,2},{4,5},{5,4},{6,7},{7,6},{8,9},{9,8},{10,11... | collective-permute-start | bytes 3145736 | tf_op jit(solution)/shard_map/ppermute | solution.py:75
  45.6 1.0 copy-start.3
  53.0 7.1 %collective-permute-start.2 = (bf16[256,512]{1,0:T(8,128)(2,1)}, bf16[256,512]{1,0:T(8,128)(2,1)S(1)}, u32[]{:S(2)}, u32[]{:S(2)}) collective-permute-start(bf16[256,512]{1,0:T(8,128)(2,1)} %get-tuple-element.47.kv_own), channel_id=1, source_target_pairs={{0,1},{1,2},{2,3},{3,4},{4,5},{5,6},{6,7},{7,8},{8,9},{9,10},{10,1... | collective-permute-start | bytes 786440 | tf_op jit(solution)/shard_map/ppermute | solution.py:19
  55.0 10.5 %collective-permute-start.1 = (bf16[256,512]{1,0:T(8,128)(2,1)}, bf16[256,512]{1,0:T(8,128)(2,1)S(1)}, u32[]{:S(2)}, u32[]{:S(2)}) collective-permute-start(bf16[256,512]{1,0:T(8,128)(2,1)} %get-tuple-element.47.kv_own), channel_id=1, source_target_pairs={{0,2},{1,3},{2,4},{3,5},{4,6},{5,7},{6,8},{7,9},{8,10},{9,11},{10,... | collective-permute-start | bytes 786440 | tf_op jit(solution)/shard_map/ppermute | solution.py:19
  60.0 5.5 %copy-start.4 = (bf16[256,512]{1,0:T(8,128)(2,1)}, bf16[256,512]{1,0:T(8,128)(2,1)S(1)}, u32[]{:S(2)}) copy-start(bf16[256,512]{1,0:T(8,128)(2,1)S(1)} %collective-permute-done.2.kv_near) | copy-start | bytes 786436
  65.5 0.7 copy-start.5
  114.3 8.8 %collective-permute-start.3 = (bf16[8,8,288,128]{3,2,1,0:T(8,128)(2,1)}, bf16[8,8,288,128]{3,2,1,0:T(8,128)(2,1)}, u32[]{:S(2)}, u32[]{:S(2)}) collective-permute-start(bf16[8,8,288,128]{3,2,1,0:T(8,128)(2,1)} %get-tuple-element.61), channel_id=1, source_target_pairs={{0,1},{1,0},{2,3},{3,2},{4,5},{5,4},{6,7},{7,6},{8,9},{9,8},{10,11... | collective-permute-start | bytes 14155784 | tf_op jit(solution)/shard_map/ppermute | solution.py:75
  120.5 9.4 %collective-permute-start.4 = (bf16[256,512]{1,0:T(8,128)(2,1)}, bf16[256,512]{1,0:T(8,128)(2,1)S(1)}, u32[]{:S(2)}, u32[]{:S(2)}) collective-permute-start(bf16[256,512]{1,0:T(8,128)(2,1)} %get-tuple-element.64), channel_id=1, source_target_pairs={{1,0},{2,1},{3,2},{4,3},{5,4},{6,5},{7,6},{8,7},{9,8},{10,9},{11,1... | collective-permute-start | bytes 786440 | tf_op jit(solution)/shard_map/ppermute | solution.py:19
  121.8 12.6 %collective-permute-start.5 = (bf16[256,512]{1,0:T(8,128)(2,1)}, bf16[256,512]{1,0:T(8,128)(2,1)S(1)}, u32[]{:S(2)}, u32[]{:S(2)}) collective-permute-start(bf16[256,512]{1,0:T(8,128)(2,1)} %get-tuple-element.62), channel_id=1, source_target_pairs={{2,0},{3,1},{4,2},{5,3},{6,4},{7,5},{8,6},{9,7},{10,8},{11,9},{12,... | collective-permute-start | bytes 786440 | tf_op jit(solution)/shard_map/ppermute | solution.py:19
  129.9 4.5 %copy-start.6 = (bf16[256,512]{1,0:T(8,128)(2,1)}, bf16[256,512]{1,0:T(8,128)(2,1)S(1)}, u32[]{:S(2)}) copy-start(bf16[256,512]{1,0:T(8,128)(2,1)S(1)} %collective-permute-done.4.near) | copy-start | bytes 786436
  134.4 0.7 copy-start.7
  135.1 78.9 %all-to-all-start.1 = ((bf16[64,288,128]{2,1,0:T(8,128)(2,1)}), bf16[64,288,128]{2,1,0:T(8,128)(2,1)}, u32[]{:S(2)}, u32[]{:S(2)}) async-start(bf16[64,288,128]{2,1,0:T(8,128)(2,1)} %bitcast.38), calls=%async_computation.2 | async-start | bytes 9437184 | tf_op jit(solution)/shard_map/all_to_all | solution.py:79
  147.6 53.4 %reduce-scatter.2.cloned.1.call-start = ((), (), s32[]{:S(2)}) async-start(), calls=%async_computation.5 | async-start | bytes 1310720 | tf_op jit(solution)/shard_map/reduce_scatter | solution.py:875
  156.0 2.9 %collective-permute-start.6 = (bf16[4096,128]{1,0:T(8,128)(2,1)}, bf16[4096,128]{1,0:T(8,128)(2,1)S(1)}, u32[]{:S(2)}, u32[]{:S(2)}) collective-permute-start(bf16[4096,128]{1,0:T(8,128)(2,1)} %get-tuple-element.73), channel_id=1, source_target_pairs={{0,1},{1,0},{2,3},{3,2},{4,5},{5,4},{6,7},{7,6},{8,9},{9,8},{10,11... | collective-permute-start | bytes 3145736 | tf_op jit(solution)/shard_map/ppermute | solution.py:75
  214.0 12.2 %all-to-all-start.2 = ((bf16[16,64,128]{2,1,0:T(8,128)(2,1)}), bf16[16,64,128]{2,1,0:T(8,128)(2,1)S(1)}, u32[]{:S(2)}, u32[]{:S(2)}) async-start(bf16[16,64,128]{2,1,0:T(8,128)(2,1)} %bitcast.41), calls=%async_computation.3 | async-start | bytes 524288 | tf_op jit(solution)/shard_map/all_to_all | solution.py:879
Sparse Core Ops, SparseCore 0:
  11.7 81.7 all-gather.1
  161.5 39.4 reduce-scatter.1
